TPU v7x, 32 devices: a whole 2x2x4 slice. The times are simulated.
32 devices in a mesh: groups: 2 (over y), space: 8 (over z, x), tm: 2 (over core).
Axes of the slice: x: 2, y: 2, z: 4, core: 2. Of those that a mesh axis runs over, the one named last changes fastest.
Arguments:
- start_state: float32 [256, 32, 16], P(('groups', 'space')), parts along dimension 0, may hold values from -6 to 6
- timesteps: int32 [8], P(('groups', 'tm')), parts along dimension 0, may hold values from 0 to 999
- step_sizes: float32 [8], P(('groups', 'tm')), parts along dimension 0, may hold values from 0.1 to 0.4
- in_weight: float32 [16, 256], replicated, may hold values from -1.5 to 1.5
- time_weight: float32 [256, 256], replicated, may hold values from -0.375 to 0.375
- conv_kernel: float32 [2, 7, 7, 256], replicated, may hold values from -0.875 to 0.875
- norm_gain: float32 [2, 256], replicated, may hold values from 0.5 to 1.5
- up_weight: bfloat16 [2, 256, 1024], replicated, may hold values from -0.375 to 0.375
- up_bias: float32 [2, 1024], replicated, may hold values from -3 to 3
- down_weight: bfloat16 [2, 1024, 256], replicated, may hold values from -0.1875 to 0.1875
- out_weight: float32 [256, 16], replicated, may hold values from -0.375 to 0.375
Outputs:
- next_states: float32 [4, 256, 32, 16], P('tm', ('groups', 'space')), parts along dimension 1
There are 2 independent parts, one for each index of `groups`. A program takes and returns all parts, laid end to end along the dimension named above; an argument that names none is the same for every part. Nothing has to cross between parts.
All inputs are finite; a program needn't handle non-finite values.
Results may differ from a plain program's by a relative error of at most 0.0035.
Values may be sent and summed in bfloat16 or wider, within the bound.
No kernel may reach another device: no remote copies, remote signals or barrier semaphores. Data moves between devices by JAX's collectives and lax.ppermute only.
A program may use at most 64 MiB of HBM per device.

v0:
```python
import math

import jax
import jax.numpy as jnp
from jax import lax
from jax.sharding import PartitionSpec as P

BLOCKS = 2
SWEEPS = 2


HIGH = lax.Precision.HIGHEST


def with_halo(x, sides, width):
    for axis, dim in sides:
        size, length = (lax.axis_size(axis), x.shape[dim])
        up = [(i, (i + 1) % size) for i in range(size - 1)]
        down = [(j, i) for i, j in up]
        last = lax.slice_in_dim(x, length - width, length, axis=dim)
        first = lax.slice_in_dim(x, 0, width, axis=dim)
        before = lax.ppermute(last, axis, up)
        after = lax.ppermute(first, axis, down)
        x = jnp.concatenate([before, x, after], axis=dim)
    return x


def entering(x, axis, join, neutral):
    place = lax.axis_index(axis)
    gathered = lax.all_gather(x.astype(jnp.bfloat16 if x.dtype == jnp.float32 else x.dtype), axis)
    state = jnp.zeros_like(x) + jnp.asarray(neutral, x.dtype)

    def one(hop, state):
        return join(state, lax.dynamic_index_in_dim(gathered, hop, 0, False).astype(x.dtype))

    return lax.fori_loop(0, place, one, state)


def embed_times(steps, time_weight):
    half = time_weight.shape[0] // 2
    freqs = jnp.exp(-math.log(10000.0) * jnp.arange(half, dtype=jnp.float32) / half)
    angle = steps.astype(jnp.float32)[:, None] * freqs[None, :]
    feats = jnp.concatenate([jnp.sin(angle), jnp.cos(angle)], axis=1)
    return jnp.dot(feats, time_weight, precision=HIGH)


def convnext_block(stream, padded, block, conv_kernel, norm_gain, up_weight, up_bias, down_weight):
    count = stream.shape[1]
    width_cols = stream.shape[2]
    wide = jnp.pad(padded, ((0, 0), (0, 0), (3, 3), (0, 0)))
    conv = jnp.zeros(stream.shape, jnp.float32)
    for dy in range(7):
        for dx in range(7):
            conv = (
                conv
                + wide[:, dy : dy + count, dx : dx + width_cols].astype(jnp.float32)
                * conv_kernel[block, dy, dx]
            )
    mean = jnp.mean(conv, axis=-1, keepdims=True)
    centered = conv - mean
    var = jnp.mean(centered * centered, axis=-1, keepdims=True)
    normed = (centered * lax.rsqrt(var + 1e-06) * norm_gain[block]).astype(jnp.bfloat16)
    upper = (
        jnp.einsum("trwc,cf->trwf", normed, up_weight[block], preferred_element_type=jnp.float32)
        + up_bias[block]
    )
    hidden = jax.nn.gelu(upper, approximate=True).astype(jnp.bfloat16)
    return stream + jnp.einsum(
        "trwf,fc->trwc", hidden, down_weight[block], preferred_element_type=jnp.float32
    )


def evaluate(
    states, temb, in_weight, conv_kernel, norm_gain, up_weight, up_bias, down_weight, out_weight
):
    stream = jnp.einsum("trwc,cd->trwd", states, in_weight, precision=HIGH) + temb[:, None, None, :]
    for block in range(BLOCKS):
        conv_in = stream.astype(jnp.bfloat16)
        padded = with_halo(conv_in, (("space", 1),), 3)
        stream = convnext_block(
            stream, padded, block, conv_kernel, norm_gain, up_weight, up_bias, down_weight
        )
    return jnp.einsum("trwd,dc->trwc", stream, out_weight, precision=HIGH)


def add_terms(earlier, later):
    return earlier + later


def on_device(
    start_state,
    timesteps,
    step_sizes,
    in_weight,
    time_weight,
    conv_kernel,
    norm_gain,
    up_weight,
    up_bias,
    down_weight,
    out_weight,
):
    local_times = timesteps.shape[0]
    temb = embed_times(timesteps, time_weight)
    states = jnp.broadcast_to(start_state[None], (local_times,) + start_state.shape)
    result = states
    for sweep in range(SWEEPS):
        drifts = evaluate(
            states,
            temb,
            in_weight,
            conv_kernel,
            norm_gain,
            up_weight,
            up_bias,
            down_weight,
            out_weight,
        )
        terms = drifts * step_sizes[:, None, None, None]
        local_total = jnp.sum(terms, axis=0)
        before = entering(local_total, "tm", add_terms, jnp.zeros_like(local_total))
        inclusive = jnp.cumsum(terms, axis=0)
        if sweep < SWEEPS - 1:
            exclusive = jnp.concatenate([jnp.zeros_like(terms[:1]), inclusive[:-1]], axis=0)
            states = start_state[None] + (before[None] + exclusive)
        else:
            result = start_state[None] + (before[None] + inclusive)
    return result


def solution(mesh):
    return jax.shard_map(
        on_device,
        mesh=mesh,
        in_specs=(
            P(("groups", "space"), None, None),
            P(("groups", "tm")),
            P(("groups", "tm")),
            P(),
            P(),
            P(),
            P(),
            P(),
            P(),
            P(),
            P(),
        ),
        out_specs=P("tm", ("groups", "space"), None, None),
        check_vma=False,
    )
```

profile of v0, /device:TPU:0, one launch (start us, length us, event | category | flops | bytes accessed | tf_op | source)
XLA Modules:
  0.0 103.5 jit_solution(2169073211164629705)
XLA Ops:
  1.2 2.0 %fusion.154 = (bf16[2,16,32,256]{3,2,1,0:T(8,128)(2,1)S(1)}, f32[2,16,32,256]{3,2,1,0:T(8,128)S(1)}) fusion(f32[2,256]{1,0:T(2,128)S(1)} %fusion.116, f32[16,256]{1,0:T(8,128)} %param.18, f32[16,32,16]{1,2,0:T(8,128)} %param.15), kind=kOutput, calls=%fused_computation.218 | convolution fusion | flops 50855936 | bytes 1624064 | tf_op jit(solution)/shard_map/trwc,cd->trwd/dot_general | solution.py:76
  3.2 1.3 %collective-permute-start.1 = (bf16[2,3,32,256]{3,2,1,0:T(8,128)(2,1)S(1)}, bf16[2,3,32,256]{3,2,1,0:T(8,128)(2,1)S(1)}, u32[]{:S(2)}, u32[]{:S(2)}) collective-permute-start(bf16[2,3,32,256]{3,2,1,0:T(8,128)(2,1)S(1)} %get-tuple-element.84), channel_id=1, source_target_pairs={{2,0},{4,2},{6,4},{8,6},{10,8},{12,10},{14,12},{3,1},{5,3},{7,5},{... | collective-permute-start | bytes 294920 | tf_op jit(solution)/shard_map/ppermute | solution.py:23
  4.5 5.5 %collective-permute-start = (bf16[2,3,32,256]{3,2,1,0:T(8,128)(2,1)S(1)}, bf16[2,3,32,256]{3,2,1,0:T(8,128)(2,1)S(1)}, u32[]{:S(2)}, u32[]{:S(2)}) collective-permute-start(bf16[2,3,32,256]{3,2,1,0:T(8,128)(2,1)S(1)} %get-tuple-element.83), channel_id=1, source_target_pairs={{0,2},{2,4},{4,6},{6,8},{8,10},{10,12},{12,14},{1,3},{3,5},{5,7},{... | collective-permute-start | bytes 294920 | tf_op jit(solution)/shard_map/ppermute | solution.py:22
  10.9 2.3 %collective-permute-done = bf16[2,3,32,256]{3,2,1,0:T(8,128)(2,1)S(1)} collective-permute-done((bf16[2,3,32,256]{3,2,1,0:T(8,128)(2,1)S(1)}, bf16[2,3,32,256]{3,2,1,0:T(8,128)(2,1)S(1)}, u32[]{:S(2)}, u32[]{:S(2)}) %collective-permute-start) | collective-permute-done | bytes 98336 | tf_op jit(solution)/shard_map/ppermute | solution.py:22
  13.6 8.0 %fusion.141 = (f32[2,16,32]{2,1,0:T(8,128)S(1)}, f32[2,16,32,256]{3,2,1,0:T(8,128)S(1)}) fusion(f32[256]{0:T(256)S(1)} %bitcast.251, bf16[2,22,38,256]{3,2,1,0:T(8,128)(2,1)S(1)} %select_maximum_fusion.6, f32[256]{0:T(256)S(1)} %bitcast.253, f32[256]{0:T(256)S(1)} %bitcast.255, f32[256]{0:T(256)S(1)} %bitcast.257, ...), kind=kLoop, calls=%fused_computation.205 | loop fusion | flops 40107008 | bytes 23843840 | tf_op jit(solution)/shard_map/reduce_sum | solution.py:59
  22.0 4.0 %fusion.155 = (bf16[2,16,32,256]{3,2,1,0:T(8,128)(2,1)S(1)}, f32[2,16,32,256]{3,2,1,0:T(8,128)}) fusion(f32[2,16,32,256]{3,2,1,0:T(8,128)S(1)} %get-tuple-element.190, bf16[2,1024,256]{2,1,0:T(8,128)(2,1)} %param.24, f32[1024]{0:T(1024)S(1)} %bitcast.389, f32[2,16,32,256]{3,2,1,0:T(8,128)S(1)} %get-tuple-element.76, f32[256]{0:T(256)S(1)} %bitcast.393, ...), kind=kOutput, calls=%fused_computation.219 | convolution fusion | flops 1085800448 | bytes 4731904 | tf_op jit(solution)/shard_map/trwf,fc->trwc/dot_general | solution.py:68
  26.1 1.3 %collective-permute-start.3 = (bf16[2,3,32,256]{3,2,1,0:T(8,128)(2,1)S(1)}, bf16[2,3,32,256]{3,2,1,0:T(8,128)(2,1)S(1)}, u32[]{:S(2)}, u32[]{:S(2)}) collective-permute-start(bf16[2,3,32,256]{3,2,1,0:T(8,128)(2,1)S(1)} %get-tuple-element.82), channel_id=1, source_target_pairs={{2,0},{4,2},{6,4},{8,6},{10,8},{12,10},{14,12},{3,1},{5,3},{7,5},{... | collective-permute-start | bytes 294920 | tf_op jit(solution)/shard_map/ppermute | solution.py:23
  27.4 5.2 %collective-permute-start.2 = (bf16[2,3,32,256]{3,2,1,0:T(8,128)(2,1)S(1)}, bf16[2,3,32,256]{3,2,1,0:T(8,128)(2,1)S(1)}, u32[]{:S(2)}, u32[]{:S(2)}) collective-permute-start(bf16[2,3,32,256]{3,2,1,0:T(8,128)(2,1)S(1)} %get-tuple-element.81), channel_id=1, source_target_pairs={{0,2},{2,4},{4,6},{6,8},{8,10},{10,12},{12,14},{1,3},{3,5},{5,7},{... | collective-permute-start | bytes 294920 | tf_op jit(solution)/shard_map/ppermute | solution.py:22
  33.4 2.3 %collective-permute-done.2 = bf16[2,3,32,256]{3,2,1,0:T(8,128)(2,1)S(1)} collective-permute-done((bf16[2,3,32,256]{3,2,1,0:T(8,128)(2,1)S(1)}, bf16[2,3,32,256]{3,2,1,0:T(8,128)(2,1)S(1)}, u32[]{:S(2)}, u32[]{:S(2)}) %collective-permute-start.2) | collective-permute-done | bytes 98336 | tf_op jit(solution)/shard_map/ppermute | solution.py:22
  36.1 7.9 %fusion.140 = (f32[2,16,32]{2,1,0:T(8,128)S(1)}, f32[2,16,32,256]{3,2,1,0:T(8,128)S(1)}) fusion(f32[256]{0:T(256)S(1)} %bitcast.211, bf16[2,22,38,256]{3,2,1,0:T(8,128)(2,1)S(1)} %select_maximum_fusion.4, f32[256]{0:T(256)S(1)} %bitcast.209, f32[256]{0:T(256)S(1)} %bitcast.215, f32[256]{0:T(256)S(1)} %bitcast.217, ...), kind=kLoop, calls=%fused_computation.204 | loop fusion | flops 40107008 | bytes 23843840 | tf_op jit(solution)/shard_map/reduce_sum | solution.py:59
  44.5 3.4 %fusion.38 = f32[2,16,32,256]{3,2,1,0:T(8,128)S(1)} fusion(f32[2,16,32,256]{3,2,1,0:T(8,128)} %get-tuple-element.192, f32[1024]{0:T(1024)S(1)} %bitcast.387, f32[2,16,32,256]{3,2,1,0:T(8,128)S(1)} %get-tuple-element.74, f32[256]{0:T(256)S(1)} %bitcast.391, f32[2,16,32]{2,1,0:T(8,128)S(1)} %add_rsqrt_fusion.2, ...), kind=kOutput, calls=%fused_computation.48 | convolution fusion | flops 1085538304 | bytes 4207616 | tf_op jit(solution)/shard_map/trwf,fc->trwc/dot_general | solution.py:68
  47.9 2.2 %fusion.158 = (bf16[16,32,16]{1,2,0:T(8,128)(2,1)S(1)}, f32[2,16,32,16]{2,3,1,0:T(8,128)S(1)}) fusion(f32[2]{0:T(128)S(1)} %copy-done.6, f32[2,16,32,256]{3,2,1,0:T(8,128)S(1)} %fusion.38, f32[256,16]{0,1:T(8,128)S(1)} %copy-done.4), kind=kOutput, calls=%fused_computation.220 | convolution fusion | flops 50356224 | bytes 1146888 | tf_op jit(solution)/shard_map/trwd,dc->trwc/dot_general | solution.py:83
  50.9 2.0 %all-gather = bf16[32,32,16]{1,2,0:T(8,128)(2,1)S(1)} all-gather(bf16[16,32,16]{1,2,0:T(8,128)(2,1)S(1)} %get-tuple-element.193), channel_id=2, replica_groups=mesh['groups'=2,'space'=8,'tm'=2] {'tm'}, dimensions={0}, use_global_device_ids=true | all-gather | bytes 49152 | tf_op jit(solution)/shard_map/all_gather | solution.py:30
  55.3 5.2 %collective-permute-start.4 = (bf16[2,3,32,256]{3,2,1,0:T(8,128)(2,1)S(1)}, bf16[2,3,32,256]{3,2,1,0:T(8,128)(2,1)S(1)}, u32[]{:S(2)}, u32[]{:S(2)}) collective-permute-start(bf16[2,3,32,256]{3,2,1,0:T(8,128)(2,1)S(1)} %get-tuple-element.79), channel_id=1, source_target_pairs={{0,2},{2,4},{4,6},{6,8},{8,10},{10,12},{12,14},{1,3},{3,5},{5,7},{... | collective-permute-start | bytes 294920 | tf_op jit(solution)/shard_map/ppermute | solution.py:22
  61.6 2.3 %collective-permute-done.4 = bf16[2,3,32,256]{3,2,1,0:T(8,128)(2,1)S(1)} collective-permute-done((bf16[2,3,32,256]{3,2,1,0:T(8,128)(2,1)S(1)}, bf16[2,3,32,256]{3,2,1,0:T(8,128)(2,1)S(1)}, u32[]{:S(2)}, u32[]{:S(2)}) %collective-permute-start.4) | collective-permute-done | bytes 98336 | tf_op jit(solution)/shard_map/ppermute | solution.py:22
  64.4 8.0 %fusion.139 = (f32[2,16,32]{2,1,0:T(8,128)S(1)}, f32[2,16,32,256]{3,2,1,0:T(8,128)S(1)}) fusion(f32[256]{0:T(256)S(1)} %bitcast.252, bf16[2,22,38,256]{3,2,1,0:T(8,128)(2,1)S(1)} %select_maximum_fusion.2, f32[256]{0:T(256)S(1)} %bitcast.254, f32[256]{0:T(256)S(1)} %bitcast.256, f32[256]{0:T(256)S(1)} %bitcast.258, ...), kind=kLoop, calls=%fused_computation.203 | loop fusion | flops 40107008 | bytes 23843840 | tf_op jit(solution)/shard_map/reduce_sum | solution.py:59
  72.8 4.0 %fusion.160 = (bf16[2,16,32,256]{3,2,1,0:T(8,128)(2,1)S(1)}, f32[2,16,32,256]{3,2,1,0:T(8,128)}) fusion(f32[2,16,32,256]{3,2,1,0:T(8,128)S(1)} %get-tuple-element.196, bf16[2,1024,256]{2,1,0:T(8,128)(2,1)} %param.24, f32[1024]{0:T(1024)S(1)} %bitcast.390, f32[2,16,32,256]{3,2,1,0:T(8,128)S(1)} %get-tuple-element.72, f32[2,16,32]{2,1,0:T(8,128)S(1)} %add_rsqrt_fusion.1, ...), kind=kOutput, calls=%fused_computation.222 | convolution fusion | flops 1085800448 | bytes 4731904 | tf_op jit(solution)/shard_map/trwf,fc->trwc/dot_general | solution.py:68
  76.8 1.3 %collective-permute-start.7 = (bf16[2,3,32,256]{3,2,1,0:T(8,128)(2,1)S(1)}, bf16[2,3,32,256]{3,2,1,0:T(8,128)(2,1)S(1)}, u32[]{:S(2)}, u32[]{:S(2)}) collective-permute-start(bf16[2,3,32,256]{3,2,1,0:T(8,128)(2,1)S(1)} %get-tuple-element.78), channel_id=1, source_target_pairs={{2,0},{4,2},{6,4},{8,6},{10,8},{12,10},{14,12},{3,1},{5,3},{7,5},{... | collective-permute-start | bytes 294920 | tf_op jit(solution)/shard_map/ppermute | solution.py:23
  78.1 5.0 %collective-permute-start.6 = (bf16[2,3,32,256]{3,2,1,0:T(8,128)(2,1)S(1)}, bf16[2,3,32,256]{3,2,1,0:T(8,128)(2,1)S(1)}, u32[]{:S(2)}, u32[]{:S(2)}) collective-permute-start(bf16[2,3,32,256]{3,2,1,0:T(8,128)(2,1)S(1)} %get-tuple-element.77), channel_id=1, source_target_pairs={{0,2},{2,4},{4,6},{6,8},{8,10},{10,12},{12,14},{1,3},{3,5},{5,7},{... | collective-permute-start | bytes 294920 | tf_op jit(solution)/shard_map/ppermute | solution.py:22
  84.2 2.3 %collective-permute-done.6 = bf16[2,3,32,256]{3,2,1,0:T(8,128)(2,1)S(1)} collective-permute-done((bf16[2,3,32,256]{3,2,1,0:T(8,128)(2,1)S(1)}, bf16[2,3,32,256]{3,2,1,0:T(8,128)(2,1)S(1)}, u32[]{:S(2)}, u32[]{:S(2)}) %collective-permute-start.6) | collective-permute-done | bytes 98336 | tf_op jit(solution)/shard_map/ppermute | solution.py:22
  86.9 7.9 %fusion.138 = (f32[2,16,32]{2,1,0:T(8,128)S(1)}, f32[2,16,32,256]{3,2,1,0:T(8,128)S(1)}) fusion(f32[256]{0:T(256)S(1)} %bitcast.212, bf16[2,22,38,256]{3,2,1,0:T(8,128)(2,1)S(1)} %select_maximum_fusion, f32[256]{0:T(256)S(1)} %bitcast.210, f32[256]{0:T(256)S(1)} %bitcast.216, f32[256]{0:T(256)S(1)} %bitcast.218, ...), kind=kLoop, calls=%fused_computation.202 | loop fusion | flops 40107008 | bytes 23843840 | tf_op jit(solution)/shard_map/reduce_sum | solution.py:59
  95.3 3.4 %fusion.40 = f32[2,16,32,256]{3,2,1,0:T(8,128)S(1)} fusion(f32[2,16,32,256]{3,2,1,0:T(8,128)} %get-tuple-element.198, f32[1024]{0:T(1024)S(1)} %bitcast.388, f32[2,16,32,256]{3,2,1,0:T(8,128)S(1)} %get-tuple-element.70, f32[2,16,32]{2,1,0:T(8,128)S(1)} %add_rsqrt_fusion, f32[2,16,32]{2,1,0:T(8,128)S(1)} %broadcast_multiply_fusion, f32[256]{0:T(256)S(1)} %bitcast.392, ...), kind=kOutput, calls=%fused_computation.50 | convolution fusion | flops 1085538304 | bytes 4207616 | tf_op jit(solution)/shard_map/trwf,fc->trwc/dot_general | solution.py:68
  98.7 2.2 %fusion.163 = (bf16[16,32,16]{1,2,0:T(8,128)(2,1)S(1)}, f32[2,16,32,16]{2,3,1,0:T(8,128)S(1)}) fusion(f32[2]{0:T(128)S(1)} %copy-done.6, f32[2,16,32,256]{3,2,1,0:T(8,128)S(1)} %fusion.40, f32[256,16]{0,1:T(8,128)S(1)} %copy-done.4), kind=kOutput, calls=%fused_computation.223 | convolution fusion | flops 50356224 | bytes 1146888 | tf_op jit(solution)/shard_map/trwd,dc->trwc/dot_general | solution.py:83
  100.8 1.9 %all-gather.1 = bf16[32,32,16]{1,2,0:T(8,128)(2,1)S(1)} all-gather(bf16[16,32,16]{1,2,0:T(8,128)(2,1)S(1)} %get-tuple-element.199), channel_id=3, replica_groups=mesh['groups'=2,'space'=8,'tm'=2] {'tm'}, dimensions={0}, use_global_device_ids=true | all-gather | bytes 49152 | tf_op jit(solution)/shard_map/all_gather | solution.py:30
  (61 shorter events, 12.3 us)
Async XLA Ops:
  0.0 1.0 copy-start
  1.2 8.9 %copy-start.2 = (f32[2,7,7,256]{3,0,2,1:T(2,128)S(1)}, f32[2,7,7,256]{3,0,2,1:T(2,128)}, u32[]{:S(2)}) copy-start(f32[2,7,7,256]{3,0,2,1:T(2,128)} %param.20) | copy-start | bytes 301060
  1.2 9.0 %copy-start.5 = (f32[2,1024]{1,0:T(2,128)S(1)}, f32[2,1024]{1,0:T(2,128)}, u32[]{:S(2)}) copy-start(f32[2,1024]{1,0:T(2,128)} %param.23) | copy-start | bytes 24580
  1.2 9.0 %copy-start.7 = (f32[2,256]{1,0:T(2,128)S(1)}, f32[2,256]{1,0:T(2,128)}, u32[]{:S(2)}) copy-start(f32[2,256]{1,0:T(2,128)} %param.21) | copy-start | bytes 6148
  3.2 7.6 %collective-permute-start.1 = (bf16[2,3,32,256]{3,2,1,0:T(8,128)(2,1)S(1)}, bf16[2,3,32,256]{3,2,1,0:T(8,128)(2,1)S(1)}, u32[]{:S(2)}, u32[]{:S(2)}) collective-permute-start(bf16[2,3,32,256]{3,2,1,0:T(8,128)(2,1)S(1)} %get-tuple-element.84), channel_id=1, source_target_pairs={{2,0},{4,2},{6,4},{8,6},{10,8},{12,10},{14,12},{3,1},{5,3},{7,5},{... | collective-permute-start | bytes 294920 | tf_op jit(solution)/shard_map/ppermute | solution.py:23
  4.5 8.6 %collective-permute-start = (bf16[2,3,32,256]{3,2,1,0:T(8,128)(2,1)S(1)}, bf16[2,3,32,256]{3,2,1,0:T(8,128)(2,1)S(1)}, u32[]{:S(2)}, u32[]{:S(2)}) collective-permute-start(bf16[2,3,32,256]{3,2,1,0:T(8,128)(2,1)S(1)} %get-tuple-element.83), channel_id=1, source_target_pairs={{0,2},{2,4},{4,6},{6,8},{8,10},{10,12},{12,14},{1,3},{3,5},{5,7},{... | collective-permute-start | bytes 294920 | tf_op jit(solution)/shard_map/ppermute | solution.py:22
  26.1 7.3 %collective-permute-start.3 = (bf16[2,3,32,256]{3,2,1,0:T(8,128)(2,1)S(1)}, bf16[2,3,32,256]{3,2,1,0:T(8,128)(2,1)S(1)}, u32[]{:S(2)}, u32[]{:S(2)}) collective-permute-start(bf16[2,3,32,256]{3,2,1,0:T(8,128)(2,1)S(1)} %get-tuple-element.82), channel_id=1, source_target_pairs={{2,0},{4,2},{6,4},{8,6},{10,8},{12,10},{14,12},{3,1},{5,3},{7,5},{... | collective-permute-start | bytes 294920 | tf_op jit(solution)/shard_map/ppermute | solution.py:23
  27.4 8.3 %collective-permute-start.2 = (bf16[2,3,32,256]{3,2,1,0:T(8,128)(2,1)S(1)}, bf16[2,3,32,256]{3,2,1,0:T(8,128)(2,1)S(1)}, u32[]{:S(2)}, u32[]{:S(2)}) collective-permute-start(bf16[2,3,32,256]{3,2,1,0:T(8,128)(2,1)S(1)} %get-tuple-element.81), channel_id=1, source_target_pairs={{0,2},{2,4},{4,6},{6,8},{8,10},{10,12},{12,14},{1,3},{3,5},{5,7},{... | collective-permute-start | bytes 294920 | tf_op jit(solution)/shard_map/ppermute | solution.py:22
  44.5 3.4 %copy-start.4 = (f32[256,16]{0,1:T(8,128)S(1)}, f32[256,16]{0,1:T(8,128)}, u32[]{:S(2)}) copy-start(f32[256,16]{0,1:T(8,128)} %param.25) | copy-start | bytes 49156
  44.5 3.4 %copy-start.6 = (f32[2]{0:T(128)S(1)}, f32[2]{0:T(128)}, u32[]{:S(2)}) copy-start(f32[2]{0:T(128)} %param.17) | copy-start | bytes 28
  50.9 2.1 %copy-start.1 = (f32[16,32,16]{1,2,0:T(8,128)S(1)}, f32[16,32,16]{1,2,0:T(8,128)}, u32[]{:S(2)}) copy-start(f32[16,32,16]{1,2,0:T(8,128)} %param.15) | copy-start | bytes 98308
  50.9 2.1 %copy-start.3 = (f32[16,256]{1,0:T(8,128)S(1)}, f32[16,256]{1,0:T(8,128)}, u32[]{:S(2)}) copy-start(f32[16,256]{1,0:T(8,128)} %param.18) | copy-start | bytes 49156
  54.0 7.5 %collective-permute-start.5 = (bf16[2,3,32,256]{3,2,1,0:T(8,128)(2,1)S(1)}, bf16[2,3,32,256]{3,2,1,0:T(8,128)(2,1)S(1)}, u32[]{:S(2)}, u32[]{:S(2)}) collective-permute-start(bf16[2,3,32,256]{3,2,1,0:T(8,128)(2,1)S(1)} %get-tuple-element.80), channel_id=1, source_target_pairs={{2,0},{4,2},{6,4},{8,6},{10,8},{12,10},{14,12},{3,1},{5,3},{7,5},{... | collective-permute-start | bytes 294920 | tf_op jit(solution)/shard_map/ppermute | solution.py:23
  55.3 8.5 %collective-permute-start.4 = (bf16[2,3,32,256]{3,2,1,0:T(8,128)(2,1)S(1)}, bf16[2,3,32,256]{3,2,1,0:T(8,128)(2,1)S(1)}, u32[]{:S(2)}, u32[]{:S(2)}) collective-permute-start(bf16[2,3,32,256]{3,2,1,0:T(8,128)(2,1)S(1)} %get-tuple-element.79), channel_id=1, source_target_pairs={{0,2},{2,4},{4,6},{6,8},{8,10},{10,12},{12,14},{1,3},{3,5},{5,7},{... | collective-permute-start | bytes 294920 | tf_op jit(solution)/shard_map/ppermute | solution.py:22
  76.8 7.4 %collective-permute-start.7 = (bf16[2,3,32,256]{3,2,1,0:T(8,128)(2,1)S(1)}, bf16[2,3,32,256]{3,2,1,0:T(8,128)(2,1)S(1)}, u32[]{:S(2)}, u32[]{:S(2)}) collective-permute-start(bf16[2,3,32,256]{3,2,1,0:T(8,128)(2,1)S(1)} %get-tuple-element.78), channel_id=1, source_target_pairs={{2,0},{4,2},{6,4},{8,6},{10,8},{12,10},{14,12},{3,1},{5,3},{7,5},{... | collective-permute-start | bytes 294920 | tf_op jit(solution)/shard_map/ppermute | solution.py:23
  78.1 8.3 %collective-permute-start.6 = (bf16[2,3,32,256]{3,2,1,0:T(8,128)(2,1)S(1)}, bf16[2,3,32,256]{3,2,1,0:T(8,128)(2,1)S(1)}, u32[]{:S(2)}, u32[]{:S(2)}) collective-permute-start(bf16[2,3,32,256]{3,2,1,0:T(8,128)(2,1)S(1)} %get-tuple-element.77), channel_id=1, source_target_pairs={{0,2},{2,4},{4,6},{6,8},{8,10},{10,12},{12,14},{1,3},{3,5},{5,7},{... | collective-permute-start | bytes 294920 | tf_op jit(solution)/shard_map/ppermute | solution.py:22
where the time goes:
time: 106 us; the launch traced here: 104 us
  other arithmetic  37.7 us (36%)
  starting transfers between devices  26.1 us (25%)
  matrix products  22.4 us (21%)
  waiting for transfers between devices  12.6 us (12%)
  blocking collectives  3.93 us (4%)
    reduce_sum x4, other arithmetic, convnext_block(): mean = jnp.mean(conv, axis=-1, keepdims=True)  31.9 us
    ppermute x4, starting transfers between devices, with_halo(): before = lax.ppermute(last, axis, up)  20.9 us
    dot_general x4, matrix products, convnext_block(): jnp.einsum('trwf,fc->trwc', hidden, down_weight[block], preferred_element...  14.9 us
    ppermute x4, waiting for transfers between devices, with_halo(): before = lax.ppermute(last, axis, up)  9.07 us
    ppermute x4, starting transfers between devices, with_halo(): after = lax.ppermute(first, axis, down)  5.17 us
    dot_general x2, matrix products, evaluate(): return jnp.einsum('trwd,dc->trwc', stream, out_weight, precision=HIGH)  4.3 us
    all_gather x2, blocking collectives, entering(): lax.all_gather(x.astype(jnp.bfloat16 if x.dtype == jnp.float32 else x.dty...  3.93 us
    ppermute x4, waiting for transfers between devices, with_halo(): after = lax.ppermute(first, axis, down)  3.5 us
  transfers between devices with their start and end apart: 8, of which 8 were waited for; matrix products, arithmetic and copies ran while one was open for 0% of the time, Pallas kernels for 0%

commit v1 on v0

v1 whole, which is shorter than its diff:
```python
import functools
import math

import jax
import jax.numpy as jnp
from jax import lax
from jax.experimental import pallas as pl
from jax.experimental.pallas import tpu as pltpu
from jax.sharding import PartitionSpec as P

HIGH = lax.Precision.HIGHEST
F32, BF16 = jnp.float32, jnp.bfloat16
COLS, CHAN, WIDTH, HIDDEN, LANES = 32, 16, 256, 1024, 128
OWN, TAPS, HALO = 8, 7, 3
FIRST = OWN + 2 * HALO
DEEP = OWN + 4 * HALO
PAD = 8
WIDE = COLS + 2 * PAD
TIMES = 3


def embed_times(steps, time_weight):
    half = time_weight.shape[0] // 2
    freqs = jnp.exp(-math.log(10000.0) * jnp.arange(half, dtype=F32) / half)
    angle = steps[:, None] * freqs[None, :]
    feats = jnp.concatenate([jnp.sin(angle), jnp.cos(angle)], axis=1)
    return jnp.dot(feats, time_weight, precision=HIGH)


def split(x):
    hi = x.astype(BF16)
    return hi, (x - hi.astype(F32)).astype(BF16)


def dot(a, b):
    return lax.dot_general(a, b, (((1,), (0,)), ((), ())), preferred_element_type=F32)


def dot_nt(a, b):
    return lax.dot_general(a, b, (((1,), (1,)), ((), ())), preferred_element_type=F32)


def lane_group(shape):
    return lax.broadcasted_iota(jnp.int32, shape, len(shape) - 1) // CHAN


def spreader():
    row = lax.broadcasted_iota(jnp.int32, (LANES, OWN * LANES), 0)
    col = lax.broadcasted_iota(jnp.int32, (LANES, OWN * LANES), 1)
    hit = (row // CHAN == col // LANES) & (row % CHAN == col % CHAN)
    return jnp.where(hit, 1.0, 0.0).astype(BF16)


def normalise(conv, gain):
    mean = jnp.mean(conv, axis=-1, keepdims=True)
    centered = conv - mean
    var = jnp.mean(centered * centered, axis=-1, keepdims=True)
    return (centered * lax.rsqrt(var + 1e-06) * gain).astype(BF16)


def gelu(x):
    inner = x * (0.7978845608028654 + 0.035677408136300125 * (x * x))
    half = 0.5 * x
    return half + half * jnp.tanh(inner)


def mlp(normed, up, bias, down):
    hidden = gelu(dot(normed, up) + bias).astype(BF16)
    return dot(hidden, down)


def sweep_kernel(
    count, first_time, flags, steps, state, temb, in_w, taps, gain, up_w, up_b, down_w, out_t,
    terms, shift, patch_hi, patch_lo, weff_hi, weff_lo, wide, conv_buf,
):
    turn, inside = flags[0], flags[1].astype(F32)

    weff_hi[...] = jnp.zeros_like(weff_hi)
    weff_lo[...] = jnp.zeros_like(weff_lo)
    for dy in range(TAPS):
        at = dy + turn * (TAPS - 1 - 2 * dy)
        for dx in range(TAPS):
            hi, lo = split(in_w[...] * taps[at, dx, 0:1, :])
            weff_hi[dy, dx * CHAN : (dx + 1) * CHAN, :] = hi
            weff_lo[dy, dx * CHAN : (dx + 1) * CHAN, :] = lo
    gap = jnp.zeros((3 * CHAN, WIDTH), F32)
    in_hi, in_lo = split(jnp.concatenate([gap, in_w[...], gap, gap[:CHAN]], axis=0))

    column = lax.broadcasted_iota(jnp.int32, (COLS, WIDTH), 0)
    by_row = []
    for dy in range(TAPS):
        at = dy + turn * (TAPS - 1 - 2 * dy)
        total = jnp.zeros((COLS, WIDTH), F32)
        for dx in range(TAPS):
            ok = (column + (dx - HALO) >= 0) & (column + (dx - HALO) < COLS)
            total = total + jnp.where(ok, taps[at, dx, 0:1, :], 0.0)
        by_row.append(total)
    ones = []
    for r in range(-HALO, OWN + HALO):
        total = jnp.zeros((COLS, WIDTH), F32)
        for dy in range(TAPS):
            total = total + (by_row[dy] if r + dy - HALO >= 0 else by_row[dy] * inside)
        ones.append(total)
    ones = jnp.concatenate(ones, axis=0)

    shift[...] = jnp.zeros_like(shift)
    wide[...] = jnp.zeros_like(wide)
    spread = spreader()
    group = lane_group((1, 1, LANES))

    def patches(piece, out):
        flat = dot(piece, spread)
        for j in range(OWN):
            lanes = slice(j * LANES, (j + 1) * LANES)
            if j < 2 * HALO:
                shift[2 * HALO - 1 - j, PAD : PAD + COLS, :] = flat[0:COLS, lanes]
            shift[2 * HALO + j, PAD : PAD + COLS, :] = flat[COLS : 2 * COLS, lanes]
            if j >= OWN - 2 * HALO:
                shift[2 * HALO + 15 - j, PAD : PAD + COLS, :] = flat[2 * COLS :, lanes]
        start = PAD - HALO
        picked = shift[:, start : start + COLS, :]
        for dx in range(1, TAPS):
            picked = jnp.where(group == dx, shift[:, start + dx : start + dx + COLS, :], picked)
        out[...] = picked.astype(BF16)

    def rows(ref, dy):
        return ref[dy : dy + FIRST].reshape(FIRST * COLS, LANES)

    for t in range(TIMES):
        if t < count:
            hi, lo = split(state[t].reshape(3 * COLS, LANES))
            patches(hi, patch_hi)
            patches(lo, patch_lo)
            base = jnp.zeros((FIRST * COLS, WIDTH), F32)
            for dy in range(TAPS):
                base = base + dot(rows(patch_hi, dy), weff_hi[dy])
                base = base + dot(rows(patch_lo, dy), weff_hi[dy])
                base = base + dot(rows(patch_hi, dy), weff_lo[dy])
            stream = dot(rows(patch_hi, HALO), in_hi) + dot(rows(patch_lo, HALO), in_hi) + dot(rows(patch_hi, HALO), in_lo)
        shown = temb[first_time + t : first_time + t + 1, :]
        normed = normalise(base + ones * shown, gain[0:1, :])
        after = stream + shown + mlp(normed, up_w[0], up_b[0:1, :], down_w[0])
        after = after.reshape(FIRST, COLS, WIDTH)
        for half in range(2):
            lanes = slice(half * LANES, (half + 1) * LANES)
            wide[2 * t + half, 0:HALO, PAD : PAD + COLS, :] = after[0:HALO, :, lanes] * inside
            wide[2 * t + half, HALO:, PAD : PAD + COLS, :] = after[HALO:, :, lanes]

    def depthwise(t, half):
        lanes = slice(half * LANES, (half + 1) * LANES)
        acc = [jnp.zeros((COLS, LANES), F32) for _ in range(OWN)]
        for dx in range(TAPS):
            tap = [taps[dy + turn * (TAPS - 1 - 2 * dy), dx, 1:2, lanes] for dy in range(TAPS)]
            for i in range(FIRST):
                x = wide[2 * t + half, i, PAD - HALO + dx : PAD - HALO + dx + COLS, :]
                for dy in range(TAPS):
                    if 0 <= i - dy < OWN:
                        acc[i - dy] = acc[i - dy] + x * tap[dy]
        for h in range(OWN):
            conv_buf[t, h, :, lanes] = acc[h]

    for half in range(2):
        lax.fori_loop(0, TIMES, lambda t, carry: (depthwise(t, half), carry)[1], 0)

    out_hi, out_lo = split(jnp.concatenate([out_t[...]] * 8, axis=0))
    for t in range(TIMES):
        normed = normalise(conv_buf[t].reshape(OWN * COLS, WIDTH), gain[1:2, :])
        stream = jnp.concatenate(
            [
                wide[2 * t + half, HALO : HALO + OWN, PAD : PAD + COLS, :].reshape(OWN * COLS, LANES)
                for half in range(2)
            ],
            axis=-1,
        )
        stream = stream + mlp(normed, up_w[1], up_b[1:2, :], down_w[1])
        hi, lo = split(stream)
        drift = dot_nt(hi, out_hi) + dot_nt(lo, out_hi) + dot_nt(hi, out_lo)
        drift = (drift * steps[first_time + t]).reshape(OWN, COLS, LANES)
        dense = drift[0]
        for j in range(1, OWN):
            dense = jnp.where(group[0] == j, drift[j], dense)
        terms[t] = dense


def sweep(first_time, flags, steps, state, temb, in_w, taps, gain, up_w, up_b, down_w, out_t):
    smem = pl.BlockSpec(memory_space=pltpu.SMEM)
    vmem = pl.BlockSpec(memory_space=pltpu.VMEM)
    return pl.pallas_call(
        functools.partial(sweep_kernel, state.shape[0], first_time),
        out_shape=jax.ShapeDtypeStruct((TIMES, COLS, LANES), F32),
        in_specs=[smem, smem] + [vmem] * 9,
        out_specs=vmem,
        scratch_shapes=[
            pltpu.VMEM((DEEP, WIDE, LANES), F32),
            pltpu.VMEM((DEEP, COLS, LANES), BF16),
            pltpu.VMEM((DEEP, COLS, LANES), BF16),
            pltpu.VMEM((TAPS, LANES, WIDTH), BF16),
            pltpu.VMEM((TAPS, LANES, WIDTH), BF16),
            pltpu.VMEM((2 * TIMES, FIRST, WIDE, LANES), F32),
            pltpu.VMEM((TIMES, OWN, COLS, WIDTH), F32),
        ],
        compiler_params=pltpu.CompilerParams(vmem_limit_bytes=48 * 2**20),
    )(flags, steps, state, temb, in_w, taps, gain, up_w, up_b, down_w, out_t)


def to_dense(x):
    return x.reshape(LANES, COLS).T


def from_dense(x):
    return x.reshape(x.shape[0], COLS, OWN, CHAN).transpose(0, 2, 1, 3)


def on_device(
    start_state, timesteps, step_sizes, in_weight, time_weight, conv_kernel, norm_gain, up_weight, up_bias, down_weight, out_weight,
):
    space = lax.axis_size("space")
    s, tm = lax.axis_index("space"), lax.axis_index("tm")
    beside = [(0, 1), (1, 0)]
    across = []
    for i in range(space - 1):
        across += [(2 * i + 1, 2 * i + 2), (2 * i + 2, 2 * i + 1)]

    def over_tm(x):
        return lax.ppermute(x, "tm", beside)

    def over_space(x):
        return lax.ppermute(x, ("space", "tm"), across)

    own_clock = jnp.concatenate([timesteps.astype(F32), step_sizes])
    other_clock = over_tm(own_clock)
    low = jnp.where(tm == 0, own_clock, other_clock)
    high = jnp.where(tm == 0, other_clock, own_clock)
    times = jnp.concatenate([low[:2], high[:2]])
    steps = jnp.concatenate([low[2:], high[2:]])
    temb = embed_times(times, time_weight)
    flags = jnp.stack([tm, jnp.where(tm == 0, s > 0, s < space - 1).astype(jnp.int32)]).astype(jnp.int32)

    turned = start_state.transpose(0, 2, 1)
    top, bottom = to_dense(turned[:OWN]), to_dense(turned[: OWN - 1 : -1])
    own = jnp.where(tm == 0, top, bottom)
    inner = jnp.where(tm == 0, bottom, top)
    outer = over_space(own)
    start = jnp.stack([outer, own, inner])

    weights = (in_weight, conv_kernel.transpose(1, 2, 0, 3), norm_gain, up_weight, up_bias, down_weight, out_weight.T)
    terms = sweep(0, flags, steps, start[None], temb, *weights)
    sent = terms.astype(BF16)
    outer_terms, inner_terms = over_space(sent), over_tm(sent)
    all_terms = jnp.stack([outer_terms.astype(F32), terms, inner_terms.astype(F32)], axis=1)
    one = start + all_terms[0]
    two = one + all_terms[1]
    three = two + all_terms[2]
    later = sweep(1, flags, steps, jnp.stack([one, two, three]), temb, *weights)
    n0 = one[1]
    n1 = n0 + later[0]
    n2 = n1 + later[1]
    n3 = n2 + later[2]
    early, late = jnp.stack([n0, n1]), jnp.stack([n2, n3])
    keep, give = jnp.where(tm == 0, early, late), jnp.where(tm == 0, late, early)
    got = over_tm(give)
    upper = from_dense(jnp.where(tm == 0, keep, got))
    lower = from_dense(jnp.where(tm == 0, got, keep))[:, ::-1]
    return jnp.concatenate([upper, lower], axis=1)


def solution(mesh):
    both = P(("groups", "tm"))
    return jax.shard_map(
        on_device,
        mesh=mesh,
        in_specs=(P(("groups", "space"), None, None), both, both) + (P(),) * 8,
        out_specs=P("tm", ("groups", "space"), None, None),
        check_vma=False,
    )
```

time: 106 us -> 55.1 us (0.52); the launches traced: 104 us -> 54.3 us
  other arithmetic: 37.7 us -> 2.99 us
  Pallas kernels: 0 us -> 31.8 us
  matrix products: 22.4 us -> 0.18 us
  starting transfers between devices: 26.1 us -> 11.9 us
  waiting for transfers between devices: 12.6 us -> 0.88 us
  local copies, waits for them, and re-layouts: 0.44 us -> 6.33 us
  blocking collectives: 3.93 us -> 0 us
    reduce_sum x8 -> x0, other arithmetic: 33.4 us -> none  [the longest x4 31.9 us: convnext_block(): mean = jnp.mean(conv, axis=-1, keepdims=True)]
    pallas_call x0 -> x2, Pallas kernels: none -> 31.8 us  [sweep(): pl.pallas_call(functools.partial(sweep_kernel, state.shape[0], first_time...]
    dot_general x8 -> x0, matrix products: 22.2 us -> none  [the longest x4 14.9 us: convnext_block(): jnp.einsum('trwf,fc->trwc', hidden, down_weight[block], preferred_element...]
    ppermute x8 -> x5, starting transfers between devices: 26.1 us -> 11.9 us  [the longest x3 10.4 us: over_tm(): return lax.ppermute(x, 'tm', beside)]
    ppermute x8 -> x5, waiting for transfers between devices: 12.6 us -> 0.88 us  [the longest x3 0.87 us: over_tm(): return lax.ppermute(x, 'tm', beside)]
    unnamed x16 -> x24, local copies, waits for them, and re-layouts: 0.22 us -> 5.09 us
    all_gather x2 -> x0, blocking collectives: 3.93 us -> none  [entering(): lax.all_gather(x.astype(jnp.bfloat16 if x.dtype == jnp.float32 else x.dty...]
    another operation x2 -> x6, other arithmetic: 1.52 us -> 0.14 us  [the longest x1 0.09 us: on_device(): jnp.stack([tm, jnp.where(tm == 0, s > 0, s < space - 1).astype(jnp.int32)])]
  transfers between devices with their start and end apart: 8 -> 5, of which waited for: 8 -> 1; matrix products, arithmetic and copies ran while one was open for 0% -> 5% of each run, Pallas kernels for 0% -> 0%
where the time goes in v1:
time: 55.1 us; the launch traced here: 54.3 us
  Pallas kernels  31.8 us (58%)
  starting transfers between devices  11.9 us (22%)
  local copies, waits for them, and re-layouts  6.33 us (11%)
  other arithmetic  2.99 us (5%)
  waiting for transfers between devices  0.88 us (2%)
    pallas_call x2, Pallas kernels, sweep(): pl.pallas_call(functools.partial(sweep_kernel, state.shape[0], first_time...  31.8 us
    ppermute x3, starting transfers between devices, over_tm(): return lax.ppermute(x, 'tm', beside)  10.4 us
    unnamed x24, local copies, waits for them, and re-layouts  5.09 us
    ppermute x2, starting transfers between devices, over_space(): return lax.ppermute(x, ('space', 'tm'), across)  1.5 us
  transfers between devices with their start and end apart: 5, of which 1 were waited for; matrix products, arithmetic and copies ran while one was open for 5% of the time, Pallas kernels for 0%

profile of v1, /device:TPU:0, one launch (start us, length us, event | category | flops | bytes accessed | tf_op | source)
XLA Modules:
  0.0 54.3 jit_solution(14982883235023892983)
XLA Ops:
  0.0 0.8 %convert_element_type.4 = f32[2]{0:T(128)S(1)} convert(s32[2]{0:T(128)} %param.12) | non-fusion elementwise | flops 2 | bytes 16 | tf_op jit(solution)/shard_map/convert_element_type | solution.py:230
  0.8 0.5 collective-permute-start.1
  1.3 0.8 %slice.53 = f32[8,16,32]{2,1,0:T(8,128)S(1)} slice(f32[16,16,32]{2,1,0:T(8,128)} %bitcast.54), slice={[8:16], [0:16], [0:32]} | slice | bytes 32768 | tf_op jit(solution)/shard_map/slice | solution.py:240
  2.1 0.8 %slice_select_fusion.1 = (f32[8,16,32]{2,1,0:T(8,128)S(1)}, f32[8,16,32]{2,1,0:T(8,128)S(1)}) fusion(f32[16,16,32]{2,1,0:T(8,128)} %bitcast.55, f32[8,16,32]{2,1,0:T(8,128)S(1)} %slice.53, pred[]{:T(512)S(6)} %eq.2), kind=kLoop, calls=%fused_computation.4 | loop fusion | flops 8192 | bytes 65537 | tf_op jit(solution)/shard_map/jit(_where)/select_n | solution.py:241
  3.1 0.7 %collective-permute-start = (f32[32,128]{1,0:T(8,128)S(1)}, f32[32,128]{1,0:T(8,128)S(1)}, u32[]{:S(2)}, u32[]{:S(2)}) collective-permute-start(f32[32,128]{1,0:T(8,128)S(1)} %bitcast.49), channel_id=1, source_target_pairs={{1,2},{2,1},{3,4},{4,3},{5,6},{6,5},{7,8},{8,7},{9,10},{10,9},{11,... | collective-permute-start | bytes 49160 | tf_op jit(solution)/shard_map/ppermute | solution.py:228
  3.8 0.1 pad_add_fusion.flags
  4.1 0.1 multiply_sine_fusion
  4.3 0.2 fusion.2.temb
  4.5 0.1 pad_maximum_fusion.7.steps
  4.6 0.7 %copy-done.9 = f32[2,1024]{1,0:T(2,128)S(1)} copy-done((f32[2,1024]{1,0:T(2,128)S(1)}, f32[2,1024]{1,0:T(2,128)}, u32[]{:S(2)}) %copy-start.9) | copy-done | bytes 8216
  5.3 1.2 %copy-done.2 = bf16[2,1024,256]{2,1,0:T(8,128)(2,1)S(1)} copy-done((bf16[2,1024,256]{2,1,0:T(8,128)(2,1)S(1)}, bf16[2,1024,256]{2,1,0:T(8,128)(2,1)}, u32[]{:S(2)}) %copy-start.2) | copy-done | bytes 1048600
  6.5 0.9 %copy-done.4 = f32[2,7,7,256]{3,0,2,1:T(2,128)S(1)} copy-done((f32[2,7,7,256]{3,0,2,1:T(2,128)S(1)}, f32[2,7,7,256]{3,0,2,1:T(2,128)}, u32[]{:S(2)}) %copy-start.4) | copy-done | bytes 100376
  7.4 0.7 %copy-done.6 = f32[16,256]{1,0:T(8,128)S(1)} copy-done((f32[16,256]{1,0:T(8,128)S(1)}, f32[16,256]{1,0:T(8,128)}, u32[]{:S(2)}) %copy-start.6) | copy-done | bytes 16408
  8.1 0.7 %copy-done.8 = f32[256,16]{0,1:T(8,128)S(1)} copy-done((f32[256,16]{0,1:T(8,128)S(1)}, f32[256,16]{0,1:T(8,128)}, u32[]{:S(2)}) %copy-start.8) | copy-done | bytes 16408
  8.8 12.5 %shard_map.109 = f32[3,32,128]{2,1,0:T(8,128)S(1)} custom-call(s32[2]{0:T(128)S(1)} %pad_add_fusion.flags, f32[4]{0:T(128)S(1)} %pad_maximum_fusion.7.steps, f32[1,3,32,128]{3,2,1,0:T(8,128)S(1)} %get-tuple-element.17.state, f32[4,256]{1,0:T(4,128)S(1)} %fusion.2.temb, f32[16,256]{1,0:T(8,128)S(1)} %copy-done.6, f32[7,7,2,256]{3,2,1,0:T(2,128)S(1)} %bitcast.41, ...), custom_call_target="tpu_custom_call" | custom-call | tf_op jit(solution)/shard_map/pallas_call | solution.py:188
  21.4 4.4 %collective-permute-start.3 = (bf16[3,32,128]{2,1,0:T(8,128)(2,1)S(1)}, bf16[3,32,128]{2,1,0:T(8,128)(2,1)S(1)}, u32[]{:S(2)}, u32[]{:S(2)}) collective-permute-start(bf16[3,32,128]{2,1,0:T(8,128)(2,1)S(1)} %convert_element_type.10), channel_id=1, source_target_pairs={{0,1},{1,0},{2,3},{3,2},{4,5},{5,4},{6,7},{7,6},{8,9},{9,8},{10,11... | collective-permute-start | bytes 73736 | tf_op jit(solution)/shard_map/ppermute | solution.py:225
  25.8 0.8 %collective-permute-start.2 = (bf16[3,32,128]{2,1,0:T(8,128)(2,1)S(1)}, bf16[3,32,128]{2,1,0:T(8,128)(2,1)S(1)}, u32[]{:S(2)}, u32[]{:S(2)}) collective-permute-start(bf16[3,32,128]{2,1,0:T(8,128)(2,1)S(1)} %convert_element_type.10), channel_id=1, source_target_pairs={{1,2},{2,1},{3,4},{4,3},{5,6},{6,5},{7,8},{8,7},{9,10},{10,9},{11,... | collective-permute-start | bytes 73736 | tf_op jit(solution)/shard_map/ppermute | solution.py:228
  26.8 0.8 %copy-done.5 = f32[2,7,7,256]{3,0,2,1:T(2,128)S(1)} copy-done((f32[2,7,7,256]{3,0,2,1:T(2,128)S(1)}, f32[2,7,7,256]{3,0,2,1:T(2,128)}, u32[]{:S(2)}) %copy-start.5) | copy-done | bytes 100376
  27.6 19.3 %shard_map.110 = f32[3,32,128]{2,1,0:T(8,128)S(1)} custom-call(s32[2]{0:T(128)S(1)} %pad_add_fusion.flags, f32[4]{0:T(128)S(1)} %pad_maximum_fusion.7.steps, f32[3,3,32,128]{3,2,1,0:T(8,128)S(1)} %pad_maximum_fusion.2.state, f32[4,256]{1,0:T(4,128)S(1)} %fusion.2.temb, f32[16,256]{1,0:T(8,128)S(1)} %copy-done.7, f32[7,7,2,256]{3,2,1,0:T(2,128)S(1)} %bitcast.42, ...), custom_call_target="tpu_custom_call" | custom-call | tf_op jit(solution)/shard_map/pallas_call | solution.py:188
  46.9 5.6 %collective-permute-start.4 = (f32[2,32,128]{2,1,0:T(8,128)S(1)}, f32[2,32,128]{2,1,0:T(8,128)S(1)}, u32[]{:S(2)}, u32[]{:S(2)}) collective-permute-start(f32[2,32,128]{2,1,0:T(8,128)S(1)} %fusion), channel_id=1, source_target_pairs={{0,1},{1,0},{2,3},{3,2},{4,5},{5,4},{6,7},{7,6},{8,9},{9,8},{10,11... | collective-permute-start | bytes 98312 | tf_op jit(solution)/shard_map/ppermute | solution.py:225
  52.5 0.9 %collective-permute-done.4 = f32[2,32,128]{2,1,0:T(8,128)S(1)} collective-permute-done((f32[2,32,128]{2,1,0:T(8,128)S(1)}, f32[2,32,128]{2,1,0:T(8,128)S(1)}, u32[]{:S(2)}, u32[]{:S(2)}) %collective-permute-start.4) | collective-permute-done | bytes 32800 | tf_op jit(solution)/shard_map/ppermute | solution.py:225
  53.4 0.1 copy.20
  53.5 0.1 copy.21
  53.6 0.7 %pad_maximum_fusion = f32[2,16,32,16]{2,3,1,0:T(8,128)} fusion(f32[2,8,32,16]{2,3,1,0:T(8,128)S(1)} %rev.7, f32[2,8,32,16]{2,3,1,0:T(8,128)S(1)} %bitcast.46), kind=kLoop, calls=%fused_computation | loop fusion | flops 16384 | bytes 131072 | tf_op jit(solution)/shard_map/concatenate | solution.py:264
  (41 shorter events, 0.6 us)
Async XLA Ops:
  0.0 4.3 %copy-start = (f32[256,256]{1,0:T(8,128)S(1)}, f32[256,256]{1,0:T(8,128)}, u32[]{:S(2)}) copy-start(f32[256,256]{1,0:T(8,128)} %param.15) | copy-start | bytes 786436
  0.0 0.8 %copy-start.11 = (f32[2]{0:T(128)S(1)}, f32[2]{0:T(128)}, u32[]{:S(2)}) copy-start(f32[2]{0:T(128)} %param.13) | copy-start | bytes 28
  0.0 4.6 %copy-start.1 = (bf16[2,256,1024]{2,1,0:T(8,128)(2,1)S(1)}, bf16[2,256,1024]{2,1,0:T(8,128)(2,1)}, u32[]{:S(2)}) copy-start(bf16[2,256,1024]{2,1,0:T(8,128)(2,1)} %up_w.3) | copy-start | bytes 3145732
  0.8 3.1 %collective-permute-start.1 = (f32[4]{0:T(128)S(1)}, f32[4]{0:T(128)S(1)}, u32[]{:S(2)}, u32[]{:S(2)}) collective-permute-start(f32[4]{0:T(128)S(1)} %pad_maximum_fusion.6), channel_id=1, source_target_pairs={{0,1},{1,0},{2,3},{3,2},{4,5},{5,4},{6,7},{7,6},{8,9},{9,8},{10,11... | collective-permute-start | bytes 56 | tf_op jit(solution)/shard_map/ppermute | solution.py:225
  3.1 1.5 %collective-permute-start = (f32[32,128]{1,0:T(8,128)S(1)}, f32[32,128]{1,0:T(8,128)S(1)}, u32[]{:S(2)}, u32[]{:S(2)}) collective-permute-start(f32[32,128]{1,0:T(8,128)S(1)} %bitcast.49), channel_id=1, source_target_pairs={{1,2},{2,1},{3,4},{4,3},{5,6},{6,5},{7,8},{8,7},{9,10},{10,9},{11,... | collective-permute-start | bytes 49160 | tf_op jit(solution)/shard_map/ppermute | solution.py:228
  4.6 0.7 %copy-start.9 = (f32[2,1024]{1,0:T(2,128)S(1)}, f32[2,1024]{1,0:T(2,128)}, u32[]{:S(2)}) copy-start(f32[2,1024]{1,0:T(2,128)} %up_b.3) | copy-start | bytes 24580
  4.6 0.7 %copy-start.10 = (f32[2,256]{1,0:T(2,128)S(1)}, f32[2,256]{1,0:T(2,128)}, u32[]{:S(2)}) copy-start(f32[2,256]{1,0:T(2,128)} %gain.3) | copy-start | bytes 6148
  5.3 1.2 %copy-start.2 = (bf16[2,1024,256]{2,1,0:T(8,128)(2,1)S(1)}, bf16[2,1024,256]{2,1,0:T(8,128)(2,1)}, u32[]{:S(2)}) copy-start(bf16[2,1024,256]{2,1,0:T(8,128)(2,1)} %down_w.3) | copy-start | bytes 3145732
  6.5 0.9 %copy-start.4 = (f32[2,7,7,256]{3,0,2,1:T(2,128)S(1)}, f32[2,7,7,256]{3,0,2,1:T(2,128)}, u32[]{:S(2)}) copy-start(f32[2,7,7,256]{3,0,2,1:T(2,128)} %param.16) | copy-start | bytes 301060
  7.4 0.7 %copy-start.6 = (f32[16,256]{1,0:T(8,128)S(1)}, f32[16,256]{1,0:T(8,128)}, u32[]{:S(2)}) copy-start(f32[16,256]{1,0:T(8,128)} %in_w.3) | copy-start | bytes 49156
  8.1 0.7 %copy-start.8 = (f32[256,16]{0,1:T(8,128)S(1)}, f32[256,16]{0,1:T(8,128)}, u32[]{:S(2)}) copy-start(f32[256,16]{0,1:T(8,128)} %param.21) | copy-start | bytes 49156
  21.4 5.4 %copy-start.3 = (bf16[2,1024,256]{2,1,0:T(8,128)(2,1)S(1)}, bf16[2,1024,256]{2,1,0:T(8,128)(2,1)}, u32[]{:S(2)}) copy-start(bf16[2,1024,256]{2,1,0:T(8,128)(2,1)} %down_w.3) | copy-start | bytes 3145732
  21.4 5.2 %collective-permute-start.3 = (bf16[3,32,128]{2,1,0:T(8,128)(2,1)S(1)}, bf16[3,32,128]{2,1,0:T(8,128)(2,1)S(1)}, u32[]{:S(2)}, u32[]{:S(2)}) collective-permute-start(bf16[3,32,128]{2,1,0:T(8,128)(2,1)S(1)} %convert_element_type.10), channel_id=1, source_target_pairs={{0,1},{1,0},{2,3},{3,2},{4,5},{5,4},{6,7},{7,6},{8,9},{9,8},{10,11... | collective-permute-start | bytes 73736 | tf_op jit(solution)/shard_map/ppermute | solution.py:225
  25.8 0.9 %collective-permute-start.2 = (bf16[3,32,128]{2,1,0:T(8,128)(2,1)S(1)}, bf16[3,32,128]{2,1,0:T(8,128)(2,1)S(1)}, u32[]{:S(2)}, u32[]{:S(2)}) collective-permute-start(bf16[3,32,128]{2,1,0:T(8,128)(2,1)S(1)} %convert_element_type.10), channel_id=1, source_target_pairs={{1,2},{2,1},{3,4},{4,3},{5,6},{6,5},{7,8},{8,7},{9,10},{10,9},{11,... | collective-permute-start | bytes 73736 | tf_op jit(solution)/shard_map/ppermute | solution.py:228
  26.7 0.9 %copy-start.5 = (f32[2,7,7,256]{3,0,2,1:T(2,128)S(1)}, f32[2,7,7,256]{3,0,2,1:T(2,128)}, u32[]{:S(2)}) copy-start(f32[2,7,7,256]{3,0,2,1:T(2,128)} %param.16) | copy-start | bytes 301060
  26.7 0.9 %copy-start.7 = (f32[16,256]{1,0:T(8,128)S(1)}, f32[16,256]{1,0:T(8,128)}, u32[]{:S(2)}) copy-start(f32[16,256]{1,0:T(8,128)} %in_w.3) | copy-start | bytes 49156
  46.9 6.4 %collective-permute-start.4 = (f32[2,32,128]{2,1,0:T(8,128)S(1)}, f32[2,32,128]{2,1,0:T(8,128)S(1)}, u32[]{:S(2)}, u32[]{:S(2)}) collective-permute-start(f32[2,32,128]{2,1,0:T(8,128)S(1)} %fusion), channel_id=1, source_target_pairs={{0,1},{1,0},{2,3},{3,2},{4,5},{5,4},{6,7},{7,6},{8,9},{9,8},{10,11... | collective-permute-start | bytes 98312 | tf_op jit(solution)/shard_map/ppermute | solution.py:225

commit v2 on v1

v2 whole, which is shorter than its diff:
```python
import functools
import math

import jax
import jax.numpy as jnp
from jax import lax
from jax.experimental import pallas as pl
from jax.experimental.pallas import tpu as pltpu
from jax.sharding import PartitionSpec as P

HIGH = lax.Precision.HIGHEST
F32, BF16 = jnp.float32, jnp.bfloat16
COLS, CHAN, WIDTH, HIDDEN, LANES = 32, 16, 256, 1024, 128
OWN, TAPS, HALO = 8, 7, 3
FIRST = OWN + 2 * HALO
DEEP = OWN + 4 * HALO
PAD = 8
WIDE = COLS + 2 * PAD
TIMES = 3


def embed_times(steps, time_weight):
    half = time_weight.shape[0] // 2
    freqs = jnp.exp(-math.log(10000.0) * jnp.arange(half, dtype=F32) / half)
    angle = steps[:, None] * freqs[None, :]
    feats = jnp.concatenate([jnp.sin(angle), jnp.cos(angle)], axis=1)
    return jnp.dot(feats, time_weight, precision=HIGH)


def split(x):
    hi = x.astype(BF16)
    return hi, (x - hi.astype(F32)).astype(BF16)


def dot(a, b):
    return lax.dot_general(a, b, (((1,), (0,)), ((), ())), preferred_element_type=F32)


def dot_nt(a, b):
    return lax.dot_general(a, b, (((1,), (1,)), ((), ())), preferred_element_type=F32)


def lane_group(shape):
    return lax.broadcasted_iota(jnp.int32, shape, len(shape) - 1) // CHAN


def spreader(wanted):
    row = lax.broadcasted_iota(jnp.int32, (LANES, OWN * LANES), 0)
    col = lax.broadcasted_iota(jnp.int32, (LANES, OWN * LANES), 1)
    hit = (row // CHAN == col // LANES) & (row % CHAN == col % CHAN) & wanted((col % LANES) // CHAN)
    return jnp.where(hit, 1.0, 0.0).astype(BF16)


def normalise(conv, gain):
    mean = jnp.mean(conv, axis=-1, keepdims=True)
    centered = conv - mean
    var = jnp.mean(centered * centered, axis=-1, keepdims=True)
    return (centered * lax.rsqrt(var + 1e-06) * gain).astype(BF16)


def gelu(x):
    inner = x * (0.7978845608028654 + 0.035677408136300125 * (x * x))
    half = 0.5 * x
    return half + half * jnp.tanh(inner)


def mlp(normed, up, bias, down):
    hidden = gelu(dot(normed, up) + bias).astype(BF16)
    return dot(hidden, down)


def prepare_kernel(flags, start, own, inner):
    turned = flags[0] == 1
    top = to_dense([start[h] for h in range(OWN)])
    bottom = to_dense([start[2 * OWN - 1 - h] for h in range(OWN)])
    own[...] = jnp.where(turned, bottom, top)
    inner[...] = jnp.where(turned, top, bottom)


def finish_kernel(flags, keep, got, out):
    turned = flags[0] == 1
    for t in range(2):
        top = jnp.where(turned, got[t], keep[t])
        bottom = jnp.where(turned, keep[t], got[t])
        out[t, 0:OWN] = top.T.reshape(OWN, CHAN, COLS)
        flipped = bottom.T.reshape(OWN, CHAN, COLS)
        for h in range(OWN):
            out[t, 2 * OWN - 1 - h] = flipped[h]


def to_dense(rows):
    return jnp.concatenate(rows, axis=0).T


def sweep_kernel(
    last, flags, steps, start, outer, mine, inner, temb, in_w, taps, gain, up_b, out_t, up_hbm, down_hbm,
    first_out, second_out,
    shift, patch, centre, weff, wide, conv_buf, up_w, down_w, sems,
):
    copies = []
    for block in range(2):
        copies.append(pltpu.make_async_copy(up_hbm.at[block], up_w.at[block], sems.at[2 * block]))
        copies.append(pltpu.make_async_copy(down_hbm.at[block], down_w.at[block], sems.at[2 * block + 1]))
    for copy in copies:
        copy.start()
    turn, inside = flags[0], flags[1].astype(F32)
    first_time = 1 if last else 0

    weff[...] = jnp.zeros_like(weff)
    for dy in range(TAPS):
        at = dy + turn * (TAPS - 1 - 2 * dy)
        for dx in range(TAPS):
            low = dy * LANES + dx * CHAN
            weff[low : low + CHAN, :] = (in_w[...] * taps[at, dx, 0:1, :]).astype(BF16)
    in_hi, in_lo = split(in_w[...])
    in_three = jnp.concatenate([in_hi, in_hi, in_lo, jnp.zeros((LANES - 3 * CHAN, WIDTH), BF16)], axis=0)

    column = lax.broadcasted_iota(jnp.int32, (COLS, WIDTH), 0)
    by_row = []
    for dy in range(TAPS):
        at = dy + turn * (TAPS - 1 - 2 * dy)
        total = jnp.zeros((COLS, WIDTH), F32)
        for dx in range(TAPS):
            ok = (column + (dx - HALO) >= 0) & (column + (dx - HALO) < COLS)
            total = total + jnp.where(ok, taps[at, dx, 0:1, :], 0.0)
        by_row.append(total)
    ones = []
    for r in range(-HALO, OWN + HALO):
        total = jnp.zeros((COLS, WIDTH), F32)
        for dy in range(TAPS):
            total = total + (by_row[dy] if r + dy - HALO >= 0 else by_row[dy] * inside)
        ones.append(total)
    ones = jnp.concatenate(ones, axis=0)

    shift[...] = jnp.zeros_like(shift)
    wide[...] = jnp.zeros_like(wide)
    group = lane_group((1, 1, LANES))
    spread = spreader(lambda column_group: column_group >= 0)
    three = jnp.concatenate(
        [spreader(lambda g: (g == 0) | (g == 2)), spreader(lambda g: g == 1)], axis=0
    )

    def by_rows(flat):
        found = {}
        for j in range(OWN):
            lanes = slice(j * LANES, (j + 1) * LANES)
            if j < 2 * HALO:
                found[2 * HALO - 1 - j] = flat[0:COLS, lanes]
            found[2 * HALO + j] = flat[COLS : 2 * COLS, lanes]
            if j >= OWN - 2 * HALO:
                found[2 * HALO + 15 - j] = flat[2 * COLS :, lanes]
        return found

    def rows(ref, dy):
        return ref[dy : dy + FIRST].reshape(FIRST * COLS, LANES)

    sums = [start[i] for i in range(3)]
    for t in range(TIMES):
        if last:
            sums[0] = sums[0] + outer[t].astype(F32)
            sums[1] = sums[1] + mine[t]
            sums[2] = sums[2] + inner[t].astype(F32)
            if t == 0:
                n0 = sums[1]
        if last or t == 0:
            hi, lo = split(jnp.concatenate(sums, axis=0))
            for i, x in by_rows(dot(hi, spread)).items():
                shift[i, PAD : PAD + COLS, :] = x
            for i, x in by_rows(dot(jnp.concatenate([hi, lo], axis=-1), three)).items():
                if HALO <= i < HALO + FIRST:
                    centre[i - HALO] = x.astype(BF16)
            at = PAD - HALO
            picked = shift[:, at : at + COLS, :]
            for dx in range(1, TAPS):
                picked = jnp.where(group == dx, shift[:, at + dx : at + dx + COLS, :], picked)
            patch[...] = picked.astype(BF16)
            base = dot(jnp.concatenate([rows(patch, dy) for dy in range(TAPS)], axis=-1), weff[...])
            stream = dot(rows(centre, 0), in_three)
        shown = temb[first_time + t : first_time + t + 1, :]
        normed = normalise(base + ones * shown, gain[0:1, :])
        if t == 0:
            copies[0].wait()
            copies[1].wait()
        after = stream + shown + mlp(normed, up_w[0], up_b[0:1, :], down_w[0])
        after = after.reshape(FIRST, COLS, WIDTH)
        for half in range(2):
            lanes = slice(half * LANES, (half + 1) * LANES)
            wide[2 * t + half, 0:HALO, PAD : PAD + COLS, :] = after[0:HALO, :, lanes] * inside
            wide[2 * t + half, HALO:, PAD : PAD + COLS, :] = after[HALO:, :, lanes]

    def depthwise(t, half):
        lanes = slice(half * LANES, (half + 1) * LANES)
        acc = [jnp.zeros((COLS, LANES), F32) for _ in range(OWN)]
        for dx in range(TAPS):
            tap = [taps[dy + turn * (TAPS - 1 - 2 * dy), dx, 1:2, lanes] for dy in range(TAPS)]
            for i in range(FIRST):
                x = wide[2 * t + half, i, PAD - HALO + dx : PAD - HALO + dx + COLS, :]
                for dy in range(TAPS):
                    if 0 <= i - dy < OWN:
                        acc[i - dy] = acc[i - dy] + x * tap[dy]
        for h in range(OWN):
            conv_buf[t, h, :, lanes] = acc[h]

    for half in range(2):
        lax.fori_loop(0, TIMES, lambda t, carry: (depthwise(t, half), carry)[1], 0)

    copies[2].wait()
    copies[3].wait()
    out_hi, out_lo = split(jnp.concatenate([out_t[...]] * 8, axis=0))
    out_three = jnp.concatenate([out_hi, out_hi, out_lo], axis=-1)
    terms = []
    for t in range(TIMES):
        normed = normalise(conv_buf[t].reshape(OWN * COLS, WIDTH), gain[1:2, :])
        stream = jnp.concatenate(
            [
                wide[2 * t + half, HALO : HALO + OWN, PAD : PAD + COLS, :].reshape(OWN * COLS, LANES)
                for half in range(2)
            ],
            axis=-1,
        )
        stream = stream + mlp(normed, up_w[1], up_b[1:2, :], down_w[1])
        hi, lo = split(stream)
        drift = dot_nt(jnp.concatenate([hi, lo, hi], axis=-1), out_three)
        drift = (drift * steps[first_time + t]).reshape(OWN, COLS, LANES)
        dense = drift[0]
        for j in range(1, OWN):
            dense = jnp.where(group[0] == j, drift[j], dense)
        terms.append(dense)
    if last:
        n1 = n0 + terms[0]
        n2 = n1 + terms[1]
        n3 = n2 + terms[2]
        turned = turn == 1
        for i, (early, late) in enumerate(((n0, n2), (n1, n3))):
            first_out[i] = jnp.where(turned, late, early)
            second_out[i] = jnp.where(turned, early, late)
    else:
        for t in range(TIMES):
            first_out[t] = terms[t]
            second_out[t] = terms[t].astype(BF16)


SMEM = pl.BlockSpec(memory_space=pltpu.SMEM)
VMEM = pl.BlockSpec(memory_space=pltpu.VMEM)
HBM = pl.BlockSpec(memory_space=pltpu.HBM)


def sweep(last, flags, steps, start, outer, mine, inner, temb, in_w, taps, gain, up_b, out_t, up_w, down_w):
    if last:
        outs = [jax.ShapeDtypeStruct((2, COLS, LANES), F32)] * 2
    else:
        outs = [jax.ShapeDtypeStruct((TIMES, COLS, LANES), kind) for kind in (F32, BF16)]
    return pl.pallas_call(
        functools.partial(sweep_kernel, last),
        out_shape=outs,
        in_specs=[SMEM, SMEM] + [VMEM] * 10 + [HBM] * 2,
        out_specs=[VMEM, VMEM],
        scratch_shapes=[
            pltpu.VMEM((DEEP, WIDE, LANES), F32),
            pltpu.VMEM((DEEP, COLS, LANES), BF16),
            pltpu.VMEM((FIRST, COLS, LANES), BF16),
            pltpu.VMEM((TAPS * LANES, WIDTH), BF16),
            pltpu.VMEM((2 * TIMES, FIRST, WIDE, LANES), F32),
            pltpu.VMEM((TIMES, OWN, COLS, WIDTH), F32),
            pltpu.VMEM(up_w.shape, BF16),
            pltpu.VMEM(down_w.shape, BF16),
            pltpu.SemaphoreType.DMA((4,)),
        ],
        compiler_params=pltpu.CompilerParams(vmem_limit_bytes=48 * 2**20),
    )(flags, steps, start, outer, mine, inner, temb, in_w, taps, gain, up_b, out_t, up_w, down_w)


def prepare(flags, turned_start):
    dense = jax.ShapeDtypeStruct((COLS, LANES), F32)
    return pl.pallas_call(
        prepare_kernel, out_shape=[dense, dense], in_specs=[SMEM, VMEM], out_specs=[VMEM, VMEM]
    )(flags, turned_start)


def finish(flags, keep, got):
    return pl.pallas_call(
        finish_kernel,
        out_shape=jax.ShapeDtypeStruct((2, 2 * OWN, CHAN, COLS), F32),
        in_specs=[SMEM, VMEM, VMEM],
        out_specs=VMEM,
    )(flags, keep, got)


def on_device(
    start_state, timesteps, step_sizes, in_weight, time_weight, conv_kernel, norm_gain, up_weight, up_bias, down_weight, out_weight,
):
    space = lax.axis_size("space")
    s, tm = lax.axis_index("space"), lax.axis_index("tm")
    beside = [(0, 1), (1, 0)]
    across = []
    for i in range(space - 1):
        across += [(2 * i + 1, 2 * i + 2), (2 * i + 2, 2 * i + 1)]

    def over_tm(x):
        return lax.ppermute(x, "tm", beside)

    def over_space(x):
        return lax.ppermute(x, ("space", "tm"), across)

    flags = jnp.stack([tm, jnp.where(tm == 0, s > 0, s < space - 1).astype(jnp.int32)]).astype(jnp.int32)
    own_clock = jnp.concatenate([timesteps.astype(F32), step_sizes])
    other_clock = over_tm(own_clock)
    own, inner = prepare(flags, start_state.transpose(0, 2, 1))
    outer = over_space(own)
    low = jnp.where(tm == 0, own_clock, other_clock)
    high = jnp.where(tm == 0, other_clock, own_clock)
    times = jnp.concatenate([low[:2], high[:2]])
    steps = jnp.concatenate([low[2:], high[2:]])
    temb = embed_times(times, time_weight)
    start = jnp.stack([outer, own, inner])

    weights = (temb, in_weight, conv_kernel.transpose(1, 2, 0, 3), norm_gain, up_bias, out_weight.T, up_weight, down_weight)
    blank = jnp.zeros((8, LANES), F32)
    terms, sent = sweep(False, flags, steps, start, blank, blank, blank, *weights)
    inner_terms, outer_terms = over_tm(sent), over_space(sent)
    keep, give = sweep(True, flags, steps, start, outer_terms, terms, inner_terms, *weights)
    return finish(flags, keep, over_tm(give)).transpose(0, 1, 3, 2)


def solution(mesh):
    both = P(("groups", "tm"))
    return jax.shard_map(
        on_device,
        mesh=mesh,
        in_specs=(P(("groups", "space"), None, None), both, both) + (P(),) * 8,
        out_specs=P("tm", ("groups", "space"), None, None),
        check_vma=False,
    )
```

time: 55.1 us -> 44.8 us (0.81)
  Pallas kernels: 31.8 us -> 24.7 us
  local copies, waits for them, and re-layouts: 6.33 us -> 4.84 us
  other arithmetic: 2.99 us -> 1.8 us
    pallas_call x2 -> x4, Pallas kernels: 31.8 us -> 24.7 us  [the longest x2 21.4 us: sweep(): pl.pallas_call(functools.partial(sweep_kernel, last), out_shape=outs, in_...]
    select_n x3 -> x0, other arithmetic: 0.87 us -> none  [the longest x1 0.85 us: on_device(): own = jnp.where(tm == 0, top, bottom)]
    slice x1 -> x0, local copies, waits for them, and re-layouts: 0.84 us -> none  [on_device(): top, bottom = (to_dense(turned[:OWN]), to_dense(turned[:OWN - 1:-1]))]
    concatenate x1 -> x0, other arithmetic: 0.72 us -> none  [on_device(): return jnp.concatenate([upper, lower], axis=1)]
    unnamed x24 -> x32, local copies, waits for them, and re-layouts: 5.09 us -> 4.77 us
  transfers between devices with their start and end apart: 5 -> 5, of which waited for: 1 -> 1; matrix products, arithmetic and copies ran while one was open for 5% -> 3% of each run, Pallas kernels for 0% -> 4%
where the time goes in v2:
time: 44.8 us; the launch traced here: 44.3 us
  Pallas kernels  24.7 us (55%)
  starting transfers between devices  11.8 us (26%)
  local copies, waits for them, and re-layouts  4.84 us (11%)
  other arithmetic  1.8 us (4%)
  waiting for transfers between devices  0.88 us (2%)
    pallas_call x2, Pallas kernels, sweep(): pl.pallas_call(functools.partial(sweep_kernel, last), out_shape=outs, in_...  21.4 us
    ppermute x3, starting transfers between devices, over_tm(): return lax.ppermute(x, 'tm', beside)  10.3 us
    unnamed x32, local copies, waits for them, and re-layouts  4.77 us
    pallas_call x1, Pallas kernels, finish(): pl.pallas_call(finish_kernel, out_shape=jax.ShapeDtypeStruct((2, 2 * OWN,...  1.62 us
    pallas_call x1, Pallas kernels, prepare(): pl.pallas_call(prepare_kernel, out_shape=[dense, dense], in_specs=[SMEM,...  1.59 us
    ppermute x2, starting transfers between devices, over_space(): return lax.ppermute(x, ('space', 'tm'), across)  1.48 us
  transfers between devices with their start and end apart: 5, of which 1 were waited for; matrix products, arithmetic and copies ran while one was open for 3% of the time, Pallas kernels for 4%

profile of v2, /device:TPU:0, one launch (start us, length us, event | category | flops | bytes accessed | tf_op | source)
XLA Modules:
  0.0 44.3 jit_solution(5629444795071527914)
XLA Ops:
  0.0 0.7 %convert_element_type.4 = f32[2]{0:T(128)S(1)} convert(s32[2]{0:T(128)} %param.12) | non-fusion elementwise | flops 2 | bytes 16 | tf_op jit(solution)/shard_map/convert_element_type | solution.py:306
  0.8 0.5 %collective-permute-start = (f32[4]{0:T(128)S(1)}, f32[4]{0:T(128)S(1)}, u32[]{:S(2)}, u32[]{:S(2)}) collective-permute-start(f32[4]{0:T(128)S(1)} %pad_maximum_fusion.1), channel_id=1, source_target_pairs={{0,1},{1,0},{2,3},{3,2},{4,5},{5,4},{6,7},{7,6},{8,9},{9,8},{10,11... | collective-permute-start | bytes 56 | tf_op jit(solution)/shard_map/ppermute | solution.py:300
  1.3 0.6 %pad_add_fusion.flags = s32[2]{0:T(128)} fusion(s32[1]{0:T(128)} %bitcast.1, s32[1]{0:T(128)} %bitcast), kind=kLoop, calls=%fused_computation.9 | loop fusion | flops 2 | bytes 16 | tf_op jit(solution)/shard_map/stack | solution.py:305
  1.9 1.6 %shard_map.109 = (f32[32,128]{1,0:T(8,128)}, f32[32,128]{1,0:T(8,128)}) custom-call(s32[2]{0:T(128)} %pad_add_fusion.flags, f32[16,16,32]{2,1,0:T(8,128)} %bitcast.14), custom_call_target="tpu_custom_call" | custom-call | tf_op jit(solution)/shard_map/pallas_call | solution.py:275
  3.5 0.7 %collective-permute-start.1 = (f32[32,128]{1,0:T(8,128)}, f32[32,128]{1,0:T(8,128)S(1)}, u32[]{:S(2)}, u32[]{:S(2)}) collective-permute-start(f32[32,128]{1,0:T(8,128)} %get-tuple-element.11), channel_id=1, source_target_pairs={{1,2},{2,1},{3,4},{4,3},{5,6},{6,5},{7,8},{8,7},{9,10},{10,9},{11,... | collective-permute-start | bytes 49160 | tf_op jit(solution)/shard_map/ppermute | solution.py:303
  4.1 0.1 broadcast_select_fusion.1
  4.2 0.1 fusion.5
  4.4 0.1 multiply_sine_fusion
  4.5 0.2 fusion.temb
  4.7 0.1 pad_maximum_fusion.2.steps
  4.9 0.4 copy-done.13
  5.3 0.4 copy-done.5
  5.7 0.3 copy-done.6
  6.0 1.2 %copy-done.1 = bf16[2,256,1024]{2,1,0:T(8,128)(2,1)S(1)} copy-done((bf16[2,256,1024]{2,1,0:T(8,128)(2,1)S(1)}, bf16[2,256,1024]{2,1,0:T(8,128)(2,1)}, u32[]{:S(2)}) %copy-start.1) | copy-done | bytes 1048600
  7.2 1.2 %copy-done.3 = bf16[2,1024,256]{2,1,0:T(8,128)(2,1)S(1)} copy-done((bf16[2,1024,256]{2,1,0:T(8,128)(2,1)S(1)}, bf16[2,1024,256]{2,1,0:T(8,128)(2,1)}, u32[]{:S(2)}) %copy-start.3) | copy-done | bytes 1048600
  8.4 10.1 %shard_map.110 = (f32[3,32,128]{2,1,0:T(8,128)S(1)}, bf16[3,32,128]{2,1,0:T(8,128)(2,1)S(1)}) custom-call(s32[2]{0:T(128)S(1)} %copy-done.11, f32[4]{0:T(128)S(1)} %pad_maximum_fusion.2.steps, f32[3,32,128]{2,1,0:T(8,128)S(1)} %pad_maximum_fusion.start, f32[8,128]{1,0:T(8,128)S(1)} %broadcast_in_dim.2.outer.mine.inner, ...), custom_call_target="tpu_custom_call" | custom-call | tf_op jit(solution)/shard_map/pallas_call | solution.py:253
  18.6 4.3 %collective-permute-start.3 = (bf16[3,32,128]{2,1,0:T(8,128)(2,1)S(1)}, bf16[3,32,128]{2,1,0:T(8,128)(2,1)S(1)}, u32[]{:S(2)}, u32[]{:S(2)}) collective-permute-start(bf16[3,32,128]{2,1,0:T(8,128)(2,1)S(1)} %get-tuple-element.13), channel_id=1, source_target_pairs={{0,1},{1,0},{2,3},{3,2},{4,5},{5,4},{6,7},{7,6},{8,9},{9,8},{10,11... | collective-permute-start | bytes 73736 | tf_op jit(solution)/shard_map/ppermute | solution.py:300
  22.9 0.8 %collective-permute-start.2 = (bf16[3,32,128]{2,1,0:T(8,128)(2,1)S(1)}, bf16[3,32,128]{2,1,0:T(8,128)(2,1)S(1)}, u32[]{:S(2)}, u32[]{:S(2)}) collective-permute-start(bf16[3,32,128]{2,1,0:T(8,128)(2,1)S(1)} %get-tuple-element.13), channel_id=1, source_target_pairs={{1,2},{2,1},{3,4},{4,3},{5,6},{6,5},{7,8},{8,7},{9,10},{10,9},{11,... | collective-permute-start | bytes 73736 | tf_op jit(solution)/shard_map/ppermute | solution.py:303
  23.8 11.3 %shard_map.111 = (f32[2,32,128]{2,1,0:T(8,128)S(1)}, f32[2,32,128]{2,1,0:T(8,128)S(1)}) custom-call(s32[2]{0:T(128)S(1)} %copy-done.11, f32[4]{0:T(128)S(1)} %pad_maximum_fusion.2.steps, f32[3,32,128]{2,1,0:T(8,128)S(1)} %pad_maximum_fusion.start, bf16[3,32,128]{2,1,0:T(8,128)(2,1)S(1)} %collective-permute-done.2.outer, ...), custom_call_target="tpu_custom_call" | custom-call | tf_op jit(solution)/shard_map/pallas_call | solution.py:253
  35.1 0.6 %copy-done.9 = f32[2,32,128]{2,1,0:T(8,128)} copy-done((f32[2,32,128]{2,1,0:T(8,128)}, f32[2,32,128]{2,1,0:T(8,128)S(1)}, u32[]{:S(2)}) %copy-start.9) | copy-done | bytes 32792
  35.7 5.5 %collective-permute-start.4 = (f32[2,32,128]{2,1,0:T(8,128)S(1)}, f32[2,32,128]{2,1,0:T(8,128)S(1)}, u32[]{:S(2)}, u32[]{:S(2)}) collective-permute-start(f32[2,32,128]{2,1,0:T(8,128)S(1)} %get-tuple-element.16), channel_id=1, source_target_pairs={{0,1},{1,0},{2,3},{3,2},{4,5},{5,4},{6,7},{7,6},{8,9},{9,8},{10,11... | collective-permute-start | bytes 98312 | tf_op jit(solution)/shard_map/ppermute | solution.py:300
  41.2 0.9 %collective-permute-done.4.got = f32[2,32,128]{2,1,0:T(8,128)S(1)} collective-permute-done((f32[2,32,128]{2,1,0:T(8,128)S(1)}, f32[2,32,128]{2,1,0:T(8,128)S(1)}, u32[]{:S(2)}, u32[]{:S(2)}) %collective-permute-start.4) | collective-permute-done | bytes 32800 | tf_op jit(solution)/shard_map/ppermute | solution.py:300
  42.1 0.6 %copy-done.12 = f32[2,32,128]{2,1,0:T(8,128)} copy-done((f32[2,32,128]{2,1,0:T(8,128)}, f32[2,32,128]{2,1,0:T(8,128)S(1)}, u32[]{:S(2)}) %copy-start.12) | copy-done | bytes 32792
  42.7 1.6 %shard_map.112 = f32[2,16,16,32]{3,2,1,0:T(8,128)} custom-call(s32[2]{0:T(128)} %pad_add_fusion.flags, f32[2,32,128]{2,1,0:T(8,128)} %copy-done.9, f32[2,32,128]{2,1,0:T(8,128)} %copy-done.12), custom_call_target="tpu_custom_call" | custom-call | tf_op jit(solution)/shard_map/pallas_call | solution.py:281
  (34 shorter events, 0.3 us)
Async XLA Ops:
  0.0 4.5 %copy-start = (f32[256,256]{1,0:T(8,128)S(1)}, f32[256,256]{1,0:T(8,128)}, u32[]{:S(2)}) copy-start(f32[256,256]{1,0:T(8,128)} %param.15) | copy-start | bytes 786436
  0.0 0.7 %copy-start.15 = (f32[2]{0:T(128)S(1)}, f32[2]{0:T(128)}, u32[]{:S(2)}) copy-start(f32[2]{0:T(128)} %param.13) | copy-start | bytes 28
  0.8 3.3 %collective-permute-start = (f32[4]{0:T(128)S(1)}, f32[4]{0:T(128)S(1)}, u32[]{:S(2)}, u32[]{:S(2)}) collective-permute-start(f32[4]{0:T(128)S(1)} %pad_maximum_fusion.1), channel_id=1, source_target_pairs={{0,1},{1,0},{2,3},{3,2},{4,5},{5,4},{6,7},{7,6},{8,9},{9,8},{10,11... | collective-permute-start | bytes 56 | tf_op jit(solution)/shard_map/ppermute | solution.py:300
  3.5 1.4 %collective-permute-start.1 = (f32[32,128]{1,0:T(8,128)}, f32[32,128]{1,0:T(8,128)S(1)}, u32[]{:S(2)}, u32[]{:S(2)}) collective-permute-start(f32[32,128]{1,0:T(8,128)} %get-tuple-element.11), channel_id=1, source_target_pairs={{1,2},{2,1},{3,4},{4,3},{5,6},{6,5},{7,8},{8,7},{9,10},{10,9},{11,... | collective-permute-start | bytes 49160 | tf_op jit(solution)/shard_map/ppermute | solution.py:303
  4.5 0.7 %copy-start.13 = (f32[32,128]{1,0:T(8,128)S(1)}, f32[32,128]{1,0:T(8,128)}, u32[]{:S(2)}) copy-start(f32[32,128]{1,0:T(8,128)} %get-tuple-element.11) | copy-start | bytes 49156
  4.5 0.7 %copy-start.14 = (f32[32,128]{1,0:T(8,128)S(1)}, f32[32,128]{1,0:T(8,128)}, u32[]{:S(2)}) copy-start(f32[32,128]{1,0:T(8,128)} %get-tuple-element.12) | copy-start | bytes 49156
  4.5 0.8 %copy-start.7 = (f32[256,16]{0,1:T(8,128)S(1)}, f32[256,16]{0,1:T(8,128)}, u32[]{:S(2)}) copy-start(f32[256,16]{0,1:T(8,128)} %param.21) | copy-start | bytes 49156
  4.5 0.7 %copy-start.8 = (f32[2,1024]{1,0:T(2,128)S(1)}, f32[2,1024]{1,0:T(2,128)}, u32[]{:S(2)}) copy-start(f32[2,1024]{1,0:T(2,128)} %up_b.3) | copy-start | bytes 24580
  4.7 0.9 %copy-start.5 = (f32[2,7,7,256]{3,0,2,1:T(2,128)S(1)}, f32[2,7,7,256]{3,0,2,1:T(2,128)}, u32[]{:S(2)}) copy-start(f32[2,7,7,256]{3,0,2,1:T(2,128)} %param.16) | copy-start | bytes 301060
  5.2 0.7 %copy-start.6 = (f32[16,256]{1,0:T(8,128)S(1)}, f32[16,256]{1,0:T(8,128)}, u32[]{:S(2)}) copy-start(f32[16,256]{1,0:T(8,128)} %in_w.3) | copy-start | bytes 49156
  5.2 0.7 %copy-start.10 = (f32[2,256]{1,0:T(2,128)S(1)}, f32[2,256]{1,0:T(2,128)}, u32[]{:S(2)}) copy-start(f32[2,256]{1,0:T(2,128)} %gain.3) | copy-start | bytes 6148
  5.2 0.7 %copy-start.11 = (s32[2]{0:T(128)S(1)}, s32[2]{0:T(128)}, u32[]{:S(2)}) copy-start(s32[2]{0:T(128)} %pad_add_fusion.flags) | copy-start | bytes 28
  6.0 1.2 %copy-start.1 = (bf16[2,256,1024]{2,1,0:T(8,128)(2,1)S(1)}, bf16[2,256,1024]{2,1,0:T(8,128)(2,1)}, u32[]{:S(2)}) copy-start(bf16[2,256,1024]{2,1,0:T(8,128)(2,1)} %up_hbm.3) | copy-start | bytes 3145732
  7.2 1.2 %copy-start.3 = (bf16[2,1024,256]{2,1,0:T(8,128)(2,1)S(1)}, bf16[2,1024,256]{2,1,0:T(8,128)(2,1)}, u32[]{:S(2)}) copy-start(bf16[2,1024,256]{2,1,0:T(8,128)(2,1)} %down_hbm.3) | copy-start | bytes 3145732
  8.4 15.3 %copy-start.2 = (bf16[2,256,1024]{2,1,0:T(8,128)(2,1)S(1)}, bf16[2,256,1024]{2,1,0:T(8,128)(2,1)}, u32[]{:S(2)}) copy-start(bf16[2,256,1024]{2,1,0:T(8,128)(2,1)} %up_hbm.3) | copy-start | bytes 3145732
  8.4 15.3 %copy-start.4 = (bf16[2,1024,256]{2,1,0:T(8,128)(2,1)S(1)}, bf16[2,1024,256]{2,1,0:T(8,128)(2,1)}, u32[]{:S(2)}) copy-start(bf16[2,1024,256]{2,1,0:T(8,128)(2,1)} %down_hbm.3) | copy-start | bytes 3145732
  18.6 5.2 %collective-permute-start.3 = (bf16[3,32,128]{2,1,0:T(8,128)(2,1)S(1)}, bf16[3,32,128]{2,1,0:T(8,128)(2,1)S(1)}, u32[]{:S(2)}, u32[]{:S(2)}) collective-permute-start(bf16[3,32,128]{2,1,0:T(8,128)(2,1)S(1)} %get-tuple-element.13), channel_id=1, source_target_pairs={{0,1},{1,0},{2,3},{3,2},{4,5},{5,4},{6,7},{7,6},{8,9},{9,8},{10,11... | collective-permute-start | bytes 73736 | tf_op jit(solution)/shard_map/ppermute | solution.py:300
  22.9 0.9 %collective-permute-start.2 = (bf16[3,32,128]{2,1,0:T(8,128)(2,1)S(1)}, bf16[3,32,128]{2,1,0:T(8,128)(2,1)S(1)}, u32[]{:S(2)}, u32[]{:S(2)}) collective-permute-start(bf16[3,32,128]{2,1,0:T(8,128)(2,1)S(1)} %get-tuple-element.13), channel_id=1, source_target_pairs={{1,2},{2,1},{3,4},{4,3},{5,6},{6,5},{7,8},{8,7},{9,10},{10,9},{11,... | collective-permute-start | bytes 73736 | tf_op jit(solution)/shard_map/ppermute | solution.py:303
  35.1 0.6 %copy-start.9 = (f32[2,32,128]{2,1,0:T(8,128)}, f32[2,32,128]{2,1,0:T(8,128)S(1)}, u32[]{:S(2)}) copy-start(f32[2,32,128]{2,1,0:T(8,128)S(1)} %get-tuple-element.15.keep) | copy-start | bytes 98308
  35.7 6.4 %collective-permute-start.4 = (f32[2,32,128]{2,1,0:T(8,128)S(1)}, f32[2,32,128]{2,1,0:T(8,128)S(1)}, u32[]{:S(2)}, u32[]{:S(2)}) collective-permute-start(f32[2,32,128]{2,1,0:T(8,128)S(1)} %get-tuple-element.16), channel_id=1, source_target_pairs={{0,1},{1,0},{2,3},{3,2},{4,5},{5,4},{6,7},{7,6},{8,9},{9,8},{10,11... | collective-permute-start | bytes 98312 | tf_op jit(solution)/shard_map/ppermute | solution.py:300
  42.1 0.6 %copy-start.12 = (f32[2,32,128]{2,1,0:T(8,128)}, f32[2,32,128]{2,1,0:T(8,128)S(1)}, u32[]{:S(2)}) copy-start(f32[2,32,128]{2,1,0:T(8,128)S(1)} %collective-permute-done.4.got) | copy-start | bytes 98308

commit v3 on v2

--- a/solution.py
+++ b/solution.py
@@ -86,6 +86,10 @@
         flipped = bottom.T.reshape(OWN, CHAN, COLS)
         for h in range(OWN):
             out[t, 2 * OWN - 1 - h] = flipped[h]
+
+
+def pinned(x):
+    return pltpu.with_memory_space_constraint(x, pltpu.HBM)
 
 
 def to_dense(rows):
@@ -243,6 +247,7 @@
 SMEM = pl.BlockSpec(memory_space=pltpu.SMEM)
 VMEM = pl.BlockSpec(memory_space=pltpu.VMEM)
 HBM = pl.BlockSpec(memory_space=pltpu.HBM)
+SMALL = pltpu.CompilerParams(vmem_limit_bytes=4 * 2**20)
 
 
 def sweep(last, flags, steps, start, outer, mine, inner, temb, in_w, taps, gain, up_b, out_t, up_w, down_w):
@@ -266,14 +271,14 @@
             pltpu.VMEM(down_w.shape, BF16),
             pltpu.SemaphoreType.DMA((4,)),
         ],
-        compiler_params=pltpu.CompilerParams(vmem_limit_bytes=48 * 2**20),
+        compiler_params=pltpu.CompilerParams(vmem_limit_bytes=24 * 2**20),
     )(flags, steps, start, outer, mine, inner, temb, in_w, taps, gain, up_b, out_t, up_w, down_w)
 
 
 def prepare(flags, turned_start):
     dense = jax.ShapeDtypeStruct((COLS, LANES), F32)
     return pl.pallas_call(
-        prepare_kernel, out_shape=[dense, dense], in_specs=[SMEM, VMEM], out_specs=[VMEM, VMEM]
+        prepare_kernel, out_shape=[dense, dense], in_specs=[SMEM, VMEM], out_specs=[VMEM, VMEM], compiler_params=SMALL
     )(flags, turned_start)
 
 
@@ -283,6 +288,7 @@
         out_shape=jax.ShapeDtypeStruct((2, 2 * OWN, CHAN, COLS), F32),
         in_specs=[SMEM, VMEM, VMEM],
         out_specs=VMEM,
+        compiler_params=SMALL,
     )(flags, keep, got)
 
 
@@ -314,7 +320,7 @@
     temb = embed_times(times, time_weight)
     start = jnp.stack([outer, own, inner])
 
-    weights = (temb, in_weight, conv_kernel.transpose(1, 2, 0, 3), norm_gain, up_bias, out_weight.T, up_weight, down_weight)
+    weights = (temb, in_weight, conv_kernel.transpose(1, 2, 0, 3), norm_gain, up_bias, out_weight.T, pinned(up_weight), pinned(down_weight))
     blank = jnp.zeros((8, LANES), F32)
     terms, sent = sweep(False, flags, steps, start, blank, blank, blank, *weights)
     inner_terms, outer_terms = over_tm(sent), over_space(sent)

time: 44.8 us -> 40.4 us (0.902)
  local copies, waits for them, and re-layouts: 4.84 us -> 1.79 us
  Pallas kernels: 24.7 us -> 23.8 us
  other arithmetic: 1.8 us -> 1.26 us
    unnamed x32 -> x16, local copies, waits for them, and re-layouts: 4.77 us -> 1.71 us
    pallas_call x1, Pallas kernels: 1.59 us -> 0.6 us  [prepare(): pl.pallas_call(prepare_kernel, out_shape=[dense, dense], in_specs=[SMEM,...]
    another operation x1, other arithmetic: 0.62 us -> 0.07 us  [on_device(): jnp.stack([tm, jnp.where(tm == 0, s > 0, s < space - 1).astype(jnp.int32)])]
  transfers between devices with their start and end apart: 5 -> 5, of which waited for: 1 -> 1; matrix products, arithmetic and copies ran while one was open for 3% -> 2% of each run, Pallas kernels for 4% -> 1%
where the time goes in v3:
time: 40.4 us; the launch traced here: 40 us
  Pallas kernels  23.8 us (59%)
  starting transfers between devices  12 us (30%)
  local copies, waits for them, and re-layouts  1.79 us (4%)
  other arithmetic  1.26 us (3%)
  waiting for transfers between devices  0.88 us (2%)
    pallas_call x2, Pallas kernels, sweep(): pl.pallas_call(functools.partial(sweep_kernel, last), out_shape=outs, in_...  21.8 us
    ppermute x3, starting transfers between devices, over_tm(): return lax.ppermute(x, 'tm', beside)  10.5 us
    unnamed x16, local copies, waits for them, and re-layouts  1.71 us
    ppermute x2, starting transfers between devices, over_space(): return lax.ppermute(x, ('space', 'tm'), across)  1.5 us
    pallas_call x1, Pallas kernels, finish(): pl.pallas_call(finish_kernel, out_shape=jax.ShapeDtypeStruct((2, 2 * OWN,...  1.38 us
    ppermute x3, waiting for transfers between devices, over_tm(): return lax.ppermute(x, 'tm', beside)  0.87 us
  transfers between devices with their start and end apart: 5, of which 1 were waited for; matrix products, arithmetic and copies ran while one was open for 2% of the time, Pallas kernels for 1%

profile of v3, /device:TPU:0, one launch (start us, length us, event | category | flops | bytes accessed | tf_op | source)
XLA Modules:
  0.0 40.0 jit_solution(8929642344539658842)
XLA Ops:
  0.0 0.7 %convert_element_type.4 = f32[2]{0:T(128)S(1)} convert(s32[2]{0:T(128)} %param.12) | non-fusion elementwise | flops 2 | bytes 16 | tf_op jit(solution)/shard_map/convert_element_type | solution.py:312
  0.7 0.1 pad_maximum_fusion.1
  0.8 0.5 %collective-permute-start = (f32[4]{0:T(128)S(1)}, f32[4]{0:T(128)S(1)}, u32[]{:S(2)}, u32[]{:S(2)}) collective-permute-start(f32[4]{0:T(128)S(1)} %pad_maximum_fusion.1), channel_id=1, source_target_pairs={{0,1},{1,0},{2,3},{3,2},{4,5},{5,4},{6,7},{7,6},{8,9},{9,8},{10,11... | collective-permute-start | bytes 56 | tf_op jit(solution)/shard_map/ppermute | solution.py:306
  1.3 0.1 pad_add_fusion.flags
  1.3 0.9 %copy-done.2 = f32[16,32,16]{1,2,0:T(8,128)S(1)} copy-done((f32[16,32,16]{1,2,0:T(8,128)S(1)}, f32[16,32,16]{1,2,0:T(8,128)}, u32[]{:S(2)}) %copy-start.2) | copy-done | bytes 32792
  2.2 0.6 %shard_map.109 = (f32[32,128]{1,0:T(8,128)S(1)}, f32[32,128]{1,0:T(8,128)S(1)}) custom-call(s32[2]{0:T(128)S(1)} %pad_add_fusion.flags, f32[16,16,32]{2,1,0:T(8,128)S(1)} %bitcast.12), custom_call_target="tpu_custom_call" | custom-call | tf_op jit(solution)/shard_map/pallas_call | solution.py:280
  2.8 0.7 %collective-permute-start.1 = (f32[32,128]{1,0:T(8,128)S(1)}, f32[32,128]{1,0:T(8,128)S(1)}, u32[]{:S(2)}, u32[]{:S(2)}) collective-permute-start(f32[32,128]{1,0:T(8,128)S(1)} %get-tuple-element.11), channel_id=1, source_target_pairs={{1,2},{2,1},{3,4},{4,3},{5,6},{6,5},{7,8},{8,7},{9,10},{10,9},{11,... | collective-permute-start | bytes 49160 | tf_op jit(solution)/shard_map/ppermute | solution.py:309
  3.5 0.1 broadcast_select_fusion.1
  3.6 0.1 fusion.5
  3.7 0.1 pad_maximum_fusion.3
  3.8 0.1 multiply_sine_fusion
  3.9 0.0 copy-start.4
  3.9 0.2 fusion.temb
  4.1 0.1 pad_maximum_fusion.2.steps
  4.2 0.4 copy-done.4
  4.6 0.4 %copy-done.1 = f32[2,7,7,256]{3,0,2,1:T(2,128)S(1)} copy-done((f32[2,7,7,256]{3,0,2,1:T(2,128)S(1)}, f32[2,7,7,256]{3,0,2,1:T(2,128)}, u32[]{:S(2)}) %copy-start.1) | copy-done | bytes 100376
  5.0 10.1 %shard_map.110 = (f32[3,32,128]{2,1,0:T(8,128)S(1)}, bf16[3,32,128]{2,1,0:T(8,128)(2,1)S(1)}) custom-call(s32[2]{0:T(128)S(1)} %pad_add_fusion.flags, f32[4]{0:T(128)S(1)} %pad_maximum_fusion.2.steps, f32[3,32,128]{2,1,0:T(8,128)S(1)} %pad_maximum_fusion.start, f32[8,128]{1,0:T(8,128)S(1)} %broadcast_in_dim.2.outer.mine.inner, ...), custom_call_target="tpu_custom_call" | custom-call | tf_op jit(solution)/shard_map/pallas_call | solution.py:258
  15.1 4.4 %collective-permute-start.3 = (bf16[3,32,128]{2,1,0:T(8,128)(2,1)S(1)}, bf16[3,32,128]{2,1,0:T(8,128)(2,1)S(1)}, u32[]{:S(2)}, u32[]{:S(2)}) collective-permute-start(bf16[3,32,128]{2,1,0:T(8,128)(2,1)S(1)} %get-tuple-element.13), channel_id=1, source_target_pairs={{0,1},{1,0},{2,3},{3,2},{4,5},{5,4},{6,7},{7,6},{8,9},{9,8},{10,11... | collective-permute-start | bytes 73736 | tf_op jit(solution)/shard_map/ppermute | solution.py:306
  19.6 0.8 %collective-permute-start.2 = (bf16[3,32,128]{2,1,0:T(8,128)(2,1)S(1)}, bf16[3,32,128]{2,1,0:T(8,128)(2,1)S(1)}, u32[]{:S(2)}, u32[]{:S(2)}) collective-permute-start(bf16[3,32,128]{2,1,0:T(8,128)(2,1)S(1)} %get-tuple-element.13), channel_id=1, source_target_pairs={{1,2},{2,1},{3,4},{4,3},{5,6},{6,5},{7,8},{8,7},{9,10},{10,9},{11,... | collective-permute-start | bytes 73736 | tf_op jit(solution)/shard_map/ppermute | solution.py:309
  20.4 0.0 collective-permute-done.3.inner
  20.4 11.7 %shard_map.111 = (f32[2,32,128]{2,1,0:T(8,128)S(1)}, f32[2,32,128]{2,1,0:T(8,128)S(1)}) custom-call(s32[2]{0:T(128)S(1)} %pad_add_fusion.flags, f32[4]{0:T(128)S(1)} %pad_maximum_fusion.2.steps, f32[3,32,128]{2,1,0:T(8,128)S(1)} %pad_maximum_fusion.start, bf16[3,32,128]{2,1,0:T(8,128)(2,1)S(1)} %collective-permute-done.2.outer, ...), custom_call_target="tpu_custom_call" | custom-call | tf_op jit(solution)/shard_map/pallas_call | solution.py:258
  32.2 5.6 %collective-permute-start.4 = (f32[2,32,128]{2,1,0:T(8,128)S(1)}, f32[2,32,128]{2,1,0:T(8,128)S(1)}, u32[]{:S(2)}, u32[]{:S(2)}) collective-permute-start(f32[2,32,128]{2,1,0:T(8,128)S(1)} %get-tuple-element.16), channel_id=1, source_target_pairs={{0,1},{1,0},{2,3},{3,2},{4,5},{5,4},{6,7},{7,6},{8,9},{9,8},{10,11... | collective-permute-start | bytes 98312 | tf_op jit(solution)/shard_map/ppermute | solution.py:306
  37.7 0.9 %collective-permute-done.4.got = f32[2,32,128]{2,1,0:T(8,128)S(1)} collective-permute-done((f32[2,32,128]{2,1,0:T(8,128)S(1)}, f32[2,32,128]{2,1,0:T(8,128)S(1)}, u32[]{:S(2)}, u32[]{:S(2)}) %collective-permute-start.4) | collective-permute-done | bytes 32800 | tf_op jit(solution)/shard_map/ppermute | solution.py:306
  38.6 1.4 %shard_map.112 = f32[2,16,16,32]{3,2,1,0:T(8,128)} custom-call(s32[2]{0:T(128)S(1)} %pad_add_fusion.flags, f32[2,32,128]{2,1,0:T(8,128)S(1)} %get-tuple-element.15.keep, f32[2,32,128]{2,1,0:T(8,128)S(1)} %collective-permute-done.4.got), custom_call_target="tpu_custom_call" | custom-call | tf_op jit(solution)/shard_map/pallas_call | solution.py:286
  (18 shorter events, 0.1 us)
Async XLA Ops:
  0.0 3.9 %copy-start = (f32[256,256]{1,0:T(8,128)S(1)}, f32[256,256]{1,0:T(8,128)}, u32[]{:S(2)}) copy-start(f32[256,256]{1,0:T(8,128)} %param.15) | copy-start | bytes 786436
  0.0 0.7 %copy-start.7 = (f32[2]{0:T(128)S(1)}, f32[2]{0:T(128)}, u32[]{:S(2)}) copy-start(f32[2]{0:T(128)} %param.13) | copy-start | bytes 28
  0.8 2.7 %collective-permute-start = (f32[4]{0:T(128)S(1)}, f32[4]{0:T(128)S(1)}, u32[]{:S(2)}, u32[]{:S(2)}) collective-permute-start(f32[4]{0:T(128)S(1)} %pad_maximum_fusion.1), channel_id=1, source_target_pairs={{0,1},{1,0},{2,3},{3,2},{4,5},{5,4},{6,7},{7,6},{8,9},{9,8},{10,11... | collective-permute-start | bytes 56 | tf_op jit(solution)/shard_map/ppermute | solution.py:306
  1.3 0.9 %copy-start.2 = (f32[16,32,16]{1,2,0:T(8,128)S(1)}, f32[16,32,16]{1,2,0:T(8,128)}, u32[]{:S(2)}) copy-start(f32[16,32,16]{1,2,0:T(8,128)} %param.11) | copy-start | bytes 98308
  2.8 1.4 %collective-permute-start.1 = (f32[32,128]{1,0:T(8,128)S(1)}, f32[32,128]{1,0:T(8,128)S(1)}, u32[]{:S(2)}, u32[]{:S(2)}) collective-permute-start(f32[32,128]{1,0:T(8,128)S(1)} %get-tuple-element.11), channel_id=1, source_target_pairs={{1,2},{2,1},{3,4},{4,3},{5,6},{6,5},{7,8},{8,7},{9,10},{10,9},{11,... | collective-permute-start | bytes 49160 | tf_op jit(solution)/shard_map/ppermute | solution.py:309
  3.9 0.7 %copy-start.4 = (f32[256,16]{0,1:T(8,128)S(1)}, f32[256,16]{0,1:T(8,128)}, u32[]{:S(2)}) copy-start(f32[256,16]{0,1:T(8,128)} %param.21) | copy-start | bytes 49156
  3.9 0.7 %copy-start.5 = (f32[2,1024]{1,0:T(2,128)S(1)}, f32[2,1024]{1,0:T(2,128)}, u32[]{:S(2)}) copy-start(f32[2,1024]{1,0:T(2,128)} %up_b.3) | copy-start | bytes 24580
  4.1 0.9 %copy-start.1 = (f32[2,7,7,256]{3,0,2,1:T(2,128)S(1)}, f32[2,7,7,256]{3,0,2,1:T(2,128)}, u32[]{:S(2)}) copy-start(f32[2,7,7,256]{3,0,2,1:T(2,128)} %param.16) | copy-start | bytes 301060
  4.2 0.8 %copy-start.3 = (f32[16,256]{1,0:T(8,128)S(1)}, f32[16,256]{1,0:T(8,128)}, u32[]{:S(2)}) copy-start(f32[16,256]{1,0:T(8,128)} %in_w.3) | copy-start | bytes 49156
  4.2 0.8 %copy-start.6 = (f32[2,256]{1,0:T(2,128)S(1)}, f32[2,256]{1,0:T(2,128)}, u32[]{:S(2)}) copy-start(f32[2,256]{1,0:T(2,128)} %gain.3) | copy-start | bytes 6148
  15.1 5.3 %collective-permute-start.3 = (bf16[3,32,128]{2,1,0:T(8,128)(2,1)S(1)}, bf16[3,32,128]{2,1,0:T(8,128)(2,1)S(1)}, u32[]{:S(2)}, u32[]{:S(2)}) collective-permute-start(bf16[3,32,128]{2,1,0:T(8,128)(2,1)S(1)} %get-tuple-element.13), channel_id=1, source_target_pairs={{0,1},{1,0},{2,3},{3,2},{4,5},{5,4},{6,7},{7,6},{8,9},{9,8},{10,11... | collective-permute-start | bytes 73736 | tf_op jit(solution)/shard_map/ppermute | solution.py:306
  19.6 0.9 %collective-permute-start.2 = (bf16[3,32,128]{2,1,0:T(8,128)(2,1)S(1)}, bf16[3,32,128]{2,1,0:T(8,128)(2,1)S(1)}, u32[]{:S(2)}, u32[]{:S(2)}) collective-permute-start(bf16[3,32,128]{2,1,0:T(8,128)(2,1)S(1)} %get-tuple-element.13), channel_id=1, source_target_pairs={{1,2},{2,1},{3,4},{4,3},{5,6},{6,5},{7,8},{8,7},{9,10},{10,9},{11,... | collective-permute-start | bytes 73736 | tf_op jit(solution)/shard_map/ppermute | solution.py:309
  32.2 6.4 %collective-permute-start.4 = (f32[2,32,128]{2,1,0:T(8,128)S(1)}, f32[2,32,128]{2,1,0:T(8,128)S(1)}, u32[]{:S(2)}, u32[]{:S(2)}) collective-permute-start(f32[2,32,128]{2,1,0:T(8,128)S(1)} %get-tuple-element.16), channel_id=1, source_target_pairs={{0,1},{1,0},{2,3},{3,2},{4,5},{5,4},{6,7},{7,6},{8,9},{9,8},{10,11... | collective-permute-start | bytes 98312 | tf_op jit(solution)/shard_map/ppermute | solution.py:306

commit v4 on v3

v4 whole, which is shorter than its diff:
```python
import functools
import math

import jax
import jax.numpy as jnp
from jax import lax
from jax.experimental import pallas as pl
from jax.experimental.pallas import tpu as pltpu
from jax.sharding import PartitionSpec as P

HIGH = lax.Precision.HIGHEST
F32, BF16 = jnp.float32, jnp.bfloat16
COLS, CHAN, WIDTH, HIDDEN, LANES = 32, 16, 256, 1024, 128
OWN, TAPS, HALO = 8, 7, 3
REACH = 2 * HALO
PAD = 8
WIDE = COLS + 2 * PAD
TIMES = 3
CHUNK = 256


def split(x):
    hi = x.astype(BF16)
    return hi, (x - hi.astype(F32)).astype(BF16)


def dot(a, b):
    return lax.dot_general(a, b, (((1,), (0,)), ((), ())), preferred_element_type=F32)


def dot_nt(a, b):
    return lax.dot_general(a, b, (((1,), (1,)), ((), ())), preferred_element_type=F32)


def lane_group(shape):
    return lax.broadcasted_iota(jnp.int32, shape, len(shape) - 1) // CHAN


def spreader(wanted):
    row = lax.broadcasted_iota(jnp.int32, (LANES, OWN * LANES), 0)
    col = lax.broadcasted_iota(jnp.int32, (LANES, OWN * LANES), 1)
    hit = (row // CHAN == col // LANES) & (row % CHAN == col % CHAN) & wanted((col % LANES) // CHAN)
    return jnp.where(hit, 1.0, 0.0).astype(BF16)


def normalise(conv, gain):
    mean = jnp.mean(conv, axis=-1, keepdims=True)
    centered = conv - mean
    var = jnp.mean(centered * centered, axis=-1, keepdims=True)
    return (centered * lax.rsqrt(var + 1e-06) * gain).astype(BF16)


def gelu(x):
    x = x.astype(BF16)
    inner = x * (BF16(0.7978845608028654) + BF16(0.035677408136300125) * (x * x))
    half = BF16(0.5) * x
    return half + half * jnp.tanh(inner)


def interleave(first, second):
    total = max(len(first), len(second))
    for i in range(total):
        for steps in (first, second):
            for at in range(i * len(steps) // total, (i + 1) * len(steps) // total):
                steps[at]()


def prepare_kernel(flags, times, sizes, start, own, inner, clock):
    turned = flags[0] == 1
    top = to_dense([start[h] for h in range(OWN)])
    bottom = to_dense([start[2 * OWN - 1 - h] for h in range(OWN)])
    own[...] = jnp.where(turned, bottom, top)
    inner[...] = jnp.where(turned, top, bottom)
    lane = lax.broadcasted_iota(jnp.int32, (8, LANES), 1)
    values = (times[0].astype(F32), times[1].astype(F32), sizes[0], sizes[1])
    filled = jnp.zeros((8, LANES), F32)
    for i, value in enumerate(values):
        filled = jnp.where(lane == i, value, filled)
    clock[...] = filled


def finish_kernel(flags, keep, got, out):
    turned = flags[0] == 1
    for t in range(2):
        top = jnp.where(turned, got[t], keep[t])
        bottom = jnp.where(turned, keep[t], got[t])
        out[t, 0:OWN] = top.T.reshape(OWN, CHAN, COLS)
        flipped = bottom.T.reshape(OWN, CHAN, COLS)
        for h in range(OWN):
            out[t, 2 * OWN - 1 - h] = flipped[h]


def pinned(x):
    return pltpu.with_memory_space_constraint(x, pltpu.HBM)


def to_dense(rows):
    return jnp.concatenate(rows, axis=0).T


def row_of(turn, dy):
    return dy + turn * (TAPS - 1 - 2 * dy)


def both_clocks(turn, mine, other):
    first = turn == 0
    return jnp.where(first, mine[0:1, :], other[0:1, :]), jnp.where(first, other[0:1, :], mine[0:1, :])


def embed(turn, mine, other, time_w):
    low, high = both_clocks(turn, mine, other)
    steps = jnp.concatenate([low[:, 0:1], low[:, 1:2], high[:, 0:1], high[:, 1:2]] * 2, axis=0)
    lane = lax.broadcasted_iota(jnp.int32, (1, LANES), 1).astype(F32)
    angle = steps * jnp.exp(lane * (-math.log(10000.0) / LANES))
    feats = jnp.concatenate([jnp.sin(angle), jnp.cos(angle)], axis=1)
    return lax.dot_general(feats, time_w[...], (((1,), (0,)), ((), ())), precision=HIGH, preferred_element_type=F32)


def make_weff(turn, in_w, taps, weff):
    weff[...] = jnp.zeros_like(weff)
    for dy in range(TAPS):
        for dx in range(TAPS):
            low = dy * LANES + dx * CHAN
            weff[low : low + CHAN, :] = (in_w[...] * taps[row_of(turn, dy), dx, 0:1, :]).astype(BF16)


def make_by_row(turn, taps, by_row):
    column = lax.broadcasted_iota(jnp.int32, (COLS, WIDTH), 0)
    for dy in range(TAPS):
        total = jnp.zeros((COLS, WIDTH), F32)
        for dx in range(TAPS):
            ok = (column + (dx - HALO) >= 0) & (column + (dx - HALO) < COLS)
            total = total + jnp.where(ok, taps[row_of(turn, dy), dx, 0:1, :], 0.0)
        by_row[dy] = total


def three_in(in_w):
    hi, lo = split(in_w[...])
    return jnp.concatenate([hi, hi, lo, jnp.zeros((LANES - 3 * CHAN, WIDTH), BF16)], axis=0)


def block_zero(sums, place, first, count, weff, in_three, shift, patch, centre, spread, three):
    rows = count + REACH
    hi, lo = split(jnp.concatenate(sums, axis=0))

    def spots(flat):
        for k in range(len(sums)):
            for j in range(OWN):
                i = place(k, j)
                if i is not None:
                    yield i, flat[k * COLS : (k + 1) * COLS, j * LANES : (j + 1) * LANES]

    for i, x in spots(dot(hi, spread)):
        shift[i, PAD : PAD + COLS, :] = x
    for i, x in spots(dot(jnp.concatenate([hi, lo], axis=-1), three)):
        if HALO <= i < HALO + count:
            centre[i - HALO] = x.astype(BF16)
    group = lane_group((1, 1, LANES))
    at = PAD - HALO
    picked = shift[0:rows, at : at + COLS, :]
    for dx in range(1, TAPS):
        picked = jnp.where(group == dx, shift[0:rows, at + dx : at + dx + COLS, :], picked)
    patch[...] = picked.astype(BF16)
    wide = [patch[dy : dy + count].reshape(count * COLS, LANES) for dy in range(TAPS)]
    base = dot(jnp.concatenate(wide, axis=-1), weff[...])
    return base, dot(centre[...].reshape(count * COLS, LANES), in_three)


def pointwise(get, block, up_w, up_b, down_w, put):
    hidden = []

    def piece(low):
        upper = dot(get(), up_w[block, :, low : low + CHUNK]) + up_b[block : block + 1, low : low + CHUNK]
        hidden.append(gelu(upper))

    steps = [functools.partial(piece, low) for low in range(0, HIDDEN, CHUNK)]
    steps.append(lambda: put(dot(jnp.concatenate(hidden, axis=-1), down_w[block])))
    return steps


def depthwise(turn, taps, source, pairs, begin, done):
    def piece(half, heights):
        lanes = slice(half * LANES, (half + 1) * LANES)
        acc = {h: begin(h, half) for h in heights}
        needed = sorted({i for h in heights for i in pairs[h]})
        for dx in range(TAPS):
            for i in needed:
                x = source(i, half, dx)
                for h in heights:
                    if i in pairs[h]:
                        acc[h] = acc[h] + x * taps[row_of(turn, i - h + HALO), dx, 1:2, lanes]
        for h in heights:
            done(h, half, acc[h])

    heights = sorted(pairs)
    groups = [heights[i : i + 4] for i in range(0, len(heights), 4)]
    return [functools.partial(piece, half, group) for half in range(2) for group in groups]


NEAR = range(HALO, OWN + HALO)
EDGE = range(-HALO, HALO)


def pairs_of(rows):
    found = {h: [i for i in rows if abs(i - h) <= HALO] for h in range(OWN)}
    return {h: listed for h, listed in found.items() if listed}


def near_kernel(last, *refs):
    if last:
        (flags, own, inner, mine, inner_terms, temb, weff, by_row, up_w, down_w, in_w, taps, gain, up_b,
         partial, kept, shift, patch, centre, *wide) = refs
        turn = flags[0]
        copies = []
    else:
        (flags, own, inner, clock, other_clock, time_w, up_hbm, down_hbm, in_w, taps, gain, up_b,
         partial, kept, temb, weff, by_row, up_w, down_w, shift, patch, centre, *wide, sems) = refs
        turn = flags[0]
        copies = []
        for block in range(2):
            copies.append(pltpu.make_async_copy(up_hbm.at[block], up_w.at[block], sems.at[2 * block]))
            copies.append(pltpu.make_async_copy(down_hbm.at[block], down_w.at[block], sems.at[2 * block + 1]))
        for copy in copies:
            copy.start()
        make_weff(turn, in_w, taps, weff)
        make_by_row(turn, taps, by_row)
        temb[...] = embed(turn, clock, other_clock, time_w)
    first_time = 1 if last else 0
    count = len(NEAR)
    ones = by_row[0]
    for dy in range(1, TAPS):
        ones = ones + by_row[dy]
    ones = jnp.concatenate([ones] * count, axis=0)
    shift[...] = jnp.zeros_like(shift)
    for ref in wide:
        ref[...] = jnp.zeros_like(ref)
    spread = spreader(lambda g: g >= 0)
    three = jnp.concatenate([spreader(lambda g: (g == 0) | (g == 2)), spreader(lambda g: g == 1)], axis=0)
    in_three = three_in(in_w)

    def place(k, j):
        i = j if k == 0 else 2 * OWN - 1 - j
        return i if i < count + REACH else None

    state = {"sums": [own[...], inner[...]]}

    def first_block(t):
        held = {}

        def begin():
            if last:
                state["sums"] = [state["sums"][0] + mine[t], state["sums"][1] + inner_terms[t].astype(F32)]
            if last or t == 0:
                state["base"], state["stream"] = block_zero(
                    state["sums"], place, HALO, count, weff, in_three, shift, patch, centre, spread, three
                )
            shown = temb[first_time + t : first_time + t + 1, :]
            held["normed"] = normalise(state["base"] + ones * shown, gain[0:1, :])
            held["stream"] = state["stream"] + shown
            if t == 0 and copies:
                copies[0].wait()
                copies[1].wait()

        def put(x):
            after = (held["stream"] + x).reshape(count, COLS, WIDTH)
            kept[t] = after[0 : OWN - HALO]
            for half in range(2):
                wide[2 * t + half][:, PAD : PAD + COLS, :] = after[:, :, half * LANES : (half + 1) * LANES]

        return [begin] + pointwise(lambda: held["normed"], 0, up_w, up_b, down_w, put)

    def taps_of(t):
        def source(i, half, dx):
            at = PAD - HALO + dx
            return wide[2 * t + half][i - HALO, at : at + COLS, :]

        def done(h, half, x):
            partial[2 * t + half, h] = x

        return depthwise(turn, taps, source, pairs_of(NEAR), lambda h, half: jnp.zeros((COLS, LANES), F32), done)

    interleave(first_block(0), [])
    for t in range(1, TIMES):
        interleave(first_block(t), taps_of(t - 1))
    interleave(taps_of(TIMES - 1), [])
    for copy in copies[2:]:
        copy.wait()


def edge_kernel(last, *refs):
    if last:
        flags, outer, own, outer_terms, mine, *refs = refs
    else:
        flags, outer, own, *refs = refs
    (clock, other_clock, partial, kept, temb, weff, by_row, up_w, down_w, in_w, taps, gain, up_b, out_t,
     first_out, second_out, shift, patch, centre, *wide) = refs
    conv_buf = wide[2 * TIMES :]
    turn, inside = flags[0], flags[1].astype(F32)
    first_time = 1 if last else 0
    count = len(EDGE)
    ones = []
    for r in EDGE:
        total = jnp.zeros((COLS, WIDTH), F32)
        for dy in range(TAPS):
            total = total + (by_row[dy] if r + dy - HALO >= 0 else by_row[dy] * inside)
        ones.append(total)
    ones = jnp.concatenate(ones, axis=0)
    shift[...] = jnp.zeros_like(shift)
    for ref in wide[: 2 * TIMES]:
        ref[...] = jnp.zeros_like(ref)
    spread = spreader(lambda g: g >= 0)
    three = jnp.concatenate([spreader(lambda g: (g == 0) | (g == 2)), spreader(lambda g: g == 1)], axis=0)
    in_three = three_in(in_w)
    out_hi, out_lo = split(jnp.concatenate([out_t[...]] * 8, axis=0))
    out_three = jnp.concatenate([out_hi, out_hi, out_lo], axis=-1)
    low, high = both_clocks(turn, clock, other_clock)
    sizes = [low[:, 2:3], low[:, 3:4], high[:, 2:3], high[:, 3:4]]
    group = lane_group((1, LANES))

    def place(k, j):
        if k == 0:
            return REACH - 1 - j if j < REACH else None
        return REACH + j if j < REACH else None

    state = {"sums": [outer[...], own[...]]}
    terms = [None] * TIMES

    def first_block(t):
        held = {}

        def begin():
            if last:
                state["sums"] = [state["sums"][0] + outer_terms[t].astype(F32), state["sums"][1] + mine[t]]
                if t == 0:
                    state["n0"] = state["sums"][1]
            if last or t == 0:
                state["base"], state["stream"] = block_zero(
                    state["sums"], place, -HALO, count, weff, in_three, shift, patch, centre, spread, three
                )
            shown = temb[first_time + t : first_time + t + 1, :]
            held["normed"] = normalise(state["base"] + ones * shown, gain[0:1, :])
            held["stream"] = state["stream"] + shown

        def put(x):
            after = (held["stream"] + x).reshape(count, COLS, WIDTH)
            for half in range(2):
                lanes = slice(half * LANES, (half + 1) * LANES)
                wide[2 * t + half][0:HALO, PAD : PAD + COLS, :] = after[0:HALO, :, lanes] * inside
                wide[2 * t + half][HALO:, PAD : PAD + COLS, :] = after[HALO:, :, lanes]

        return [begin] + pointwise(lambda: held["normed"], 0, up_w, up_b, down_w, put)

    def taps_of(t):
        def source(i, half, dx):
            at = PAD - HALO + dx
            return wide[2 * t + half][i + HALO, at : at + COLS, :]

        def done(h, half, x):
            conv_buf[t][h, :, half * LANES : (half + 1) * LANES] = x

        return depthwise(turn, taps, source, pairs_of(EDGE), lambda h, half: partial[2 * t + half, h], done)

    def second_block(t):
        held = {}
        touched = len(pairs_of(EDGE))

        def begin():
            conv = [conv_buf[t][...].reshape(touched * COLS, WIDTH)]
            rest = [partial[2 * t + half, touched:].reshape((OWN - touched) * COLS, LANES) for half in range(2)]
            conv.append(jnp.concatenate(rest, axis=-1))
            held["normed"] = normalise(jnp.concatenate(conv, axis=0), gain[1:2, :])

        def put(x):
            ends = [wide[2 * t + half][HALO:, PAD : PAD + COLS, :].reshape(HALO * COLS, LANES) for half in range(2)]
            stream = [jnp.concatenate(ends, axis=-1), kept[t].reshape((OWN - HALO) * COLS, WIDTH)]
            hi, lo = split(jnp.concatenate(stream, axis=0) + x)
            drift = dot_nt(jnp.concatenate([hi, lo, hi], axis=-1), out_three) * sizes[first_time + t]
            drift = drift.reshape(OWN, COLS, LANES)
            dense = drift[0]
            for j in range(1, OWN):
                dense = jnp.where(group == j, drift[j], dense)
            terms[t] = dense

        return [begin] + pointwise(lambda: held["normed"], 1, up_w, up_b, down_w, put)

    interleave(first_block(0), [])
    for t in range(1, TIMES):
        interleave(first_block(t), taps_of(t - 1))
    interleave(second_block(0), taps_of(TIMES - 1))
    for t in range(1, TIMES):
        interleave(second_block(t), [])
    if last:
        n0 = state["n0"]
        n1 = n0 + terms[0]
        n2 = n1 + terms[1]
        n3 = n2 + terms[2]
        turned = turn == 1
        for i, (early, late) in enumerate(((n0, n2), (n1, n3))):
            first_out[i] = jnp.where(turned, late, early)
            second_out[i] = jnp.where(turned, early, late)
    else:
        for t in range(TIMES):
            first_out[t] = terms[t]
            second_out[t] = terms[t].astype(BF16)


SMEM = pl.BlockSpec(memory_space=pltpu.SMEM)
VMEM = pl.BlockSpec(memory_space=pltpu.VMEM)
HBM = pl.BlockSpec(memory_space=pltpu.HBM)
SMALL = pltpu.CompilerParams(vmem_limit_bytes=4 * 2**20)
LARGE = pltpu.CompilerParams(vmem_limit_bytes=20 * 2**20)


def working(count):
    return [
        pltpu.VMEM((count + REACH, WIDE, LANES), F32),
        pltpu.VMEM((count + REACH, COLS, LANES), BF16),
        pltpu.VMEM((count, COLS, LANES), BF16),
    ] + [pltpu.VMEM((count, WIDE, LANES), F32)] * (2 * TIMES)


def near(last, up_w, down_w, *args):
    outs = [pltpu.VMEM((2 * TIMES, OWN, COLS, LANES), F32), pltpu.VMEM((TIMES, OWN - HALO, COLS, WIDTH), F32)]
    scratch = working(len(NEAR))
    if last:
        specs = [SMEM] + [VMEM] * (len(args) - 1)
    else:
        outs += [pltpu.VMEM((8, WIDTH), F32), pltpu.VMEM((TAPS * LANES, WIDTH), BF16), pltpu.VMEM((TAPS, COLS, WIDTH), F32)]
        outs += [pltpu.VMEM(up_w.shape, BF16), pltpu.VMEM(down_w.shape, BF16)]
        scratch += [pltpu.SemaphoreType.DMA((4,))]
        specs = [SMEM] + [VMEM] * 5 + [HBM] * 2 + [VMEM] * 4
    return pl.pallas_call(
        functools.partial(near_kernel, last),
        out_shape=outs,
        in_specs=specs,
        out_specs=[VMEM] * len(outs),
        scratch_shapes=scratch,
        compiler_params=LARGE,
    )(*args)


def edge(last, *args):
    if last:
        outs = [jax.ShapeDtypeStruct((2, COLS, LANES), F32)] * 2
    else:
        outs = [jax.ShapeDtypeStruct((TIMES, COLS, LANES), kind) for kind in (F32, BF16)]
    touched = len(pairs_of(EDGE))
    return pl.pallas_call(
        functools.partial(edge_kernel, last),
        out_shape=outs,
        in_specs=[SMEM] + [VMEM] * (len(args) - 1),
        out_specs=[VMEM, VMEM],
        scratch_shapes=working(len(EDGE)) + [pltpu.VMEM((touched, COLS, WIDTH), F32)] * TIMES,
        compiler_params=LARGE,
    )(*args)


def prepare(flags, times, sizes, turned_start):
    dense = jax.ShapeDtypeStruct((COLS, LANES), F32)
    return pl.pallas_call(
        prepare_kernel,
        out_shape=[dense, dense, jax.ShapeDtypeStruct((8, LANES), F32)],
        in_specs=[SMEM, SMEM, SMEM, VMEM],
        out_specs=[VMEM] * 3,
        compiler_params=SMALL,
    )(flags, times, sizes, turned_start)


def finish(flags, keep, got):
    return pl.pallas_call(
        finish_kernel,
        out_shape=jax.ShapeDtypeStruct((2, 2 * OWN, CHAN, COLS), F32),
        in_specs=[SMEM, VMEM, VMEM],
        out_specs=VMEM,
        compiler_params=SMALL,
    )(flags, keep, got)


def on_device(
    start_state, timesteps, step_sizes, in_weight, time_weight, conv_kernel, norm_gain, up_weight, up_bias, down_weight, out_weight,
):
    space = lax.axis_size("space")
    s, tm = lax.axis_index("space"), lax.axis_index("tm")
    beside = [(0, 1), (1, 0)]
    across = []
    for i in range(space - 1):
        across += [(2 * i + 1, 2 * i + 2), (2 * i + 2, 2 * i + 1)]

    def over_tm(x):
        return lax.ppermute(x, "tm", beside)

    def over_space(x):
        return lax.ppermute(x, ("space", "tm"), across)

    flags = jnp.stack([tm, jnp.where(tm == 0, s > 0, s < space - 1).astype(jnp.int32)]).astype(jnp.int32)
    own, inner, clock = prepare(flags, timesteps, step_sizes, start_state.transpose(0, 2, 1))
    outer = over_space(own)
    other_clock = over_tm(clock)
    taps = conv_kernel.transpose(1, 2, 0, 3)
    up_hbm, down_hbm = pinned(up_weight), pinned(down_weight)

    partial, kept, *made = near(
        False, up_weight, down_weight,
        flags, own, inner, clock, other_clock, time_weight, up_hbm, down_hbm, in_weight, taps, norm_gain, up_bias,
    )
    rest = (in_weight, taps, norm_gain, up_bias, out_weight.T)
    terms, sent = edge(False, flags, outer, own, clock, other_clock, partial, kept, *made, *rest)
    inner_terms, outer_terms = over_tm(sent), over_space(sent)
    partial, kept = near(True, up_weight, down_weight, flags, own, inner, terms, inner_terms, *made, *rest[:-1])
    keep, give = edge(True, flags, outer, own, outer_terms, terms, clock, other_clock, partial, kept, *made, *rest)
    return finish(flags, keep, over_tm(give)).transpose(0, 1, 3, 2)


def solution(mesh):
    both = P(("groups", "tm"))
    return jax.shard_map(
        on_device,
        mesh=mesh,
        in_specs=(P(("groups", "space"), None, None), both, both) + (P(),) * 8,
        out_specs=P("tm", ("groups", "space"), None, None),
        check_vma=False,
    )
```

time: 40.4 us -> 40.2 us (level)
  starting transfers between devices: 12 us -> 9.86 us
  local copies, waits for them, and re-layouts: 1.79 us -> 3.18 us
  Pallas kernels: 23.8 us -> 25.1 us
  other arithmetic: 1.26 us -> 0.07 us
  waiting for transfers between devices: 0.88 us -> 1.7 us
    ppermute x3, starting transfers between devices: 10.5 us -> 8.36 us  [over_tm(): return lax.ppermute(x, 'tm', beside)]
    unnamed x16 -> x18, local copies, waits for them, and re-layouts: 1.71 us -> 3.18 us
    pallas_call x3 -> x5, Pallas kernels: 22.4 us -> 23.7 us  [the longest x2 11.6 us: edge(): pl.pallas_call(functools.partial(edge_kernel, last), out_shape=outs, in_s...]
    ppermute x3, waiting for transfers between devices: 0.87 us -> 1.69 us  [over_tm(): return lax.ppermute(x, 'tm', beside)]
    convert_element_type x1 -> x0, other arithmetic: 0.71 us -> none  [on_device(): own_clock = jnp.concatenate([timesteps.astype(F32), step_sizes])]
  transfers between devices with their start and end apart: 5 -> 5, of which waited for: 1 -> 2; matrix products, arithmetic and copies ran while one was open for 2% -> 0% of each run, Pallas kernels for 1% -> 29%
where the time goes in v4:
time: 40.2 us; the launch traced here: 40 us
  Pallas kernels  25.1 us (62%)
  starting transfers between devices  9.86 us (25%)
  local copies, waits for them, and re-layouts  3.18 us (8%)
  waiting for transfers between devices  1.7 us (4%)
    pallas_call x2, Pallas kernels, edge(): pl.pallas_call(functools.partial(edge_kernel, last), out_shape=outs, in_s...  11.6 us
    pallas_call x2, Pallas kernels, near(): pl.pallas_call(functools.partial(near_kernel, last), out_shape=outs, in_s...  11.5 us
    ppermute x3, starting transfers between devices, over_tm(): return lax.ppermute(x, 'tm', beside)  8.36 us
    unnamed x18, local copies, waits for them, and re-layouts  3.18 us
    ppermute x3, waiting for transfers between devices, over_tm(): return lax.ppermute(x, 'tm', beside)  1.69 us
    ppermute x2, starting transfers between devices, over_space(): return lax.ppermute(x, ('space', 'tm'), across)  1.5 us
    pallas_call x1, Pallas kernels, finish(): pl.pallas_call(finish_kernel, out_shape=jax.ShapeDtypeStruct((2, 2 * OWN,...  1.38 us
  transfers between devices with their start and end apart: 5, of which 2 were waited for; matrix products, arithmetic and copies ran while one was open for 0% of the time, Pallas kernels for 29%

profile of v4, /device:TPU:0, one launch (start us, length us, event | category | flops | bytes accessed | tf_op | source)
XLA Modules:
  0.0 40.0 jit_solution(17173692866295115358)
XLA Ops:
  0.0 0.1 pad_add_fusion.flags.refs_0_
  0.1 0.9 %copy-done.3 = f32[16,32,16]{1,2,0:T(8,128)S(1)} copy-done((f32[16,32,16]{1,2,0:T(8,128)S(1)}, f32[16,32,16]{1,2,0:T(8,128)}, u32[]{:S(2)}) %copy-start.3) | copy-done | bytes 32792
  1.0 0.7 %copy-done.7 = s32[2]{0:T(128)S(1)} copy-done((s32[2]{0:T(128)S(1)}, s32[2]{0:T(128)}, u32[]{:S(2)}) %copy-start.7) | copy-done | bytes 32
  1.6 0.7 %copy-done.8 = f32[2]{0:T(128)S(1)} copy-done((f32[2]{0:T(128)S(1)}, f32[2]{0:T(128)}, u32[]{:S(2)}) %copy-start.8) | copy-done | bytes 32
  2.3 0.6 %shard_map.109 = (f32[32,128]{1,0:T(8,128)S(1)}, f32[32,128]{1,0:T(8,128)S(1)}, f32[8,128]{1,0:T(8,128)S(1)}) custom-call(s32[2]{0:T(128)S(1)} %pad_add_fusion.flags.refs_0_, s32[2]{0:T(128)S(1)} %copy-done.7, f32[2]{0:T(128)S(1)} %copy-done.8, f32[16,16,32]{2,1,0:T(8,128)S(1)} %bitcast.10), custom_call_target="tpu_custom_call" | custom-call | tf_op jit(solution)/shard_map/pallas_call | solution.py:460
  2.9 0.7 %collective-permute-start = (f32[32,128]{1,0:T(8,128)S(1)}, f32[32,128]{1,0:T(8,128)S(1)}, u32[]{:S(2)}, u32[]{:S(2)}) collective-permute-start(f32[32,128]{1,0:T(8,128)S(1)} %get-tuple-element.21.refs_1_.refs_2_), channel_id=1, source_target_pairs={{1,2},{2,1},{3,4},{4,3},{5,6},{6,5},{7,8},{8,7},{9,10},{10,9},{11,... | collective-permute-start | bytes 49160 | tf_op jit(solution)/shard_map/ppermute | solution.py:493
  3.6 0.0 copy-start.6
  3.6 4.4 %collective-permute-start.1 = (f32[8,128]{1,0:T(8,128)S(1)}, f32[8,128]{1,0:T(8,128)S(1)}, u32[]{:S(2)}, u32[]{:S(2)}) collective-permute-start(f32[8,128]{1,0:T(8,128)S(1)} %get-tuple-element.22.refs_3_.refs_5_), channel_id=1, source_target_pairs={{0,1},{1,0},{2,3},{3,2},{4,5},{5,4},{6,7},{7,6},{8,9},{9,8},{10,11... | collective-permute-start | bytes 12296 | tf_op jit(solution)/shard_map/ppermute | solution.py:490
  8.0 0.8 %collective-permute-done.1.refs_4_.refs_6_ = f32[8,128]{1,0:T(8,128)S(1)} collective-permute-done((f32[8,128]{1,0:T(8,128)S(1)}, f32[8,128]{1,0:T(8,128)S(1)}, u32[]{:S(2)}, u32[]{:S(2)}) %collective-permute-start.1) | collective-permute-done | bytes 4128 | tf_op jit(solution)/shard_map/ppermute | solution.py:490
  8.8 0.0 copy-done
  8.8 0.0 copy-start.1
  8.8 0.9 %copy-done.1 = f32[256,256]{1,0:T(8,128)S(1)} copy-done((f32[256,256]{1,0:T(8,128)S(1)}, f32[256,256]{1,0:T(8,128)}, u32[]{:S(2)}) %copy-start.1) | copy-done | bytes 262168
  9.8 5.6 %shard_map.110 = (f32[6,8,32,128]{3,2,1,0:T(8,128)S(1)}, f32[3,5,32,256]{3,2,1,0:T(8,128)S(1)}, f32[8,256]{1,0:T(8,128)S(1)}, bf16[896,256]{1,0:T(8,128)(2,1)S(1...) custom-call(s32[2]{0:T(128)S(1)} %pad_add_fusion.flags.refs_0_, ...), custom_call_target="tpu_custom_call" | custom-call | tf_op jit(solution)/shard_map/pallas_call | solution.py:432
  15.4 0.0 collective-permute-done.refs_1_
  15.4 5.7 %shard_map.111 = (f32[3,32,128]{2,1,0:T(8,128)S(1)}, bf16[3,32,128]{2,1,0:T(8,128)(2,1)S(1)}) custom-call(s32[2]{0:T(128)S(1)} %pad_add_fusion.flags.refs_0_, f32[32,128]{1,0:T(8,128)S(1)} %collective-permute-done.refs_1_, f32[32,128]{1,0:T(8,128)S(1)} %get-tuple-element.21.refs_1_.refs_2_, f32[8,128]{1,0:T(8,128)S(1)} %get-tuple-element.22.refs_3_.refs_5_, ...), custom_call_target="tpu_custom_call" | custom-call | tf_op jit(solution)/shard_map/pallas_call | solution.py:448
  21.1 0.7 %collective-permute-start.3 = (bf16[3,32,128]{2,1,0:T(8,128)(2,1)S(1)}, bf16[3,32,128]{2,1,0:T(8,128)(2,1)S(1)}, u32[]{:S(2)}, u32[]{:S(2)}) collective-permute-start(bf16[3,32,128]{2,1,0:T(8,128)(2,1)S(1)} %get-tuple-element.31), channel_id=1, source_target_pairs={{0,1},{1,0},{2,3},{3,2},{4,5},{5,4},{6,7},{7,6},{8,9},{9,8},{10,11... | collective-permute-start | bytes 73736 | tf_op jit(solution)/shard_map/ppermute | solution.py:490
  21.8 0.8 %collective-permute-start.2 = (bf16[3,32,128]{2,1,0:T(8,128)(2,1)S(1)}, bf16[3,32,128]{2,1,0:T(8,128)(2,1)S(1)}, u32[]{:S(2)}, u32[]{:S(2)}) collective-permute-start(bf16[3,32,128]{2,1,0:T(8,128)(2,1)S(1)} %get-tuple-element.31), channel_id=1, source_target_pairs={{1,2},{2,1},{3,4},{4,3},{5,6},{6,5},{7,8},{8,7},{9,10},{10,9},{11,... | collective-permute-start | bytes 73736 | tf_op jit(solution)/shard_map/ppermute | solution.py:493
  22.6 0.0 collective-permute-done.3.refs_4_
  22.6 5.9 %shard_map.112 = (f32[6,8,32,128]{3,2,1,0:T(8,128)S(1)}, f32[3,5,32,256]{3,2,1,0:T(8,128)S(1)}) custom-call(s32[2]{0:T(128)S(1)} %pad_add_fusion.flags.refs_0_, f32[32,128]{1,0:T(8,128)S(1)} %get-tuple-element.21.refs_1_.refs_2_, f32[32,128]{1,0:T(8,128)S(1)} %get-tuple-element.23.refs_2_, f32[3,32,128]{2,1,0:T(8,128)S(1)} %get-tuple-element.32.refs_3_.refs_4_, ...), custom_call_target="tpu_custom_call" | custom-call | tf_op jit(solution)/shard_map/pallas_call | solution.py:432
  28.5 0.0 collective-permute-done.2.refs_3_
  28.5 5.9 %shard_map.113 = (f32[2,32,128]{2,1,0:T(8,128)S(1)}, f32[2,32,128]{2,1,0:T(8,128)S(1)}) custom-call(s32[2]{0:T(128)S(1)} %pad_add_fusion.flags.refs_0_, f32[32,128]{1,0:T(8,128)S(1)} %collective-permute-done.refs_1_, f32[32,128]{1,0:T(8,128)S(1)} %get-tuple-element.21.refs_1_.refs_2_, bf16[3,32,128]{2,1,0:T(8,128)(2,1)S(1)} %collective-permute-done.2.refs_3_, ...), custom_call_target="tpu_custom_call" | custom-call | tf_op jit(solution)/shard_map/pallas_call | solution.py:448
  34.5 3.3 %collective-permute-start.4 = (f32[2,32,128]{2,1,0:T(8,128)S(1)}, f32[2,32,128]{2,1,0:T(8,128)S(1)}, u32[]{:S(2)}, u32[]{:S(2)}) collective-permute-start(f32[2,32,128]{2,1,0:T(8,128)S(1)} %get-tuple-element.36), channel_id=1, source_target_pairs={{0,1},{1,0},{2,3},{3,2},{4,5},{5,4},{6,7},{7,6},{8,9},{9,8},{10,11... | collective-permute-start | bytes 98312 | tf_op jit(solution)/shard_map/ppermute | solution.py:490
  37.8 0.9 %collective-permute-done.4.got = f32[2,32,128]{2,1,0:T(8,128)S(1)} collective-permute-done((f32[2,32,128]{2,1,0:T(8,128)S(1)}, f32[2,32,128]{2,1,0:T(8,128)S(1)}, u32[]{:S(2)}, u32[]{:S(2)}) %collective-permute-start.4) | collective-permute-done | bytes 32800 | tf_op jit(solution)/shard_map/ppermute | solution.py:490
  38.6 1.4 %shard_map.114 = f32[2,16,16,32]{3,2,1,0:T(8,128)} custom-call(s32[2]{0:T(128)S(1)} %pad_add_fusion.flags.refs_0_, f32[2,32,128]{2,1,0:T(8,128)S(1)} %get-tuple-element.35.keep, f32[2,32,128]{2,1,0:T(8,128)S(1)} %collective-permute-done.4.got), custom_call_target="tpu_custom_call" | custom-call | tf_op jit(solution)/shard_map/pallas_call | solution.py:470
  (11 shorter events, 0.0 us)
Async XLA Ops:
  0.0 8.8 %copy-start = (f32[2,7,7,256]{3,0,2,1:T(2,128)S(1)}, f32[2,7,7,256]{3,0,2,1:T(2,128)}, u32[]{:S(2)}) copy-start(f32[2,7,7,256]{3,0,2,1:T(2,128)} %param.16) | copy-start | bytes 301060
  0.1 0.9 %copy-start.3 = (f32[16,32,16]{1,2,0:T(8,128)S(1)}, f32[16,32,16]{1,2,0:T(8,128)}, u32[]{:S(2)}) copy-start(f32[16,32,16]{1,2,0:T(8,128)} %param.11) | copy-start | bytes 98308
  1.0 0.7 %copy-start.7 = (s32[2]{0:T(128)S(1)}, s32[2]{0:T(128)}, u32[]{:S(2)}) copy-start(s32[2]{0:T(128)} %times.1) | copy-start | bytes 28
  1.6 0.7 %copy-start.8 = (f32[2]{0:T(128)S(1)}, f32[2]{0:T(128)}, u32[]{:S(2)}) copy-start(f32[2]{0:T(128)} %sizes.1) | copy-start | bytes 28
  2.3 6.5 %copy-start.2 = (f32[16,256]{1,0:T(8,128)S(1)}, f32[16,256]{1,0:T(8,128)}, u32[]{:S(2)}) copy-start(f32[16,256]{1,0:T(8,128)} %refs_14_.3) | copy-start | bytes 49156
  2.3 6.5 %copy-start.4 = (f32[2,1024]{1,0:T(2,128)S(1)}, f32[2,1024]{1,0:T(2,128)}, u32[]{:S(2)}) copy-start(f32[2,1024]{1,0:T(2,128)} %refs_17_.1) | copy-start | bytes 24580
  2.9 12.5 %collective-permute-start = (f32[32,128]{1,0:T(8,128)S(1)}, f32[32,128]{1,0:T(8,128)S(1)}, u32[]{:S(2)}, u32[]{:S(2)}) collective-permute-start(f32[32,128]{1,0:T(8,128)S(1)} %get-tuple-element.21.refs_1_.refs_2_), channel_id=1, source_target_pairs={{1,2},{2,1},{3,4},{4,3},{5,6},{6,5},{7,8},{8,7},{9,10},{10,9},{11,... | collective-permute-start | bytes 49160 | tf_op jit(solution)/shard_map/ppermute | solution.py:493
  3.6 5.2 %copy-start.6 = (f32[2,256]{1,0:T(2,128)S(1)}, f32[2,256]{1,0:T(2,128)}, u32[]{:S(2)}) copy-start(f32[2,256]{1,0:T(2,128)} %refs_16_.1) | copy-start | bytes 6148
  3.6 5.2 %collective-permute-start.1 = (f32[8,128]{1,0:T(8,128)S(1)}, f32[8,128]{1,0:T(8,128)S(1)}, u32[]{:S(2)}, u32[]{:S(2)}) collective-permute-start(f32[8,128]{1,0:T(8,128)S(1)} %get-tuple-element.22.refs_3_.refs_5_), channel_id=1, source_target_pairs={{0,1},{1,0},{2,3},{3,2},{4,5},{5,4},{6,7},{7,6},{8,9},{9,8},{10,11... | collective-permute-start | bytes 12296 | tf_op jit(solution)/shard_map/ppermute | solution.py:490
  8.8 1.0 %copy-start.1 = (f32[256,256]{1,0:T(8,128)S(1)}, f32[256,256]{1,0:T(8,128)}, u32[]{:S(2)}) copy-start(f32[256,256]{1,0:T(8,128)} %refs_5_.1) | copy-start | bytes 786436
  9.8 5.6 %copy-start.5 = (f32[256,16]{0,1:T(8,128)S(1)}, f32[256,16]{0,1:T(8,128)}, u32[]{:S(2)}) copy-start(f32[256,16]{0,1:T(8,128)} %param.21) | copy-start | bytes 49156
  21.1 1.6 %collective-permute-start.3 = (bf16[3,32,128]{2,1,0:T(8,128)(2,1)S(1)}, bf16[3,32,128]{2,1,0:T(8,128)(2,1)S(1)}, u32[]{:S(2)}, u32[]{:S(2)}) collective-permute-start(bf16[3,32,128]{2,1,0:T(8,128)(2,1)S(1)} %get-tuple-element.31), channel_id=1, source_target_pairs={{0,1},{1,0},{2,3},{3,2},{4,5},{5,4},{6,7},{7,6},{8,9},{9,8},{10,11... | collective-permute-start | bytes 73736 | tf_op jit(solution)/shard_map/ppermute | solution.py:490
  21.8 6.7 %collective-permute-start.2 = (bf16[3,32,128]{2,1,0:T(8,128)(2,1)S(1)}, bf16[3,32,128]{2,1,0:T(8,128)(2,1)S(1)}, u32[]{:S(2)}, u32[]{:S(2)}) collective-permute-start(bf16[3,32,128]{2,1,0:T(8,128)(2,1)S(1)} %get-tuple-element.31), channel_id=1, source_target_pairs={{1,2},{2,1},{3,4},{4,3},{5,6},{6,5},{7,8},{8,7},{9,10},{10,9},{11,... | collective-permute-start | bytes 73736 | tf_op jit(solution)/shard_map/ppermute | solution.py:493
  34.5 4.2 %collective-permute-start.4 = (f32[2,32,128]{2,1,0:T(8,128)S(1)}, f32[2,32,128]{2,1,0:T(8,128)S(1)}, u32[]{:S(2)}, u32[]{:S(2)}) collective-permute-start(f32[2,32,128]{2,1,0:T(8,128)S(1)} %get-tuple-element.36), channel_id=1, source_target_pairs={{0,1},{1,0},{2,3},{3,2},{4,5},{5,4},{6,7},{7,6},{8,9},{9,8},{10,11... | collective-permute-start | bytes 98312 | tf_op jit(solution)/shard_map/ppermute | solution.py:490

commit v5 on v4

v5 whole, which is shorter than its diff:
```python
import functools
import math

import jax
import jax.numpy as jnp
from jax import lax
from jax.experimental import pallas as pl
from jax.experimental.pallas import tpu as pltpu
from jax.sharding import PartitionSpec as P

HIGH = lax.Precision.HIGHEST
F32, BF16 = jnp.float32, jnp.bfloat16
COLS, CHAN, WIDTH, HIDDEN, LANES = 32, 16, 256, 1024, 128
OWN, TAPS, HALO = 8, 7, 3
REACH = 2 * HALO
PAD = 8
WIDE = COLS + 2 * PAD
TIMES = 3
CHUNK = 256


def split(x):
    hi = x.astype(BF16)
    return hi, (x - hi.astype(F32)).astype(BF16)


def dot(a, b):
    return lax.dot_general(a, b, (((1,), (0,)), ((), ())), preferred_element_type=F32)


def dot_nt(a, b):
    return lax.dot_general(a, b, (((1,), (1,)), ((), ())), preferred_element_type=F32)


def lane_group(shape):
    return lax.broadcasted_iota(jnp.int32, shape, len(shape) - 1) // CHAN


def make_spread(spread, three):
    row = lax.broadcasted_iota(jnp.int32, (CHAN, LANES), 0)
    col = lax.broadcasted_iota(jnp.int32, (CHAN, LANES), 1)
    hit, group = row == col % CHAN, col // CHAN
    spread[...] = jnp.zeros_like(spread)
    three[...] = jnp.zeros_like(three)

    def cells(where):
        return jnp.where(where, 1.0, 0.0).astype(BF16)

    for j in range(OWN):
        rows, lanes = slice(j * CHAN, (j + 1) * CHAN), slice(j * LANES, (j + 1) * LANES)
        spread[rows, lanes] = cells(hit)
        three[rows, lanes] = cells(hit & ((group == 0) | (group == 2)))
        three[LANES + j * CHAN : LANES + (j + 1) * CHAN, lanes] = cells(hit & (group == 1))


def normalise(conv, gain):
    mean = jnp.mean(conv, axis=-1, keepdims=True)
    centered = conv - mean
    var = jnp.mean(centered * centered, axis=-1, keepdims=True)
    return (centered * lax.rsqrt(var + 1e-06) * gain).astype(BF16)


def gelu(x):
    x = x.astype(BF16)
    inner = x * (BF16(0.7978845608028654) + BF16(0.035677408136300125) * (x * x))
    half = BF16(0.5) * x
    return half + half * jnp.tanh(inner)


def prepare_kernel(flags, times, sizes, start, own, inner, clock):
    turned = flags[0] == 1
    top = to_dense([start[h] for h in range(OWN)])
    bottom = to_dense([start[2 * OWN - 1 - h] for h in range(OWN)])
    own[...] = jnp.where(turned, bottom, top)
    inner[...] = jnp.where(turned, top, bottom)
    lane = lax.broadcasted_iota(jnp.int32, (8, LANES), 1)
    values = (times[0].astype(F32), times[1].astype(F32), sizes[0], sizes[1])
    filled = jnp.zeros((8, LANES), F32)
    for i, value in enumerate(values):
        filled = jnp.where(lane == i, value, filled)
    clock[...] = filled


def finish_kernel(flags, keep, got, out):
    turned = flags[0] == 1
    for t in range(2):
        top = jnp.where(turned, got[t], keep[t])
        bottom = jnp.where(turned, keep[t], got[t])
        out[t, 0:OWN] = top.T.reshape(OWN, CHAN, COLS)
        flipped = bottom.T.reshape(OWN, CHAN, COLS)
        for h in range(OWN):
            out[t, 2 * OWN - 1 - h] = flipped[h]


def pinned(x):
    return pltpu.with_memory_space_constraint(x, pltpu.HBM)


def to_dense(rows):
    return jnp.concatenate(rows, axis=0).T


def row_of(turn, dy):
    return dy + turn * (TAPS - 1 - 2 * dy)


def both_clocks(turn, mine, other):
    first = turn == 0
    return jnp.where(first, mine[0:1, :], other[0:1, :]), jnp.where(first, other[0:1, :], mine[0:1, :])


def embed(turn, mine, other, time_w):
    low, high = both_clocks(turn, mine, other)
    steps = jnp.concatenate([low[:, 0:1], low[:, 1:2], high[:, 0:1], high[:, 1:2]] * 2, axis=0)
    lane = lax.broadcasted_iota(jnp.int32, (1, LANES), 1).astype(F32)
    angle = steps * jnp.exp(lane * (-math.log(10000.0) / LANES))
    feats = jnp.concatenate([jnp.sin(angle), jnp.cos(angle)], axis=1)
    return lax.dot_general(feats, time_w[...], (((1,), (0,)), ((), ())), precision=HIGH, preferred_element_type=F32)


def make_weff(turn, in_w, taps, weff):
    weff[...] = jnp.zeros_like(weff)
    for dy in range(TAPS):
        for dx in range(TAPS):
            low = dy * LANES + dx * CHAN
            weff[low : low + CHAN, :] = (in_w[...] * taps[row_of(turn, dy), dx, 0:1, :]).astype(BF16)


def make_by_row(turn, taps, by_row):
    column = lax.broadcasted_iota(jnp.int32, (COLS, WIDTH), 0)
    for dy in range(TAPS):
        total = jnp.zeros((COLS, WIDTH), F32)
        for dx in range(TAPS):
            ok = (column + (dx - HALO) >= 0) & (column + (dx - HALO) < COLS)
            total = total + jnp.where(ok, taps[row_of(turn, dy), dx, 0:1, :], 0.0)
        by_row[dy] = total


def make_in_three(in_w, in_three):
    hi, lo = split(in_w[...])
    in_three[...] = jnp.concatenate([hi, hi, lo, jnp.zeros((LANES - 3 * CHAN, WIDTH), BF16)], axis=0)


def make_tap_rows(turn, taps, tap_rows):
    for dy in range(TAPS):
        for dx in range(TAPS):
            for half in range(2):
                lanes = slice(half * LANES, (half + 1) * LANES)
                tap_rows[half, dy * TAPS + dx : dy * TAPS + dx + 1, :] = taps[row_of(turn, dy), dx, 1:2, lanes]


def clear_sides(ref):
    side = jnp.zeros(ref.shape[:-2] + (PAD, LANES), F32)
    ref[..., 0:PAD, :] = side
    ref[..., PAD + COLS :, :] = side


def block_zero(states, place, count, weff, in_three, shift, patch, centre, spread, three):
    rows, many, blocks = count + REACH, len(states), len(states[0])
    hi, lo = split(jnp.concatenate([block for state in states for block in state], axis=0))

    def spots(flat):
        for n in range(many):
            for k in range(blocks):
                low = (n * blocks + k) * COLS
                for j in range(OWN):
                    i = place(k, j)
                    if i is not None:
                        yield n, i, flat[low : low + COLS, j * LANES : (j + 1) * LANES]

    clear_sides(shift)
    for n, i, x in spots(dot(hi, spread[...])):
        shift[n, i, PAD : PAD + COLS, :] = x
    for n, i, x in spots(dot(jnp.concatenate([hi, lo], axis=-1), three[...])):
        if HALO <= i < HALO + count:
            centre[n, i - HALO] = x.astype(BF16)
    group = lane_group((1, 1, 1, LANES))
    at = PAD - HALO
    picked = shift[0:many, :, at : at + COLS, :]
    for dx in range(1, TAPS):
        picked = jnp.where(group == dx, shift[0:many, :, at + dx : at + dx + COLS, :], picked)
    patch[0:many] = picked.astype(BF16)
    cells = many * count * COLS
    wide = [patch[0:many, dy : dy + count].reshape(cells, LANES) for dy in range(TAPS)]
    base = dot(jnp.concatenate(wide, axis=-1), weff[...])
    stream = dot(centre[0:many].reshape(cells, LANES), in_three[...])
    shape = (many, count, COLS, WIDTH)
    return base.reshape(shape), stream.reshape(shape)


def first_block(states, place, count, ones, first_time, temb, gain, up_w, up_b, down_w, weff, in_three, *scratch):
    base, stream = block_zero(states, place, count, weff, in_three, *scratch)
    normed, residual = [], []
    for t in range(TIMES):
        n = min(t, len(states) - 1)
        shown = temb[first_time + t : first_time + t + 1, :]
        conv = base[n] + ones * shown
        normed.append(normalise(conv.reshape(count * COLS, WIDTH), gain[0:1, :]))
        residual.append(stream[n] + shown)
    out = pointwise(jnp.concatenate(normed, axis=0), 0, up_w, up_b, down_w).reshape(TIMES, count, COLS, WIDTH)
    return [residual[t] + out[t] for t in range(TIMES)]


def pointwise(normed, block, up_w, up_b, down_w):
    hidden = []
    for low in range(0, HIDDEN, CHUNK):
        hidden.append(gelu(dot(normed, up_w[block, :, low : low + CHUNK]) + up_b[block : block + 1, low : low + CHUNK]))
    return dot(jnp.concatenate(hidden, axis=-1), down_w[block])


def depthwise(tap_rows, source, pairs, begin, done):
    heights = sorted(pairs)
    groups = [heights[i : i + 4] for i in range(0, len(heights), 4)]
    for half in range(2):
        for group in groups:
            acc = {h: begin(h, half) for h in group}
            needed = sorted({i for h in group for i in pairs[h]})
            for dx in range(TAPS):
                for i in needed:
                    x = source(i, half, dx)
                    for h in group:
                        if i in pairs[h]:
                            at = (i - h + HALO) * TAPS + dx
                            acc[h] = acc[h] + x * tap_rows[half, at : at + 1, :]
            for h in group:
                done(h, half, acc[h])


NEAR = range(HALO, OWN + HALO)
EDGE = range(-HALO, HALO)


def pairs_of(rows):
    found = {h: [i for i in rows if abs(i - h) <= HALO] for h in range(OWN)}
    return {h: listed for h, listed in found.items() if listed}


def near_kernel(last, *refs):
    first_time = 1 if last else 0
    count = len(NEAR)
    if last:
        (flags, own, inner, mine, inner_terms, temb, weff, by_row, tap_rows, spread, three, in_three, up_w, down_w, gain, up_b,
         partial, kept, shift, patch, centre, *wide) = refs
        turn = flags[0]
        states, state = [], [own[...], inner[...]]
        for t in range(TIMES):
            state = [state[0] + mine[t], state[1] + inner_terms[t].astype(F32)]
            states.append(state)
    else:
        (flags, own, inner, clock, other_clock, time_hbm, up_hbm, down_hbm, in_w, taps, gain, up_b,
         partial, kept, temb, weff, by_row, tap_rows, spread, three, in_three, up_w, down_w,
         shift, patch, centre, *wide, time_w, sems) = refs
        turn = flags[0]
        copies = [pltpu.make_async_copy(time_hbm, time_w, sems.at[4])]
        for block in range(2):
            copies.append(pltpu.make_async_copy(up_hbm.at[block], up_w.at[block], sems.at[2 * block]))
            copies.append(pltpu.make_async_copy(down_hbm.at[block], down_w.at[block], sems.at[2 * block + 1]))
        for copy in copies:
            copy.start()
        make_weff(turn, in_w, taps, weff)
        make_by_row(turn, taps, by_row)
        make_tap_rows(turn, taps, tap_rows)
        make_spread(spread, three)
        make_in_three(in_w, in_three)
        copies[0].wait()
        temb[...] = embed(turn, clock, other_clock, time_w)
        states = [[own[...], inner[...]]]
        copies[1].wait()
        copies[2].wait()
    ones = by_row[0]
    for dy in range(1, TAPS):
        ones = ones + by_row[dy]
    for ref in wide:
        clear_sides(ref)

    def place(k, j):
        i = j if k == 0 else 2 * OWN - 1 - j
        return i if i < count + REACH else None

    after = first_block(
        states, place, count, ones[None], first_time, temb, gain, up_w, up_b, down_w, weff, in_three,
        shift, patch, centre, spread, three,
    )
    for t in range(TIMES):
        kept[t] = after[t][0 : OWN - HALO]
        for half in range(2):
            wide[2 * t + half][:, PAD : PAD + COLS, :] = after[t][:, :, half * LANES : (half + 1) * LANES]
    for t in range(TIMES):

        def source(i, half, dx):
            at = PAD - HALO + dx
            return wide[2 * t + half][i - HALO, at : at + COLS, :]

        def done(h, half, x):
            partial[2 * t + half, h] = x

        depthwise(tap_rows, source, pairs_of(NEAR), lambda h, half: jnp.zeros((COLS, LANES), F32), done)
    if not last:
        copies[3].wait()
        copies[4].wait()


def edge_kernel(last, *refs):
    if last:
        flags, outer, own, outer_terms, mine, *refs = refs
    else:
        flags, outer, own, *refs = refs
    (clock, other_clock, partial, kept, temb, weff, by_row, tap_rows, spread, three, in_three, up_w, down_w, gain, up_b, out_t,
     first_out, second_out, shift, patch, centre, *wide) = refs
    conv_buf = wide[2 * TIMES :]
    turn, inside = flags[0], flags[1].astype(F32)
    first_time = 1 if last else 0
    count = len(EDGE)
    ones = []
    for r in EDGE:
        seen = jnp.zeros((COLS, WIDTH), F32)
        hidden = jnp.zeros((COLS, WIDTH), F32)
        for dy in range(TAPS):
            if r + dy - HALO >= 0:
                seen = seen + by_row[dy]
            else:
                hidden = hidden + by_row[dy]
        ones.append(seen + hidden * inside)
    ones = jnp.concatenate(ones, axis=0).reshape(count, COLS, WIDTH)
    for ref in wide[: 2 * TIMES]:
        clear_sides(ref)
    out_hi, out_lo = split(jnp.concatenate([out_t[...]] * 8, axis=0))
    out_three = jnp.concatenate([out_hi, out_hi, out_lo], axis=-1)
    low, high = both_clocks(turn, clock, other_clock)
    sizes = [low[:, 2:3], low[:, 3:4], high[:, 2:3], high[:, 3:4]]
    group = lane_group((1, LANES))

    def place(k, j):
        if j >= REACH:
            return None
        return REACH - 1 - j if k == 0 else REACH + j

    states, state = [], [outer[...], own[...]]
    for t in range(TIMES if last else 0):
        state = [state[0] + outer_terms[t].astype(F32), state[1] + mine[t]]
        states.append(state)
    after = first_block(
        states if last else [state], place, count, ones, first_time, temb, gain, up_w, up_b, down_w, weff, in_three,
        shift, patch, centre, spread, three,
    )
    for t in range(TIMES):
        for half in range(2):
            lanes = slice(half * LANES, (half + 1) * LANES)
            wide[2 * t + half][0:HALO, PAD : PAD + COLS, :] = after[t][0:HALO, :, lanes] * inside
            wide[2 * t + half][HALO:, PAD : PAD + COLS, :] = after[t][HALO:, :, lanes]
    touched = len(pairs_of(EDGE))
    normed, stream = [], []
    for t in range(TIMES):

        def source(i, half, dx):
            at = PAD - HALO + dx
            return wide[2 * t + half][i + HALO, at : at + COLS, :]

        def done(h, half, x):
            conv_buf[t][h, :, half * LANES : (half + 1) * LANES] = x

        depthwise(tap_rows, source, pairs_of(EDGE), lambda h, half: partial[2 * t + half, h], done)
        rest = [partial[2 * t + half, touched:].reshape((OWN - touched) * COLS, LANES) for half in range(2)]
        conv = [conv_buf[t][...].reshape(touched * COLS, WIDTH), jnp.concatenate(rest, axis=-1)]
        normed.append(normalise(jnp.concatenate(conv, axis=0), gain[1:2, :]))
        stream += [after[t][HALO:].reshape(HALO * COLS, WIDTH), kept[t].reshape((OWN - HALO) * COLS, WIDTH)]
    out = pointwise(jnp.concatenate(normed, axis=0), 1, up_w, up_b, down_w)
    hi, lo = split(jnp.concatenate(stream, axis=0) + out)
    drifts = dot_nt(jnp.concatenate([hi, lo, hi], axis=-1), out_three).reshape(TIMES, OWN, COLS, LANES)
    terms = []
    for t in range(TIMES):
        dense = drifts[t, 0]
        for j in range(1, OWN):
            dense = jnp.where(group == j, drifts[t, j], dense)
        terms.append(dense * sizes[first_time + t])
    if last:
        n0 = states[0][1]
        n1 = n0 + terms[0]
        n2 = n1 + terms[1]
        n3 = n2 + terms[2]
        turned = turn == 1
        for i, (early, late) in enumerate(((n0, n2), (n1, n3))):
            first_out[i] = jnp.where(turned, late, early)
            second_out[i] = jnp.where(turned, early, late)
    else:
        for t in range(TIMES):
            first_out[t] = terms[t]
            second_out[t] = terms[t].astype(BF16)


SMEM = pl.BlockSpec(memory_space=pltpu.SMEM)
VMEM = pl.BlockSpec(memory_space=pltpu.VMEM)
HBM = pl.BlockSpec(memory_space=pltpu.HBM)
SMALL = pltpu.CompilerParams(vmem_limit_bytes=4 * 2**20)
LARGE = pltpu.CompilerParams(vmem_limit_bytes=20 * 2**20)


def working(count, many):
    return [
        pltpu.VMEM((many, count + REACH, WIDE, LANES), F32),
        pltpu.VMEM((many, count + REACH, COLS, LANES), BF16),
        pltpu.VMEM((many, count, COLS, LANES), BF16),
    ] + [pltpu.VMEM((count, WIDE, LANES), F32)] * (2 * TIMES)


def near(last, up_w, down_w, *args):
    outs = [pltpu.VMEM((2 * TIMES, OWN, COLS, LANES), F32), pltpu.VMEM((TIMES, OWN - HALO, COLS, WIDTH), F32)]
    scratch = working(len(NEAR), TIMES if last else 1)
    if last:
        specs = [SMEM] + [VMEM] * (len(args) - 1)
    else:
        outs += [pltpu.VMEM((8, WIDTH), F32), pltpu.VMEM((TAPS * LANES, WIDTH), BF16), pltpu.VMEM((TAPS, COLS, WIDTH), F32)]
        outs += [pltpu.VMEM((2, 56, LANES), F32), pltpu.VMEM((LANES, OWN * LANES), BF16)]
        outs += [pltpu.VMEM((2 * LANES, OWN * LANES), BF16), pltpu.VMEM((LANES, WIDTH), BF16)]
        outs += [pltpu.VMEM(up_w.shape, BF16), pltpu.VMEM(down_w.shape, BF16)]
        scratch += [pltpu.VMEM((WIDTH, WIDTH), F32), pltpu.SemaphoreType.DMA((5,))]
        specs = [SMEM] + [VMEM] * 4 + [HBM] * 3 + [VMEM] * 4
    return pl.pallas_call(
        functools.partial(near_kernel, last),
        out_shape=outs,
        in_specs=specs,
        out_specs=[VMEM] * len(outs),
        scratch_shapes=scratch,
        compiler_params=LARGE,
    )(*args)


def edge(last, *args):
    if last:
        outs = [jax.ShapeDtypeStruct((2, COLS, LANES), F32)] * 2
    else:
        outs = [jax.ShapeDtypeStruct((TIMES, COLS, LANES), kind) for kind in (F32, BF16)]
    touched = len(pairs_of(EDGE))
    return pl.pallas_call(
        functools.partial(edge_kernel, last),
        out_shape=outs,
        in_specs=[SMEM] + [VMEM] * (len(args) - 1),
        out_specs=[VMEM, VMEM],
        scratch_shapes=working(len(EDGE), TIMES if last else 1) + [pltpu.VMEM((touched, COLS, WIDTH), F32)] * TIMES,
        compiler_params=LARGE,
    )(*args)


def prepare(flags, times, sizes, turned_start):
    dense = jax.ShapeDtypeStruct((COLS, LANES), F32)
    return pl.pallas_call(
        prepare_kernel,
        out_shape=[dense, dense, jax.ShapeDtypeStruct((8, LANES), F32)],
        in_specs=[SMEM, SMEM, SMEM, VMEM],
        out_specs=[VMEM] * 3,
        compiler_params=SMALL,
    )(flags, times, sizes, turned_start)


def finish(flags, keep, got):
    return pl.pallas_call(
        finish_kernel,
        out_shape=jax.ShapeDtypeStruct((2, 2 * OWN, CHAN, COLS), F32),
        in_specs=[SMEM, VMEM, VMEM],
        out_specs=VMEM,
        compiler_params=SMALL,
    )(flags, keep, got)


def on_device(
    start_state, timesteps, step_sizes, in_weight, time_weight, conv_kernel, norm_gain, up_weight, up_bias, down_weight, out_weight,
):
    space = lax.axis_size("space")
    s, tm = lax.axis_index("space"), lax.axis_index("tm")
    beside = [(0, 1), (1, 0)]
    across = []
    for i in range(space - 1):
        across += [(2 * i + 1, 2 * i + 2), (2 * i + 2, 2 * i + 1)]

    def over_tm(x):
        return lax.ppermute(x, "tm", beside)

    def over_space(x):
        return lax.ppermute(x, ("space", "tm"), across)

    flags = jnp.stack([tm, jnp.where(tm == 0, s > 0, s < space - 1).astype(jnp.int32)]).astype(jnp.int32)
    own, inner, clock = prepare(flags, pinned(timesteps), pinned(step_sizes), pinned(start_state.transpose(0, 2, 1)))
    other_clock = over_tm(clock)
    outer = over_space(own)
    taps = conv_kernel.transpose(1, 2, 0, 3)

    partial, kept, *made = near(
        False, up_weight, down_weight, flags, own, inner, clock, other_clock,
        pinned(time_weight), pinned(up_weight), pinned(down_weight), in_weight, taps, norm_gain, up_bias,
    )
    rest = (norm_gain, up_bias, out_weight.T)
    terms, sent = edge(False, flags, outer, own, clock, other_clock, partial, kept, *made, *rest)
    inner_terms, outer_terms = over_tm(sent), over_space(sent)
    partial, kept = near(True, up_weight, down_weight, flags, own, inner, terms, inner_terms, *made, *rest[:-1])
    keep, give = edge(True, flags, outer, own, outer_terms, terms, clock, other_clock, partial, kept, *made, *rest)
    return finish(flags, keep, over_tm(give)).transpose(0, 1, 3, 2)


def solution(mesh):
    both = P(("groups", "tm"))
    return jax.shard_map(
        on_device,
        mesh=mesh,
        in_specs=(P(("groups", "space"), None, None), both, both) + (P(),) * 8,
        out_specs=P("tm", ("groups", "space"), None, None),
        check_vma=False,
    )
```

time: 40.2 us -> 39.1 us (0.973)
  local copies, waits for them, and re-layouts: 3.18 us -> 0.72 us
  Pallas kernels: 25.1 us -> 27 us
  starting transfers between devices: 9.86 us -> 9.25 us
    unnamed x18 -> x10, local copies, waits for them, and re-layouts: 3.18 us -> 0.72 us
    pallas_call x2, Pallas kernels: 11.6 us -> 12.4 us  [edge(): pl.pallas_call(functools.partial(edge_kernel, last), out_shape=outs, in_s...]
    pallas_call x2, Pallas kernels: 11.5 us -> 12.2 us  [near(): pl.pallas_call(functools.partial(near_kernel, last), out_shape=outs, in_s...]
    ppermute x3, starting transfers between devices: 8.36 us -> 7.76 us  [over_tm(): return lax.ppermute(x, 'tm', beside)]
  transfers between devices with their start and end apart: 5 -> 5, of which waited for: 2 -> 2; matrix products, arithmetic and copies ran while one was open for 0% -> 0% of each run, Pallas kernels for 29% -> 31%
where the time goes in v5:
time: 39.1 us; the launch traced here: 38.8 us
  Pallas kernels  27 us (69%)
  starting transfers between devices  9.25 us (24%)
  waiting for transfers between devices  1.7 us (4%)
  local copies, waits for them, and re-layouts  0.72 us (2%)
    pallas_call x2, Pallas kernels, edge(): pl.pallas_call(functools.partial(edge_kernel, last), out_shape=outs, in_s...  12.4 us
    pallas_call x2, Pallas kernels, near(): pl.pallas_call(functools.partial(near_kernel, last), out_shape=outs, in_s...  12.2 us
    ppermute x3, starting transfers between devices, over_tm(): return lax.ppermute(x, 'tm', beside)  7.76 us
    ppermute x3, waiting for transfers between devices, over_tm(): return lax.ppermute(x, 'tm', beside)  1.69 us
    ppermute x2, starting transfers between devices, over_space(): return lax.ppermute(x, ('space', 'tm'), across)  1.5 us
    pallas_call x1, Pallas kernels, finish(): pl.pallas_call(finish_kernel, out_shape=jax.ShapeDtypeStruct((2, 2 * OWN,...  1.38 us
    pallas_call x1, Pallas kernels, prepare(): pl.pallas_call(prepare_kernel, out_shape=[dense, dense, jax.ShapeDtypeStr...  1 us
  transfers between devices with their start and end apart: 5, of which 2 were waited for; matrix products, arithmetic and copies ran while one was open for 0% of the time, Pallas kernels for 31%

profile of v5, /device:TPU:0, one launch (start us, length us, event | category | flops | bytes accessed | tf_op | source)
XLA Modules:
  0.0 38.8 jit_solution(16622995231384173736)
XLA Ops:
  0.0 0.1 pad_add_fusion.flags.refs_0_
  0.1 1.0 %shard_map.109 = (f32[32,128]{1,0:T(8,128)S(1)}, f32[32,128]{1,0:T(8,128)S(1)}, f32[8,128]{1,0:T(8,128)S(1)}) custom-call(s32[2]{0:T(128)S(1)} %pad_add_fusion.flags.refs_0_, s32[2]{0:T(128)} %times.1, f32[2]{0:T(128)} %sizes.1, f32[16,16,32]{2,1,0:T(8,128)} %bitcast.9), custom_call_target="tpu_custom_call" | custom-call | tf_op jit(solution)/shard_map/pallas_call | solution.py:446
  1.1 0.7 %collective-permute-start = (f32[32,128]{1,0:T(8,128)S(1)}, f32[32,128]{1,0:T(8,128)S(1)}, u32[]{:S(2)}, u32[]{:S(2)}) collective-permute-start(f32[32,128]{1,0:T(8,128)S(1)} %get-tuple-element.25.refs_1_.refs_2_), channel_id=1, source_target_pairs={{1,2},{2,1},{3,4},{4,3},{5,6},{6,5},{7,8},{8,7},{9,10},{10,9},{11,... | collective-permute-start | bytes 49160 | tf_op jit(solution)/shard_map/ppermute | solution.py:479
  1.8 0.0 copy-start.3
  1.8 4.4 %collective-permute-start.1 = (f32[8,128]{1,0:T(8,128)S(1)}, f32[8,128]{1,0:T(8,128)S(1)}, u32[]{:S(2)}, u32[]{:S(2)}) collective-permute-start(f32[8,128]{1,0:T(8,128)S(1)} %get-tuple-element.26.refs_3_.refs_5_), channel_id=1, source_target_pairs={{0,1},{1,0},{2,3},{3,2},{4,5},{5,4},{6,7},{7,6},{8,9},{9,8},{10,11... | collective-permute-start | bytes 12296 | tf_op jit(solution)/shard_map/ppermute | solution.py:476
  6.1 0.8 %collective-permute-done.1.refs_4_.refs_6_ = f32[8,128]{1,0:T(8,128)S(1)} collective-permute-done((f32[8,128]{1,0:T(8,128)S(1)}, f32[8,128]{1,0:T(8,128)S(1)}, u32[]{:S(2)}, u32[]{:S(2)}) %collective-permute-start.1) | collective-permute-done | bytes 4128 | tf_op jit(solution)/shard_map/ppermute | solution.py:476
  7.0 0.0 copy-done.1
  7.0 0.0 copy-done
  7.0 0.0 copy-done.4
  7.0 0.0 copy-done.3
  7.0 6.4 %shard_map.110 = (f32[6,8,32,128]{3,2,1,0:T(8,128)S(1)}, f32[3,5,32,256]{3,2,1,0:T(8,128)S(1)}, f32[8,256]{1,0:T(8,128)S(1)}, bf16[896,256]{1,0:T(8,128)(2,1)S(1...) custom-call(s32[2]{0:T(128)S(1)} %pad_add_fusion.flags.refs_0_, ...), custom_call_target="tpu_custom_call" | custom-call | tf_op jit(solution)/shard_map/pallas_call | solution.py:418
  13.4 0.0 copy-start.2
  13.4 0.0 collective-permute-done.refs_1_
  13.4 0.7 %copy-done.2 = f32[256,16]{0,1:T(8,128)S(1)} copy-done((f32[256,16]{0,1:T(8,128)S(1)}, f32[256,16]{0,1:T(8,128)}, u32[]{:S(2)}) %copy-start.2) | copy-done | bytes 16408
  14.1 5.9 %shard_map.111 = (f32[3,32,128]{2,1,0:T(8,128)S(1)}, bf16[3,32,128]{2,1,0:T(8,128)(2,1)S(1)}) custom-call(s32[2]{0:T(128)S(1)} %pad_add_fusion.flags.refs_0_, f32[32,128]{1,0:T(8,128)S(1)} %collective-permute-done.refs_1_, f32[32,128]{1,0:T(8,128)S(1)} %get-tuple-element.25.refs_1_.refs_2_, f32[8,128]{1,0:T(8,128)S(1)} %get-tuple-element.26.refs_3_.refs_5_, ...), custom_call_target="tpu_custom_call" | custom-call | tf_op jit(solution)/shard_map/pallas_call | solution.py:434
  20.1 0.4 %collective-permute-start.3 = (bf16[3,32,128]{2,1,0:T(8,128)(2,1)S(1)}, bf16[3,32,128]{2,1,0:T(8,128)(2,1)S(1)}, u32[]{:S(2)}, u32[]{:S(2)}) collective-permute-start(bf16[3,32,128]{2,1,0:T(8,128)(2,1)S(1)} %get-tuple-element.39), channel_id=1, source_target_pairs={{0,1},{1,0},{2,3},{3,2},{4,5},{5,4},{6,7},{7,6},{8,9},{9,8},{10,11... | collective-permute-start | bytes 73736 | tf_op jit(solution)/shard_map/ppermute | solution.py:476
  20.5 0.8 %collective-permute-start.2 = (bf16[3,32,128]{2,1,0:T(8,128)(2,1)S(1)}, bf16[3,32,128]{2,1,0:T(8,128)(2,1)S(1)}, u32[]{:S(2)}, u32[]{:S(2)}) collective-permute-start(bf16[3,32,128]{2,1,0:T(8,128)(2,1)S(1)} %get-tuple-element.39), channel_id=1, source_target_pairs={{1,2},{2,1},{3,4},{4,3},{5,6},{6,5},{7,8},{8,7},{9,10},{10,9},{11,... | collective-permute-start | bytes 73736 | tf_op jit(solution)/shard_map/ppermute | solution.py:479
  21.3 0.0 collective-permute-done.3.refs_4_
  21.3 5.7 %shard_map.112 = (f32[6,8,32,128]{3,2,1,0:T(8,128)S(1)}, f32[3,5,32,256]{3,2,1,0:T(8,128)S(1)}) custom-call(s32[2]{0:T(128)S(1)} %pad_add_fusion.flags.refs_0_, f32[32,128]{1,0:T(8,128)S(1)} %get-tuple-element.25.refs_1_.refs_2_, f32[32,128]{1,0:T(8,128)S(1)} %get-tuple-element.27.refs_2_, f32[3,32,128]{2,1,0:T(8,128)S(1)} %get-tuple-element.40.refs_3_.refs_4_, ...), custom_call_target="tpu_custom_call" | custom-call | tf_op jit(solution)/shard_map/pallas_call | solution.py:418
  27.1 0.0 collective-permute-done.2.refs_3_
  27.1 6.5 %shard_map.113 = (f32[2,32,128]{2,1,0:T(8,128)S(1)}, f32[2,32,128]{2,1,0:T(8,128)S(1)}) custom-call(s32[2]{0:T(128)S(1)} %pad_add_fusion.flags.refs_0_, f32[32,128]{1,0:T(8,128)S(1)} %collective-permute-done.refs_1_, f32[32,128]{1,0:T(8,128)S(1)} %get-tuple-element.25.refs_1_.refs_2_, bf16[3,32,128]{2,1,0:T(8,128)(2,1)S(1)} %collective-permute-done.2.refs_3_, ...), custom_call_target="tpu_custom_call" | custom-call | tf_op jit(solution)/shard_map/pallas_call | solution.py:434
  33.6 3.0 %collective-permute-start.4 = (f32[2,32,128]{2,1,0:T(8,128)S(1)}, f32[2,32,128]{2,1,0:T(8,128)S(1)}, u32[]{:S(2)}, u32[]{:S(2)}) collective-permute-start(f32[2,32,128]{2,1,0:T(8,128)S(1)} %get-tuple-element.44), channel_id=1, source_target_pairs={{0,1},{1,0},{2,3},{3,2},{4,5},{5,4},{6,7},{7,6},{8,9},{9,8},{10,11... | collective-permute-start | bytes 98312 | tf_op jit(solution)/shard_map/ppermute | solution.py:476
  36.6 0.9 %collective-permute-done.4.got = f32[2,32,128]{2,1,0:T(8,128)S(1)} collective-permute-done((f32[2,32,128]{2,1,0:T(8,128)S(1)}, f32[2,32,128]{2,1,0:T(8,128)S(1)}, u32[]{:S(2)}, u32[]{:S(2)}) %collective-permute-start.4) | collective-permute-done | bytes 32800 | tf_op jit(solution)/shard_map/ppermute | solution.py:476
  37.4 1.4 %shard_map.114 = f32[2,16,16,32]{3,2,1,0:T(8,128)} custom-call(s32[2]{0:T(128)S(1)} %pad_add_fusion.flags.refs_0_, f32[2,32,128]{2,1,0:T(8,128)S(1)} %get-tuple-element.43.keep, f32[2,32,128]{2,1,0:T(8,128)S(1)} %collective-permute-done.4.got), custom_call_target="tpu_custom_call" | custom-call | tf_op jit(solution)/shard_map/pallas_call | solution.py:456
  (3 shorter events, 0.0 us)
Async XLA Ops:
  0.0 7.0 %copy-start.1 = (f32[2,7,7,256]{3,0,2,1:T(2,128)S(1)}, f32[2,7,7,256]{3,0,2,1:T(2,128)}, u32[]{:S(2)}) copy-start(f32[2,7,7,256]{3,0,2,1:T(2,128)} %param.16) | copy-start | bytes 301060
  0.1 6.9 %copy-start = (f32[2,1024]{1,0:T(2,128)S(1)}, f32[2,1024]{1,0:T(2,128)}, u32[]{:S(2)}) copy-start(f32[2,1024]{1,0:T(2,128)} %refs_19_.1) | copy-start | bytes 24580
  0.1 6.9 %copy-start.4 = (f32[16,256]{1,0:T(8,128)S(1)}, f32[16,256]{1,0:T(8,128)}, u32[]{:S(2)}) copy-start(f32[16,256]{1,0:T(8,128)} %refs_8_.1) | copy-start | bytes 49156
  1.1 12.3 %collective-permute-start = (f32[32,128]{1,0:T(8,128)S(1)}, f32[32,128]{1,0:T(8,128)S(1)}, u32[]{:S(2)}, u32[]{:S(2)}) collective-permute-start(f32[32,128]{1,0:T(8,128)S(1)} %get-tuple-element.25.refs_1_.refs_2_), channel_id=1, source_target_pairs={{1,2},{2,1},{3,4},{4,3},{5,6},{6,5},{7,8},{8,7},{9,10},{10,9},{11,... | collective-permute-start | bytes 49160 | tf_op jit(solution)/shard_map/ppermute | solution.py:479
  1.8 5.2 %copy-start.3 = (f32[2,256]{1,0:T(2,128)S(1)}, f32[2,256]{1,0:T(2,128)}, u32[]{:S(2)}) copy-start(f32[2,256]{1,0:T(2,128)} %refs_18_.1) | copy-start | bytes 6148
  1.8 5.2 %collective-permute-start.1 = (f32[8,128]{1,0:T(8,128)S(1)}, f32[8,128]{1,0:T(8,128)S(1)}, u32[]{:S(2)}, u32[]{:S(2)}) collective-permute-start(f32[8,128]{1,0:T(8,128)S(1)} %get-tuple-element.26.refs_3_.refs_5_), channel_id=1, source_target_pairs={{0,1},{1,0},{2,3},{3,2},{4,5},{5,4},{6,7},{7,6},{8,9},{9,8},{10,11... | collective-permute-start | bytes 12296 | tf_op jit(solution)/shard_map/ppermute | solution.py:476
  13.4 0.7 %copy-start.2 = (f32[256,16]{0,1:T(8,128)S(1)}, f32[256,16]{0,1:T(8,128)}, u32[]{:S(2)}) copy-start(f32[256,16]{0,1:T(8,128)} %param.21) | copy-start | bytes 49156
  20.1 1.3 %collective-permute-start.3 = (bf16[3,32,128]{2,1,0:T(8,128)(2,1)S(1)}, bf16[3,32,128]{2,1,0:T(8,128)(2,1)S(1)}, u32[]{:S(2)}, u32[]{:S(2)}) collective-permute-start(bf16[3,32,128]{2,1,0:T(8,128)(2,1)S(1)} %get-tuple-element.39), channel_id=1, source_target_pairs={{0,1},{1,0},{2,3},{3,2},{4,5},{5,4},{6,7},{7,6},{8,9},{9,8},{10,11... | collective-permute-start | bytes 73736 | tf_op jit(solution)/shard_map/ppermute | solution.py:476
  20.5 6.6 %collective-permute-start.2 = (bf16[3,32,128]{2,1,0:T(8,128)(2,1)S(1)}, bf16[3,32,128]{2,1,0:T(8,128)(2,1)S(1)}, u32[]{:S(2)}, u32[]{:S(2)}) collective-permute-start(bf16[3,32,128]{2,1,0:T(8,128)(2,1)S(1)} %get-tuple-element.39), channel_id=1, source_target_pairs={{1,2},{2,1},{3,4},{4,3},{5,6},{6,5},{7,8},{8,7},{9,10},{10,9},{11,... | collective-permute-start | bytes 73736 | tf_op jit(solution)/shard_map/ppermute | solution.py:479
  33.6 3.8 %collective-permute-start.4 = (f32[2,32,128]{2,1,0:T(8,128)S(1)}, f32[2,32,128]{2,1,0:T(8,128)S(1)}, u32[]{:S(2)}, u32[]{:S(2)}) collective-permute-start(f32[2,32,128]{2,1,0:T(8,128)S(1)} %get-tuple-element.44), channel_id=1, source_target_pairs={{0,1},{1,0},{2,3},{3,2},{4,5},{5,4},{6,7},{7,6},{8,9},{9,8},{10,11... | collective-permute-start | bytes 98312 | tf_op jit(solution)/shard_map/ppermute | solution.py:476

commit v6 on v5

--- a/solution.py
+++ b/solution.py
@@ -174,12 +174,14 @@
     for n, i, x in spots(dot(jnp.concatenate([hi, lo], axis=-1), three[...])):
         if HALO <= i < HALO + count:
             centre[n, i - HALO] = x.astype(BF16)
-    group = lane_group((1, 1, 1, LANES))
+    group = lane_group((COLS, LANES))
     at = PAD - HALO
-    picked = shift[0:many, :, at : at + COLS, :]
-    for dx in range(1, TAPS):
-        picked = jnp.where(group == dx, shift[0:many, :, at + dx : at + dx + COLS, :], picked)
-    patch[0:many] = picked.astype(BF16)
+    for n in range(many):
+        for i in range(rows):
+            picked = shift[n, i, at : at + COLS, :]
+            for dx in range(1, TAPS):
+                picked = jnp.where(group == dx, shift[n, i, at + dx : at + dx + COLS, :], picked)
+            patch[n, i] = picked.astype(BF16)
     cells = many * count * COLS
     wide = [patch[0:many, dy : dy + count].reshape(cells, LANES) for dy in range(TAPS)]
     base = dot(jnp.concatenate(wide, axis=-1), weff[...])
@@ -189,15 +191,18 @@
 
 
 def first_block(states, place, count, ones, first_time, temb, gain, up_w, up_b, down_w, weff, in_three, *scratch):
+    *scratch, normed = scratch
     base, stream = block_zero(states, place, count, weff, in_three, *scratch)
-    normed, residual = [], []
+    residual = []
     for t in range(TIMES):
         n = min(t, len(states) - 1)
         shown = temb[first_time + t : first_time + t + 1, :]
-        conv = base[n] + ones * shown
-        normed.append(normalise(conv.reshape(count * COLS, WIDTH), gain[0:1, :]))
+        lift = [ones[i] * shown for i in range(len(ones))]
+        for i in range(count):
+            low = (t * count + i) * COLS
+            normed[low : low + COLS, :] = normalise(base[n, i] + lift[min(i, len(ones) - 1)], gain[0:1, :])
         residual.append(stream[n] + shown)
-    out = pointwise(jnp.concatenate(normed, axis=0), 0, up_w, up_b, down_w).reshape(TIMES, count, COLS, WIDTH)
+    out = pointwise(normed[...], 0, up_w, up_b, down_w).reshape(TIMES, count, COLS, WIDTH)
     return [residual[t] + out[t] for t in range(TIMES)]
 
 
@@ -239,17 +244,17 @@
     first_time = 1 if last else 0
     count = len(NEAR)
     if last:
-        (flags, own, inner, mine, inner_terms, temb, weff, by_row, tap_rows, spread, three, in_three, up_w, down_w, gain, up_b,
-         partial, kept, shift, patch, centre, *wide) = refs
+        (flags, own, inner, mine, inner_terms, temb, weff, by_row, tap_rows, spread, three, in_three, _, up_w, down_w, gain, up_b,
+         partial, kept, shift, patch, centre, normed, *wide) = refs
         turn = flags[0]
         states, state = [], [own[...], inner[...]]
         for t in range(TIMES):
             state = [state[0] + mine[t], state[1] + inner_terms[t].astype(F32)]
             states.append(state)
     else:
-        (flags, own, inner, clock, other_clock, time_hbm, up_hbm, down_hbm, in_w, taps, gain, up_b,
-         partial, kept, temb, weff, by_row, tap_rows, spread, three, in_three, up_w, down_w,
-         shift, patch, centre, *wide, time_w, sems) = refs
+        (flags, own, inner, clock, other_clock, time_hbm, up_hbm, down_hbm, in_w, taps, gain, up_b, out_t,
+         partial, kept, temb, weff, by_row, tap_rows, spread, three, in_three, out_three, up_w, down_w,
+         shift, patch, centre, normed, *wide, time_w, sems) = refs
         turn = flags[0]
         copies = [pltpu.make_async_copy(time_hbm, time_w, sems.at[4])]
         for block in range(2):
@@ -262,6 +267,8 @@
         make_tap_rows(turn, taps, tap_rows)
         make_spread(spread, three)
         make_in_three(in_w, in_three)
+        out_hi, out_lo = split(jnp.concatenate([out_t[...]] * 8, axis=0))
+        out_three[...] = jnp.concatenate([out_hi, out_hi, out_lo], axis=-1)
         copies[0].wait()
         temb[...] = embed(turn, clock, other_clock, time_w)
         states = [[own[...], inner[...]]]
@@ -278,8 +285,8 @@
         return i if i < count + REACH else None
 
     after = first_block(
-        states, place, count, ones[None], first_time, temb, gain, up_w, up_b, down_w, weff, in_three,
-        shift, patch, centre, spread, three,
+        states, place, count, [ones], first_time, temb, gain, up_w, up_b, down_w, weff, in_three,
+        shift, patch, centre, spread, three, normed,
     )
     for t in range(TIMES):
         kept[t] = after[t][0 : OWN - HALO]
@@ -305,8 +312,8 @@
         flags, outer, own, outer_terms, mine, *refs = refs
     else:
         flags, outer, own, *refs = refs
-    (clock, other_clock, partial, kept, temb, weff, by_row, tap_rows, spread, three, in_three, up_w, down_w, gain, up_b, out_t,
-     first_out, second_out, shift, patch, centre, *wide) = refs
+    (clock, other_clock, partial, kept, temb, weff, by_row, tap_rows, spread, three, in_three, out_three, up_w, down_w, gain, up_b,
+     first_out, second_out, shift, patch, centre, normed, second_normed, *wide) = refs
     conv_buf = wide[2 * TIMES :]
     turn, inside = flags[0], flags[1].astype(F32)
     first_time = 1 if last else 0
@@ -321,11 +328,8 @@
             else:
                 hidden = hidden + by_row[dy]
         ones.append(seen + hidden * inside)
-    ones = jnp.concatenate(ones, axis=0).reshape(count, COLS, WIDTH)
     for ref in wide[: 2 * TIMES]:
         clear_sides(ref)
-    out_hi, out_lo = split(jnp.concatenate([out_t[...]] * 8, axis=0))
-    out_three = jnp.concatenate([out_hi, out_hi, out_lo], axis=-1)
     low, high = both_clocks(turn, clock, other_clock)
     sizes = [low[:, 2:3], low[:, 3:4], high[:, 2:3], high[:, 3:4]]
     group = lane_group((1, LANES))
@@ -341,7 +345,7 @@
         states.append(state)
     after = first_block(
         states if last else [state], place, count, ones, first_time, temb, gain, up_w, up_b, down_w, weff, in_three,
-        shift, patch, centre, spread, three,
+        shift, patch, centre, spread, three, normed,
     )
     for t in range(TIMES):
         for half in range(2):
@@ -349,7 +353,7 @@
             wide[2 * t + half][0:HALO, PAD : PAD + COLS, :] = after[t][0:HALO, :, lanes] * inside
             wide[2 * t + half][HALO:, PAD : PAD + COLS, :] = after[t][HALO:, :, lanes]
     touched = len(pairs_of(EDGE))
-    normed, stream = [], []
+    stream = []
     for t in range(TIMES):
 
         def source(i, half, dx):
@@ -360,13 +364,17 @@
             conv_buf[t][h, :, half * LANES : (half + 1) * LANES] = x
 
         depthwise(tap_rows, source, pairs_of(EDGE), lambda h, half: partial[2 * t + half, h], done)
-        rest = [partial[2 * t + half, touched:].reshape((OWN - touched) * COLS, LANES) for half in range(2)]
-        conv = [conv_buf[t][...].reshape(touched * COLS, WIDTH), jnp.concatenate(rest, axis=-1)]
-        normed.append(normalise(jnp.concatenate(conv, axis=0), gain[1:2, :]))
+        for h in range(OWN):
+            low = (t * OWN + h) * COLS
+            if h < touched:
+                conv = conv_buf[t][h]
+            else:
+                conv = jnp.concatenate([partial[2 * t + half, h] for half in range(2)], axis=-1)
+            second_normed[low : low + COLS, :] = normalise(conv, gain[1:2, :])
         stream += [after[t][HALO:].reshape(HALO * COLS, WIDTH), kept[t].reshape((OWN - HALO) * COLS, WIDTH)]
-    out = pointwise(jnp.concatenate(normed, axis=0), 1, up_w, up_b, down_w)
+    out = pointwise(second_normed[...], 1, up_w, up_b, down_w)
     hi, lo = split(jnp.concatenate(stream, axis=0) + out)
-    drifts = dot_nt(jnp.concatenate([hi, lo, hi], axis=-1), out_three).reshape(TIMES, OWN, COLS, LANES)
+    drifts = dot_nt(jnp.concatenate([hi, lo, hi], axis=-1), out_three[...]).reshape(TIMES, OWN, COLS, LANES)
     terms = []
     for t in range(TIMES):
         dense = drifts[t, 0]
@@ -400,21 +408,22 @@
         pltpu.VMEM((many, count + REACH, WIDE, LANES), F32),
         pltpu.VMEM((many, count + REACH, COLS, LANES), BF16),
         pltpu.VMEM((many, count, COLS, LANES), BF16),
-    ] + [pltpu.VMEM((count, WIDE, LANES), F32)] * (2 * TIMES)
+        pltpu.VMEM((TIMES * count * COLS, WIDTH), BF16),
+    ]
 
 
 def near(last, up_w, down_w, *args):
     outs = [pltpu.VMEM((2 * TIMES, OWN, COLS, LANES), F32), pltpu.VMEM((TIMES, OWN - HALO, COLS, WIDTH), F32)]
-    scratch = working(len(NEAR), TIMES if last else 1)
+    scratch = working(len(NEAR), TIMES if last else 1) + [pltpu.VMEM((len(NEAR), WIDE, LANES), F32)] * (2 * TIMES)
     if last:
         specs = [SMEM] + [VMEM] * (len(args) - 1)
     else:
         outs += [pltpu.VMEM((8, WIDTH), F32), pltpu.VMEM((TAPS * LANES, WIDTH), BF16), pltpu.VMEM((TAPS, COLS, WIDTH), F32)]
         outs += [pltpu.VMEM((2, 56, LANES), F32), pltpu.VMEM((LANES, OWN * LANES), BF16)]
-        outs += [pltpu.VMEM((2 * LANES, OWN * LANES), BF16), pltpu.VMEM((LANES, WIDTH), BF16)]
+        outs += [pltpu.VMEM((2 * LANES, OWN * LANES), BF16), pltpu.VMEM((LANES, WIDTH), BF16), pltpu.VMEM((LANES, 3 * WIDTH), BF16)]
         outs += [pltpu.VMEM(up_w.shape, BF16), pltpu.VMEM(down_w.shape, BF16)]
         scratch += [pltpu.VMEM((WIDTH, WIDTH), F32), pltpu.SemaphoreType.DMA((5,))]
-        specs = [SMEM] + [VMEM] * 4 + [HBM] * 3 + [VMEM] * 4
+        specs = [SMEM] + [VMEM] * 4 + [HBM] * 3 + [VMEM] * 5
     return pl.pallas_call(
         functools.partial(near_kernel, last),
         out_shape=outs,
@@ -436,7 +445,10 @@
         out_shape=outs,
         in_specs=[SMEM] + [VMEM] * (len(args) - 1),
         out_specs=[VMEM, VMEM],
-        scratch_shapes=working(len(EDGE), TIMES if last else 1) + [pltpu.VMEM((touched, COLS, WIDTH), F32)] * TIMES,
+        scratch_shapes=working(len(EDGE), TIMES if last else 1)
+        + [pltpu.VMEM((TIMES * OWN * COLS, WIDTH), BF16)]
+        + [pltpu.VMEM((len(EDGE), WIDE, LANES), F32)] * (2 * TIMES)
+        + [pltpu.VMEM((touched, COLS, WIDTH), F32)] * TIMES,
         compiler_params=LARGE,
     )(*args)
 
@@ -481,17 +493,17 @@
     flags = jnp.stack([tm, jnp.where(tm == 0, s > 0, s < space - 1).astype(jnp.int32)]).astype(jnp.int32)
     own, inner, clock = prepare(flags, pinned(timesteps), pinned(step_sizes), pinned(start_state.transpose(0, 2, 1)))
     other_clock = over_tm(clock)
-    outer = over_space(own)
+    outer = over_space(jnp.where(s < space, own, 0.0))
     taps = conv_kernel.transpose(1, 2, 0, 3)
 
     partial, kept, *made = near(
         False, up_weight, down_weight, flags, own, inner, clock, other_clock,
-        pinned(time_weight), pinned(up_weight), pinned(down_weight), in_weight, taps, norm_gain, up_bias,
+        pinned(time_weight), pinned(up_weight), pinned(down_weight), in_weight, taps, norm_gain, up_bias, out_weight.T,
     )
-    rest = (norm_gain, up_bias, out_weight.T)
+    rest = (norm_gain, up_bias)
     terms, sent = edge(False, flags, outer, own, clock, other_clock, partial, kept, *made, *rest)
     inner_terms, outer_terms = over_tm(sent), over_space(sent)
-    partial, kept = near(True, up_weight, down_weight, flags, own, inner, terms, inner_terms, *made, *rest[:-1])
+    partial, kept = near(True, up_weight, down_weight, flags, own, inner, terms, inner_terms, *made, *rest)
     keep, give = edge(True, flags, outer, own, outer_terms, terms, clock, other_clock, partial, kept, *made, *rest)
     return finish(flags, keep, over_tm(give)).transpose(0, 1, 3, 2)
 

time: 39.1 us -> 39 us (level)
  no operation moved by 1% of the time
where the time goes in v6:
time: 39 us; the launch traced here: 38.7 us
  Pallas kernels  26.9 us (69%)
  starting transfers between devices  9.25 us (24%)
  waiting for transfers between devices  1.7 us (4%)
  local copies, waits for them, and re-layouts  0.69 us (2%)
    pallas_call x2, Pallas kernels, edge(): pl.pallas_call(functools.partial(edge_kernel, last), out_shape=outs, in_s...  12.4 us
    pallas_call x2, Pallas kernels, near(): pl.pallas_call(functools.partial(near_kernel, last), out_shape=outs, in_s...  12.2 us
    ppermute x3, starting transfers between devices, over_tm(): return lax.ppermute(x, 'tm', beside)  7.76 us
    ppermute x3, waiting for transfers between devices, over_tm(): return lax.ppermute(x, 'tm', beside)  1.69 us
    ppermute x2, starting transfers between devices, over_space(): return lax.ppermute(x, ('space', 'tm'), across)  1.49 us
    pallas_call x1, Pallas kernels, finish(): pl.pallas_call(finish_kernel, out_shape=jax.ShapeDtypeStruct((2, 2 * OWN,...  1.38 us
    pallas_call x1, Pallas kernels, prepare(): pl.pallas_call(prepare_kernel, out_shape=[dense, dense, jax.ShapeDtypeStr...  0.99 us
  transfers between devices with their start and end apart: 5, of which 2 were waited for; matrix products, arithmetic and copies ran while one was open for 0% of the time, Pallas kernels for 31%

profile of v6, /device:TPU:0, one launch (start us, length us, event | category | flops | bytes accessed | tf_op | source)
XLA Modules:
  0.0 38.7 jit_solution(9678293614131406809)
XLA Ops:
  0.0 0.1 pad_add_fusion.flags.refs_0_
  0.1 1.0 %shard_map.109 = (f32[32,128]{1,0:T(8,128)S(1)}, f32[32,128]{1,0:T(8,128)S(1)}, f32[8,128]{1,0:T(8,128)S(1)}) custom-call(s32[2]{0:T(128)S(1)} %pad_add_fusion.flags.refs_0_, s32[2]{0:T(128)} %times.1, f32[2]{0:T(128)} %sizes.1, f32[16,16,32]{2,1,0:T(8,128)} %bitcast.8), custom_call_target="tpu_custom_call" | custom-call | tf_op jit(solution)/shard_map/pallas_call | solution.py:458
  1.1 0.0 copy-start
  1.1 0.0 copy-start.3
  1.1 0.7 %collective-permute-start = (f32[32,128]{1,0:T(8,128)S(1)}, f32[32,128]{1,0:T(8,128)S(1)}, u32[]{:S(2)}, u32[]{:S(2)}) collective-permute-start(f32[32,128]{1,0:T(8,128)S(1)} %broadcast_select_fusion), channel_id=1, source_target_pairs={{1,2},{2,1},{3,4},{4,3},{5,6},{6,5},{7,8},{8,7},{9,10},{10,9},{11,... | collective-permute-start | bytes 49160 | tf_op jit(solution)/shard_map/ppermute | solution.py:491
  1.8 4.4 %collective-permute-start.1 = (f32[8,128]{1,0:T(8,128)S(1)}, f32[8,128]{1,0:T(8,128)S(1)}, u32[]{:S(2)}, u32[]{:S(2)}) collective-permute-start(f32[8,128]{1,0:T(8,128)S(1)} %get-tuple-element.27.refs_3_.refs_5_), channel_id=1, source_target_pairs={{0,1},{1,0},{2,3},{3,2},{4,5},{5,4},{6,7},{7,6},{8,9},{9,8},{10,11... | collective-permute-start | bytes 12296 | tf_op jit(solution)/shard_map/ppermute | solution.py:488
  6.1 0.8 %collective-permute-done.1.refs_4_.refs_6_ = f32[8,128]{1,0:T(8,128)S(1)} collective-permute-done((f32[8,128]{1,0:T(8,128)S(1)}, f32[8,128]{1,0:T(8,128)S(1)}, u32[]{:S(2)}, u32[]{:S(2)}) %collective-permute-start.1) | collective-permute-done | bytes 4128 | tf_op jit(solution)/shard_map/ppermute | solution.py:488
  7.0 0.0 copy-done.1
  7.0 0.0 copy-done.4
  7.0 0.0 copy-done
  7.0 0.0 copy-done.3
  7.0 0.7 %copy-done.2 = f32[2,256]{1,0:T(2,128)S(1)} copy-done((f32[2,256]{1,0:T(2,128)S(1)}, f32[2,256]{1,0:T(2,128)}, u32[]{:S(2)}) %copy-start.2) | copy-done | bytes 2072
  7.7 6.4 %shard_map.110 = (f32[6,8,32,128]{3,2,1,0:T(8,128)S(1)}, f32[3,5,32,256]{3,2,1,0:T(8,128)S(1)}, f32[8,256]{1,0:T(8,128)S(1)}, bf16[896,256]{1,0:T(8,128)(2,1)S(1...) custom-call(s32[2]{0:T(128)S(1)} %pad_add_fusion.flags.refs_0_, ...), custom_call_target="tpu_custom_call" | custom-call | tf_op jit(solution)/shard_map/pallas_call | solution.py:427
  14.1 0.0 collective-permute-done.refs_1_
  14.1 6.0 %shard_map.111 = (f32[3,32,128]{2,1,0:T(8,128)S(1)}, bf16[3,32,128]{2,1,0:T(8,128)(2,1)S(1)}) custom-call(s32[2]{0:T(128)S(1)} %pad_add_fusion.flags.refs_0_, f32[32,128]{1,0:T(8,128)S(1)} %collective-permute-done.refs_1_, f32[32,128]{1,0:T(8,128)S(1)} %get-tuple-element.26.refs_1_.refs_2_, f32[8,128]{1,0:T(8,128)S(1)} %get-tuple-element.27.refs_3_.refs_5_, ...), custom_call_target="tpu_custom_call" | custom-call | tf_op jit(solution)/shard_map/pallas_call | solution.py:443
  20.1 0.4 %collective-permute-start.3 = (bf16[3,32,128]{2,1,0:T(8,128)(2,1)S(1)}, bf16[3,32,128]{2,1,0:T(8,128)(2,1)S(1)}, u32[]{:S(2)}, u32[]{:S(2)}) collective-permute-start(bf16[3,32,128]{2,1,0:T(8,128)(2,1)S(1)} %get-tuple-element.41), channel_id=1, source_target_pairs={{0,1},{1,0},{2,3},{3,2},{4,5},{5,4},{6,7},{7,6},{8,9},{9,8},{10,11... | collective-permute-start | bytes 73736 | tf_op jit(solution)/shard_map/ppermute | solution.py:488
  20.5 0.8 %collective-permute-start.2 = (bf16[3,32,128]{2,1,0:T(8,128)(2,1)S(1)}, bf16[3,32,128]{2,1,0:T(8,128)(2,1)S(1)}, u32[]{:S(2)}, u32[]{:S(2)}) collective-permute-start(bf16[3,32,128]{2,1,0:T(8,128)(2,1)S(1)} %get-tuple-element.41), channel_id=1, source_target_pairs={{1,2},{2,1},{3,4},{4,3},{5,6},{6,5},{7,8},{8,7},{9,10},{10,9},{11,... | collective-permute-start | bytes 73736 | tf_op jit(solution)/shard_map/ppermute | solution.py:491
  21.3 0.0 collective-permute-done.3.refs_4_
  21.3 5.7 %shard_map.112 = (f32[6,8,32,128]{3,2,1,0:T(8,128)S(1)}, f32[3,5,32,256]{3,2,1,0:T(8,128)S(1)}) custom-call(s32[2]{0:T(128)S(1)} %pad_add_fusion.flags.refs_0_, f32[32,128]{1,0:T(8,128)S(1)} %get-tuple-element.26.refs_1_.refs_2_, f32[32,128]{1,0:T(8,128)S(1)} %get-tuple-element.28.refs_2_, f32[3,32,128]{2,1,0:T(8,128)S(1)} %get-tuple-element.42.refs_3_.refs_4_, ...), custom_call_target="tpu_custom_call" | custom-call | tf_op jit(solution)/shard_map/pallas_call | solution.py:427
  27.1 0.0 collective-permute-done.2.refs_3_
  27.1 6.4 %shard_map.113 = (f32[2,32,128]{2,1,0:T(8,128)S(1)}, f32[2,32,128]{2,1,0:T(8,128)S(1)}) custom-call(s32[2]{0:T(128)S(1)} %pad_add_fusion.flags.refs_0_, f32[32,128]{1,0:T(8,128)S(1)} %collective-permute-done.refs_1_, f32[32,128]{1,0:T(8,128)S(1)} %get-tuple-element.26.refs_1_.refs_2_, bf16[3,32,128]{2,1,0:T(8,128)(2,1)S(1)} %collective-permute-done.2.refs_3_, ...), custom_call_target="tpu_custom_call" | custom-call | tf_op jit(solution)/shard_map/pallas_call | solution.py:443
  33.5 3.0 %collective-permute-start.4 = (f32[2,32,128]{2,1,0:T(8,128)S(1)}, f32[2,32,128]{2,1,0:T(8,128)S(1)}, u32[]{:S(2)}, u32[]{:S(2)}) collective-permute-start(f32[2,32,128]{2,1,0:T(8,128)S(1)} %get-tuple-element.46), channel_id=1, source_target_pairs={{0,1},{1,0},{2,3},{3,2},{4,5},{5,4},{6,7},{7,6},{8,9},{9,8},{10,11... | collective-permute-start | bytes 98312 | tf_op jit(solution)/shard_map/ppermute | solution.py:488
  36.5 0.9 %collective-permute-done.4.got = f32[2,32,128]{2,1,0:T(8,128)S(1)} collective-permute-done((f32[2,32,128]{2,1,0:T(8,128)S(1)}, f32[2,32,128]{2,1,0:T(8,128)S(1)}, u32[]{:S(2)}, u32[]{:S(2)}) %collective-permute-start.4) | collective-permute-done | bytes 32800 | tf_op jit(solution)/shard_map/ppermute | solution.py:488
  37.4 1.4 %shard_map.114 = f32[2,16,16,32]{3,2,1,0:T(8,128)} custom-call(s32[2]{0:T(128)S(1)} %pad_add_fusion.flags.refs_0_, f32[2,32,128]{2,1,0:T(8,128)S(1)} %get-tuple-element.45.keep, f32[2,32,128]{2,1,0:T(8,128)S(1)} %collective-permute-done.4.got), custom_call_target="tpu_custom_call" | custom-call | tf_op jit(solution)/shard_map/pallas_call | solution.py:468
  (4 shorter events, 0.0 us)
Async XLA Ops:
  0.0 7.0 %copy-start.1 = (f32[2,7,7,256]{3,0,2,1:T(2,128)S(1)}, f32[2,7,7,256]{3,0,2,1:T(2,128)}, u32[]{:S(2)}) copy-start(f32[2,7,7,256]{3,0,2,1:T(2,128)} %param.16) | copy-start | bytes 301060
  0.1 6.9 %copy-start.4 = (f32[256,16]{0,1:T(8,128)S(1)}, f32[256,16]{0,1:T(8,128)}, u32[]{:S(2)}) copy-start(f32[256,16]{0,1:T(8,128)} %param.21) | copy-start | bytes 49156
  1.1 5.9 %copy-start = (f32[2,1024]{1,0:T(2,128)S(1)}, f32[2,1024]{1,0:T(2,128)}, u32[]{:S(2)}) copy-start(f32[2,1024]{1,0:T(2,128)} %refs_20_.1) | copy-start | bytes 24580
  1.1 5.9 %copy-start.3 = (f32[16,256]{1,0:T(8,128)S(1)}, f32[16,256]{1,0:T(8,128)}, u32[]{:S(2)}) copy-start(f32[16,256]{1,0:T(8,128)} %refs_8_.1) | copy-start | bytes 49156
  1.1 13.0 %collective-permute-start = (f32[32,128]{1,0:T(8,128)S(1)}, f32[32,128]{1,0:T(8,128)S(1)}, u32[]{:S(2)}, u32[]{:S(2)}) collective-permute-start(f32[32,128]{1,0:T(8,128)S(1)} %broadcast_select_fusion), channel_id=1, source_target_pairs={{1,2},{2,1},{3,4},{4,3},{5,6},{6,5},{7,8},{8,7},{9,10},{10,9},{11,... | collective-permute-start | bytes 49160 | tf_op jit(solution)/shard_map/ppermute | solution.py:491
  1.8 5.2 %collective-permute-start.1 = (f32[8,128]{1,0:T(8,128)S(1)}, f32[8,128]{1,0:T(8,128)S(1)}, u32[]{:S(2)}, u32[]{:S(2)}) collective-permute-start(f32[8,128]{1,0:T(8,128)S(1)} %get-tuple-element.27.refs_3_.refs_5_), channel_id=1, source_target_pairs={{0,1},{1,0},{2,3},{3,2},{4,5},{5,4},{6,7},{7,6},{8,9},{9,8},{10,11... | collective-permute-start | bytes 12296 | tf_op jit(solution)/shard_map/ppermute | solution.py:488
  7.0 0.7 %copy-start.2 = (f32[2,256]{1,0:T(2,128)S(1)}, f32[2,256]{1,0:T(2,128)}, u32[]{:S(2)}) copy-start(f32[2,256]{1,0:T(2,128)} %refs_19_.1) | copy-start | bytes 6148
  20.1 1.3 %collective-permute-start.3 = (bf16[3,32,128]{2,1,0:T(8,128)(2,1)S(1)}, bf16[3,32,128]{2,1,0:T(8,128)(2,1)S(1)}, u32[]{:S(2)}, u32[]{:S(2)}) collective-permute-start(bf16[3,32,128]{2,1,0:T(8,128)(2,1)S(1)} %get-tuple-element.41), channel_id=1, source_target_pairs={{0,1},{1,0},{2,3},{3,2},{4,5},{5,4},{6,7},{7,6},{8,9},{9,8},{10,11... | collective-permute-start | bytes 73736 | tf_op jit(solution)/shard_map/ppermute | solution.py:488
  20.5 6.6 %collective-permute-start.2 = (bf16[3,32,128]{2,1,0:T(8,128)(2,1)S(1)}, bf16[3,32,128]{2,1,0:T(8,128)(2,1)S(1)}, u32[]{:S(2)}, u32[]{:S(2)}) collective-permute-start(bf16[3,32,128]{2,1,0:T(8,128)(2,1)S(1)} %get-tuple-element.41), channel_id=1, source_target_pairs={{1,2},{2,1},{3,4},{4,3},{5,6},{6,5},{7,8},{8,7},{9,10},{10,9},{11,... | collective-permute-start | bytes 73736 | tf_op jit(solution)/shard_map/ppermute | solution.py:491
  33.5 3.8 %collective-permute-start.4 = (f32[2,32,128]{2,1,0:T(8,128)S(1)}, f32[2,32,128]{2,1,0:T(8,128)S(1)}, u32[]{:S(2)}, u32[]{:S(2)}) collective-permute-start(f32[2,32,128]{2,1,0:T(8,128)S(1)} %get-tuple-element.46), channel_id=1, source_target_pairs={{0,1},{1,0},{2,3},{3,2},{4,5},{5,4},{6,7},{7,6},{8,9},{9,8},{10,11... | collective-permute-start | bytes 98312 | tf_op jit(solution)/shard_map/ppermute | solution.py:488

commit v7 on v6

--- a/solution.py
+++ b/solution.py
@@ -73,9 +73,9 @@
     bottom = to_dense([start[2 * OWN - 1 - h] for h in range(OWN)])
     own[...] = jnp.where(turned, bottom, top)
     inner[...] = jnp.where(turned, top, bottom)
-    lane = lax.broadcasted_iota(jnp.int32, (8, LANES), 1)
+    lane = lax.broadcasted_iota(jnp.int32, clock.shape, 1)
     values = (times[0].astype(F32), times[1].astype(F32), sizes[0], sizes[1])
-    filled = jnp.zeros((8, LANES), F32)
+    filled = jnp.zeros(clock.shape, F32)
     for i, value in enumerate(values):
         filled = jnp.where(lane == i, value, filled)
     clock[...] = filled
@@ -244,7 +244,7 @@
     first_time = 1 if last else 0
     count = len(NEAR)
     if last:
-        (flags, own, inner, mine, inner_terms, temb, weff, by_row, tap_rows, spread, three, in_three, _, up_w, down_w, gain, up_b,
+        (flags, own, inner, mine, inner_terms, temb, weff, by_row, tap_rows, spread, three, in_three, _, gain, up_w, down_w, up_b,
          partial, kept, shift, patch, centre, normed, *wide) = refs
         turn = flags[0]
         states, state = [], [own[...], inner[...]]
@@ -252,14 +252,15 @@
             state = [state[0] + mine[t], state[1] + inner_terms[t].astype(F32)]
             states.append(state)
     else:
-        (flags, own, inner, clock, other_clock, time_hbm, up_hbm, down_hbm, in_w, taps, gain, up_b, out_t,
-         partial, kept, temb, weff, by_row, tap_rows, spread, three, in_three, out_three, up_w, down_w,
+        (flags, own, inner, clock, other_clock, time_hbm, up_hbm, down_hbm, gain_hbm, in_w, taps, up_b, out_t,
+         partial, kept, temb, weff, by_row, tap_rows, spread, three, in_three, out_three, gain, up_w, down_w,
          shift, patch, centre, normed, *wide, time_w, sems) = refs
         turn = flags[0]
         copies = [pltpu.make_async_copy(time_hbm, time_w, sems.at[4])]
         for block in range(2):
             copies.append(pltpu.make_async_copy(up_hbm.at[block], up_w.at[block], sems.at[2 * block]))
             copies.append(pltpu.make_async_copy(down_hbm.at[block], down_w.at[block], sems.at[2 * block + 1]))
+        copies.append(pltpu.make_async_copy(gain_hbm, gain, sems.at[5]))
         for copy in copies:
             copy.start()
         make_weff(turn, in_w, taps, weff)
@@ -274,6 +275,7 @@
         states = [[own[...], inner[...]]]
         copies[1].wait()
         copies[2].wait()
+        copies[5].wait()
     ones = by_row[0]
     for dy in range(1, TAPS):
         ones = ones + by_row[dy]
@@ -312,7 +314,7 @@
         flags, outer, own, outer_terms, mine, *refs = refs
     else:
         flags, outer, own, *refs = refs
-    (clock, other_clock, partial, kept, temb, weff, by_row, tap_rows, spread, three, in_three, out_three, up_w, down_w, gain, up_b,
+    (clock, other_clock, partial, kept, temb, weff, by_row, tap_rows, spread, three, in_three, out_three, gain, up_w, down_w, up_b,
      first_out, second_out, shift, patch, centre, normed, second_normed, *wide) = refs
     conv_buf = wide[2 * TIMES :]
     turn, inside = flags[0], flags[1].astype(F32)
@@ -421,9 +423,10 @@
         outs += [pltpu.VMEM((8, WIDTH), F32), pltpu.VMEM((TAPS * LANES, WIDTH), BF16), pltpu.VMEM((TAPS, COLS, WIDTH), F32)]
         outs += [pltpu.VMEM((2, 56, LANES), F32), pltpu.VMEM((LANES, OWN * LANES), BF16)]
         outs += [pltpu.VMEM((2 * LANES, OWN * LANES), BF16), pltpu.VMEM((LANES, WIDTH), BF16), pltpu.VMEM((LANES, 3 * WIDTH), BF16)]
+        outs += [pltpu.VMEM((2, WIDTH), F32)]
         outs += [pltpu.VMEM(up_w.shape, BF16), pltpu.VMEM(down_w.shape, BF16)]
-        scratch += [pltpu.VMEM((WIDTH, WIDTH), F32), pltpu.SemaphoreType.DMA((5,))]
-        specs = [SMEM] + [VMEM] * 4 + [HBM] * 3 + [VMEM] * 5
+        scratch += [pltpu.VMEM((WIDTH, WIDTH), F32), pltpu.SemaphoreType.DMA((6,))]
+        specs = [SMEM] + [VMEM] * 4 + [HBM] * 4 + [VMEM] * 4
     return pl.pallas_call(
         functools.partial(near_kernel, last),
         out_shape=outs,
@@ -457,7 +460,7 @@
     dense = jax.ShapeDtypeStruct((COLS, LANES), F32)
     return pl.pallas_call(
         prepare_kernel,
-        out_shape=[dense, dense, jax.ShapeDtypeStruct((8, LANES), F32)],
+        out_shape=[dense, dense, jax.ShapeDtypeStruct((32, LANES), F32)],
         in_specs=[SMEM, SMEM, SMEM, VMEM],
         out_specs=[VMEM] * 3,
         compiler_params=SMALL,
@@ -493,14 +496,14 @@
     flags = jnp.stack([tm, jnp.where(tm == 0, s > 0, s < space - 1).astype(jnp.int32)]).astype(jnp.int32)
     own, inner, clock = prepare(flags, pinned(timesteps), pinned(step_sizes), pinned(start_state.transpose(0, 2, 1)))
     other_clock = over_tm(clock)
-    outer = over_space(jnp.where(s < space, own, 0.0))
+    outer = over_space(own)
     taps = conv_kernel.transpose(1, 2, 0, 3)
 
     partial, kept, *made = near(
         False, up_weight, down_weight, flags, own, inner, clock, other_clock,
-        pinned(time_weight), pinned(up_weight), pinned(down_weight), in_weight, taps, norm_gain, up_bias, out_weight.T,
+        pinned(time_weight), pinned(up_weight), pinned(down_weight), pinned(norm_gain), in_weight, taps, up_bias, out_weight.T,
     )
-    rest = (norm_gain, up_bias)
+    rest = (up_bias,)
     terms, sent = edge(False, flags, outer, own, clock, other_clock, partial, kept, *made, *rest)
     inner_terms, outer_terms = over_tm(sent), over_space(sent)
     partial, kept = near(True, up_weight, down_weight, flags, own, inner, terms, inner_terms, *made, *rest)

time: 39 us -> 36.7 us (0.941)
  local copies, waits for them, and re-layouts: 0.69 us -> 0.02 us
  waiting for transfers between devices: 1.7 us -> 1.06 us
  starting transfers between devices: 9.25 us -> 8.77 us
  Pallas kernels: 26.9 us -> 26.5 us
    unnamed x10 -> x8, local copies, waits for them, and re-layouts: 0.69 us -> 0.02 us
    ppermute x3, waiting for transfers between devices: 1.69 us -> 1.05 us  [over_tm(): return lax.ppermute(x, 'tm', beside)]
    ppermute x3, starting transfers between devices: 7.76 us -> 7.29 us  [over_tm(): return lax.ppermute(x, 'tm', beside)]
  transfers between devices with their start and end apart: 5 -> 5, of which waited for: 2 -> 2; matrix products, arithmetic and copies ran while one was open for 0% -> 0% of each run, Pallas kernels for 31% -> 32%
where the time goes in v7:
time: 36.7 us; the launch traced here: 36.5 us
  Pallas kernels  26.5 us (72%)
  starting transfers between devices  8.77 us (24%)
  waiting for transfers between devices  1.06 us (3%)
    pallas_call x2, Pallas kernels, edge(): pl.pallas_call(functools.partial(edge_kernel, last), out_shape=outs, in_s...  12.3 us
    pallas_call x2, Pallas kernels, near(): pl.pallas_call(functools.partial(near_kernel, last), out_shape=outs, in_s...  11.8 us
    ppermute x3, starting transfers between devices, over_tm(): return lax.ppermute(x, 'tm', beside)  7.29 us
    ppermute x2, starting transfers between devices, over_space(): return lax.ppermute(x, ('space', 'tm'), across)  1.48 us
    pallas_call x1, Pallas kernels, finish(): pl.pallas_call(finish_kernel, out_shape=jax.ShapeDtypeStruct((2, 2 * OWN,...  1.38 us
    ppermute x3, waiting for transfers between devices, over_tm(): return lax.ppermute(x, 'tm', beside)  1.05 us
    pallas_call x1, Pallas kernels, prepare(): pl.pallas_call(prepare_kernel, out_shape=[dense, dense, jax.ShapeDtypeStr...  1 us
  transfers between devices with their start and end apart: 5, of which 2 were waited for; matrix products, arithmetic and copies ran while one was open for 0% of the time, Pallas kernels for 32%

profile of v7, /device:TPU:0, one launch (start us, length us, event | category | flops | bytes accessed | tf_op | source)
XLA Modules:
  0.0 36.5 jit_solution(12629272109748127406)
XLA Ops:
  0.0 0.0 copy-start.1
  0.0 0.1 pad_add_fusion.flags.refs_0_
  0.1 0.0 copy-start.2
  0.1 1.0 %shard_map.109 = (f32[32,128]{1,0:T(8,128)S(1)}, f32[32,128]{1,0:T(8,128)S(1)}, f32[32,128]{1,0:T(8,128)S(1)}) custom-call(s32[2]{0:T(128)S(1)} %pad_add_fusion.flags.refs_0_, s32[2]{0:T(128)} %times.1, f32[2]{0:T(128)} %sizes.1, f32[16,16,32]{2,1,0:T(8,128)} %bitcast.8), custom_call_target="tpu_custom_call" | custom-call | tf_op jit(solution)/shard_map/pallas_call | solution.py:461
  1.1 0.0 copy-start
  1.1 0.5 %collective-permute-start.1 = (f32[32,128]{1,0:T(8,128)S(1)}, f32[32,128]{1,0:T(8,128)S(1)}, u32[]{:S(2)}, u32[]{:S(2)}) collective-permute-start(f32[32,128]{1,0:T(8,128)S(1)} %get-tuple-element.28.refs_3_.refs_5_), channel_id=1, source_target_pairs={{0,1},{1,0},{2,3},{3,2},{4,5},{5,4},{6,7},{7,6},{8,9},{9,8},{10,11... | collective-permute-start | bytes 49160 | tf_op jit(solution)/shard_map/ppermute | solution.py:491
  1.6 0.7 %collective-permute-start = (f32[32,128]{1,0:T(8,128)S(1)}, f32[32,128]{1,0:T(8,128)S(1)}, u32[]{:S(2)}, u32[]{:S(2)}) collective-permute-start(f32[32,128]{1,0:T(8,128)S(1)} %get-tuple-element.27.refs_1_.refs_2_), channel_id=1, source_target_pairs={{1,2},{2,1},{3,4},{4,3},{5,6},{6,5},{7,8},{8,7},{9,10},{10,9},{11,... | collective-permute-start | bytes 49160 | tf_op jit(solution)/shard_map/ppermute | solution.py:494
  2.3 0.2 collective-permute-done.1.refs_4_.refs_6_
  2.5 0.0 copy-done.1
  2.5 0.0 copy-done.2
  2.5 0.0 copy-done.3
  2.5 0.0 copy-done
  2.5 6.3 %shard_map.110 = (f32[6,8,32,128]{3,2,1,0:T(8,128)S(1)}, f32[3,5,32,256]{3,2,1,0:T(8,128)S(1)}, f32[8,256]{1,0:T(8,128)S(1)}, bf16[896,256]{1,0:T(8,128)(2,1)S(1...) custom-call(s32[2]{0:T(128)S(1)} %pad_add_fusion.flags.refs_0_, ...), custom_call_target="tpu_custom_call" | custom-call | tf_op jit(solution)/shard_map/pallas_call | solution.py:430
  8.8 0.0 collective-permute-done.refs_1_
  8.8 5.9 %shard_map.111 = (f32[3,32,128]{2,1,0:T(8,128)S(1)}, bf16[3,32,128]{2,1,0:T(8,128)(2,1)S(1)}) custom-call(s32[2]{0:T(128)S(1)} %pad_add_fusion.flags.refs_0_, f32[32,128]{1,0:T(8,128)S(1)} %collective-permute-done.refs_1_, f32[32,128]{1,0:T(8,128)S(1)} %get-tuple-element.27.refs_1_.refs_2_, f32[32,128]{1,0:T(8,128)S(1)} %get-tuple-element.28.refs_3_.refs_5_, ...), custom_call_target="tpu_custom_call" | custom-call | tf_op jit(solution)/shard_map/pallas_call | solution.py:446
  14.6 3.8 %collective-permute-start.3 = (bf16[3,32,128]{2,1,0:T(8,128)(2,1)S(1)}, bf16[3,32,128]{2,1,0:T(8,128)(2,1)S(1)}, u32[]{:S(2)}, u32[]{:S(2)}) collective-permute-start(bf16[3,32,128]{2,1,0:T(8,128)(2,1)S(1)} %get-tuple-element.43), channel_id=1, source_target_pairs={{0,1},{1,0},{2,3},{3,2},{4,5},{5,4},{6,7},{7,6},{8,9},{9,8},{10,11... | collective-permute-start | bytes 73736 | tf_op jit(solution)/shard_map/ppermute | solution.py:491
  18.4 0.8 %collective-permute-start.2 = (bf16[3,32,128]{2,1,0:T(8,128)(2,1)S(1)}, bf16[3,32,128]{2,1,0:T(8,128)(2,1)S(1)}, u32[]{:S(2)}, u32[]{:S(2)}) collective-permute-start(bf16[3,32,128]{2,1,0:T(8,128)(2,1)S(1)} %get-tuple-element.43), channel_id=1, source_target_pairs={{1,2},{2,1},{3,4},{4,3},{5,6},{6,5},{7,8},{8,7},{9,10},{10,9},{11,... | collective-permute-start | bytes 73736 | tf_op jit(solution)/shard_map/ppermute | solution.py:494
  19.3 0.0 collective-permute-done.3.refs_4_
  19.3 5.6 %shard_map.112 = (f32[6,8,32,128]{3,2,1,0:T(8,128)S(1)}, f32[3,5,32,256]{3,2,1,0:T(8,128)S(1)}) custom-call(s32[2]{0:T(128)S(1)} %pad_add_fusion.flags.refs_0_, f32[32,128]{1,0:T(8,128)S(1)} %get-tuple-element.27.refs_1_.refs_2_, f32[32,128]{1,0:T(8,128)S(1)} %get-tuple-element.29.refs_2_, f32[3,32,128]{2,1,0:T(8,128)S(1)} %get-tuple-element.44.refs_3_.refs_4_, ...), custom_call_target="tpu_custom_call" | custom-call | tf_op jit(solution)/shard_map/pallas_call | solution.py:430
  24.8 0.0 collective-permute-done.2.refs_3_
  24.8 6.4 %shard_map.113 = (f32[2,32,128]{2,1,0:T(8,128)S(1)}, f32[2,32,128]{2,1,0:T(8,128)S(1)}) custom-call(s32[2]{0:T(128)S(1)} %pad_add_fusion.flags.refs_0_, f32[32,128]{1,0:T(8,128)S(1)} %collective-permute-done.refs_1_, f32[32,128]{1,0:T(8,128)S(1)} %get-tuple-element.27.refs_1_.refs_2_, bf16[3,32,128]{2,1,0:T(8,128)(2,1)S(1)} %collective-permute-done.2.refs_3_, ...), custom_call_target="tpu_custom_call" | custom-call | tf_op jit(solution)/shard_map/pallas_call | solution.py:446
  31.3 3.0 %collective-permute-start.4 = (f32[2,32,128]{2,1,0:T(8,128)S(1)}, f32[2,32,128]{2,1,0:T(8,128)S(1)}, u32[]{:S(2)}, u32[]{:S(2)}) collective-permute-start(f32[2,32,128]{2,1,0:T(8,128)S(1)} %get-tuple-element.48), channel_id=1, source_target_pairs={{0,1},{1,0},{2,3},{3,2},{4,5},{5,4},{6,7},{7,6},{8,9},{9,8},{10,11... | collective-permute-start | bytes 98312 | tf_op jit(solution)/shard_map/ppermute | solution.py:491
  34.2 0.9 %collective-permute-done.4.got = f32[2,32,128]{2,1,0:T(8,128)S(1)} collective-permute-done((f32[2,32,128]{2,1,0:T(8,128)S(1)}, f32[2,32,128]{2,1,0:T(8,128)S(1)}, u32[]{:S(2)}, u32[]{:S(2)}) %collective-permute-start.4) | collective-permute-done | bytes 32800 | tf_op jit(solution)/shard_map/ppermute | solution.py:491
  35.1 1.4 %shard_map.114 = f32[2,16,16,32]{3,2,1,0:T(8,128)} custom-call(s32[2]{0:T(128)S(1)} %pad_add_fusion.flags.refs_0_, f32[2,32,128]{2,1,0:T(8,128)S(1)} %get-tuple-element.47.keep, f32[2,32,128]{2,1,0:T(8,128)S(1)} %collective-permute-done.4.got), custom_call_target="tpu_custom_call" | custom-call | tf_op jit(solution)/shard_map/pallas_call | solution.py:471
  (1 shorter events, 0.0 us)
Async XLA Ops:
  0.0 2.5 %copy-start.1 = (f32[2,7,7,256]{3,0,2,1:T(2,128)S(1)}, f32[2,7,7,256]{3,0,2,1:T(2,128)}, u32[]{:S(2)}) copy-start(f32[2,7,7,256]{3,0,2,1:T(2,128)} %param.16) | copy-start | bytes 301060
  0.1 2.4 %copy-start.2 = (f32[16,256]{1,0:T(8,128)S(1)}, f32[16,256]{1,0:T(8,128)}, u32[]{:S(2)}) copy-start(f32[16,256]{1,0:T(8,128)} %refs_9_.1) | copy-start | bytes 49156
  0.1 2.4 %copy-start.3 = (f32[256,16]{0,1:T(8,128)S(1)}, f32[256,16]{0,1:T(8,128)}, u32[]{:S(2)}) copy-start(f32[256,16]{0,1:T(8,128)} %param.21) | copy-start | bytes 49156
  1.1 1.4 %copy-start = (f32[2,1024]{1,0:T(2,128)S(1)}, f32[2,1024]{1,0:T(2,128)}, u32[]{:S(2)}) copy-start(f32[2,1024]{1,0:T(2,128)} %refs_20_.1) | copy-start | bytes 24580
  1.1 1.4 %collective-permute-start.1 = (f32[32,128]{1,0:T(8,128)S(1)}, f32[32,128]{1,0:T(8,128)S(1)}, u32[]{:S(2)}, u32[]{:S(2)}) collective-permute-start(f32[32,128]{1,0:T(8,128)S(1)} %get-tuple-element.28.refs_3_.refs_5_), channel_id=1, source_target_pairs={{0,1},{1,0},{2,3},{3,2},{4,5},{5,4},{6,7},{7,6},{8,9},{9,8},{10,11... | collective-permute-start | bytes 49160 | tf_op jit(solution)/shard_map/ppermute | solution.py:491
  1.6 7.1 %collective-permute-start = (f32[32,128]{1,0:T(8,128)S(1)}, f32[32,128]{1,0:T(8,128)S(1)}, u32[]{:S(2)}, u32[]{:S(2)}) collective-permute-start(f32[32,128]{1,0:T(8,128)S(1)} %get-tuple-element.27.refs_1_.refs_2_), channel_id=1, source_target_pairs={{1,2},{2,1},{3,4},{4,3},{5,6},{6,5},{7,8},{8,7},{9,10},{10,9},{11,... | collective-permute-start | bytes 49160 | tf_op jit(solution)/shard_map/ppermute | solution.py:494
  14.6 4.6 %collective-permute-start.3 = (bf16[3,32,128]{2,1,0:T(8,128)(2,1)S(1)}, bf16[3,32,128]{2,1,0:T(8,128)(2,1)S(1)}, u32[]{:S(2)}, u32[]{:S(2)}) collective-permute-start(bf16[3,32,128]{2,1,0:T(8,128)(2,1)S(1)} %get-tuple-element.43), channel_id=1, source_target_pairs={{0,1},{1,0},{2,3},{3,2},{4,5},{5,4},{6,7},{7,6},{8,9},{9,8},{10,11... | collective-permute-start | bytes 73736 | tf_op jit(solution)/shard_map/ppermute | solution.py:491
  18.4 6.4 %collective-permute-start.2 = (bf16[3,32,128]{2,1,0:T(8,128)(2,1)S(1)}, bf16[3,32,128]{2,1,0:T(8,128)(2,1)S(1)}, u32[]{:S(2)}, u32[]{:S(2)}) collective-permute-start(bf16[3,32,128]{2,1,0:T(8,128)(2,1)S(1)} %get-tuple-element.43), channel_id=1, source_target_pairs={{1,2},{2,1},{3,4},{4,3},{5,6},{6,5},{7,8},{8,7},{9,10},{10,9},{11,... | collective-permute-start | bytes 73736 | tf_op jit(solution)/shard_map/ppermute | solution.py:494
  31.3 3.8 %collective-permute-start.4 = (f32[2,32,128]{2,1,0:T(8,128)S(1)}, f32[2,32,128]{2,1,0:T(8,128)S(1)}, u32[]{:S(2)}, u32[]{:S(2)}) collective-permute-start(f32[2,32,128]{2,1,0:T(8,128)S(1)} %get-tuple-element.48), channel_id=1, source_target_pairs={{0,1},{1,0},{2,3},{3,2},{4,5},{5,4},{6,7},{7,6},{8,9},{9,8},{10,11... | collective-permute-start | bytes 98312 | tf_op jit(solution)/shard_map/ppermute | solution.py:491

commit v8 on v7

--- a/solution.py
+++ b/solution.py
@@ -213,22 +213,21 @@
     return dot(jnp.concatenate(hidden, axis=-1), down_w[block])
 
 
-def depthwise(tap_rows, source, pairs, begin, done):
+def depthwise(tap_rows, half, source, pairs, begin, done, group_size=4):
     heights = sorted(pairs)
-    groups = [heights[i : i + 4] for i in range(0, len(heights), 4)]
-    for half in range(2):
-        for group in groups:
-            acc = {h: begin(h, half) for h in group}
-            needed = sorted({i for h in group for i in pairs[h]})
-            for dx in range(TAPS):
-                for i in needed:
-                    x = source(i, half, dx)
-                    for h in group:
-                        if i in pairs[h]:
-                            at = (i - h + HALO) * TAPS + dx
-                            acc[h] = acc[h] + x * tap_rows[half, at : at + 1, :]
-            for h in group:
-                done(h, half, acc[h])
+    groups = [heights[i : i + group_size] for i in range(0, len(heights), group_size)]
+    for group in groups:
+        acc = {h: begin(h) for h in group}
+        needed = sorted({i for h in group for i in pairs[h]})
+        for dx in range(TAPS):
+            for i in needed:
+                x = source(i, dx)
+                for h in group:
+                    if i in pairs[h]:
+                        at = (i - h + HALO) * TAPS + dx
+                        acc[h] = acc[h] + x * tap_rows[half, at : at + 1, :]
+        for h in group:
+            done(h, acc[h])
 
 
 NEAR = range(HALO, OWN + HALO)
@@ -245,7 +244,7 @@
     count = len(NEAR)
     if last:
         (flags, own, inner, mine, inner_terms, temb, weff, by_row, tap_rows, spread, three, in_three, _, gain, up_w, down_w, up_b,
-         partial, kept, shift, patch, centre, normed, *wide) = refs
+         partial, kept, shift, patch, centre, normed, wide) = refs
         turn = flags[0]
         states, state = [], [own[...], inner[...]]
         for t in range(TIMES):
@@ -254,7 +253,7 @@
     else:
         (flags, own, inner, clock, other_clock, time_hbm, up_hbm, down_hbm, gain_hbm, in_w, taps, up_b, out_t,
          partial, kept, temb, weff, by_row, tap_rows, spread, three, in_three, out_three, gain, up_w, down_w,
-         shift, patch, centre, normed, *wide, time_w, sems) = refs
+         shift, patch, centre, normed, wide, time_w, sems) = refs
         turn = flags[0]
         copies = [pltpu.make_async_copy(time_hbm, time_w, sems.at[4])]
         for block in range(2):
@@ -279,8 +278,7 @@
     ones = by_row[0]
     for dy in range(1, TAPS):
         ones = ones + by_row[dy]
-    for ref in wide:
-        clear_sides(ref)
+    clear_sides(wide)
 
     def place(k, j):
         i = j if k == 0 else 2 * OWN - 1 - j
@@ -293,17 +291,21 @@
     for t in range(TIMES):
         kept[t] = after[t][0 : OWN - HALO]
         for half in range(2):
-            wide[2 * t + half][:, PAD : PAD + COLS, :] = after[t][:, :, half * LANES : (half + 1) * LANES]
-    for t in range(TIMES):
-
-        def source(i, half, dx):
-            at = PAD - HALO + dx
-            return wide[2 * t + half][i - HALO, at : at + COLS, :]
-
-        def done(h, half, x):
+            wide[2 * t + half, :, PAD : PAD + COLS, :] = after[t][:, :, half * LANES : (half + 1) * LANES]
+
+    def tapped(half, t, carry):
+        def source(i, dx):
+            low = PAD - HALO + dx
+            return wide[2 * t + half, i - HALO, low : low + COLS, :]
+
+        def done(h, x):
             partial[2 * t + half, h] = x
 
-        depthwise(tap_rows, source, pairs_of(NEAR), lambda h, half: jnp.zeros((COLS, LANES), F32), done)
+        depthwise(tap_rows, half, source, pairs_of(NEAR), lambda h: jnp.zeros((COLS, LANES), F32), done, OWN)
+        return carry
+
+    for half in range(2):
+        lax.fori_loop(0, TIMES, functools.partial(tapped, half), 0)
     if not last:
         copies[3].wait()
         copies[4].wait()
@@ -358,14 +360,18 @@
     stream = []
     for t in range(TIMES):
 
-        def source(i, half, dx):
-            at = PAD - HALO + dx
-            return wide[2 * t + half][i + HALO, at : at + COLS, :]
-
-        def done(h, half, x):
+        def source(half, i, dx):
+            low = PAD - HALO + dx
+            return wide[2 * t + half][i + HALO, low : low + COLS, :]
+
+        def done(half, h, x):
             conv_buf[t][h, :, half * LANES : (half + 1) * LANES] = x
 
-        depthwise(tap_rows, source, pairs_of(EDGE), lambda h, half: partial[2 * t + half, h], done)
+        for half in range(2):
+            depthwise(
+                tap_rows, half, functools.partial(source, half), pairs_of(EDGE), lambda h: partial[2 * t + half, h],
+                functools.partial(done, half),
+            )
         for h in range(OWN):
             low = (t * OWN + h) * COLS
             if h < touched:
@@ -416,7 +422,7 @@
 
 def near(last, up_w, down_w, *args):
     outs = [pltpu.VMEM((2 * TIMES, OWN, COLS, LANES), F32), pltpu.VMEM((TIMES, OWN - HALO, COLS, WIDTH), F32)]
-    scratch = working(len(NEAR), TIMES if last else 1) + [pltpu.VMEM((len(NEAR), WIDE, LANES), F32)] * (2 * TIMES)
+    scratch = working(len(NEAR), TIMES if last else 1) + [pltpu.VMEM((2 * TIMES, len(NEAR), WIDE, LANES), F32)]
     if last:
         specs = [SMEM] + [VMEM] * (len(args) - 1)
     else:

time: 36.7 us -> 35.7 us (0.973)
  Pallas kernels: 26.5 us -> 25.6 us
    pallas_call x2, Pallas kernels: 11.8 us -> 10.9 us  [near(): pl.pallas_call(functools.partial(near_kernel, last), out_shape=outs, in_s...]
  transfers between devices with their start and end apart: 5 -> 5, of which waited for: 2 -> 2; matrix products, arithmetic and copies ran while one was open for 0% -> 0% of each run, Pallas kernels for 32% -> 31%
where the time goes in v8:
time: 35.7 us; the launch traced here: 35.6 us
  Pallas kernels  25.6 us (72%)
  starting transfers between devices  8.77 us (25%)
  waiting for transfers between devices  1.06 us (3%)
    pallas_call x2, Pallas kernels, edge(): pl.pallas_call(functools.partial(edge_kernel, last), out_shape=outs, in_s...  12.2 us
    pallas_call x2, Pallas kernels, near(): pl.pallas_call(functools.partial(near_kernel, last), out_shape=outs, in_s...  10.9 us
    ppermute x3, starting transfers between devices, over_tm(): return lax.ppermute(x, 'tm', beside)  7.29 us
    ppermute x2, starting transfers between devices, over_space(): return lax.ppermute(x, ('space', 'tm'), across)  1.48 us
    pallas_call x1, Pallas kernels, finish(): pl.pallas_call(finish_kernel, out_shape=jax.ShapeDtypeStruct((2, 2 * OWN,...  1.38 us
    ppermute x3, waiting for transfers between devices, over_tm(): return lax.ppermute(x, 'tm', beside)  1.05 us
    pallas_call x1, Pallas kernels, prepare(): pl.pallas_call(prepare_kernel, out_shape=[dense, dense, jax.ShapeDtypeStr...  1 us
  transfers between devices with their start and end apart: 5, of which 2 were waited for; matrix products, arithmetic and copies ran while one was open for 0% of the time, Pallas kernels for 31%

profile of v8, /device:TPU:0, one launch (start us, length us, event | category | flops | bytes accessed | tf_op | source)
XLA Modules:
  0.0 35.6 jit_solution(9601284300612764953)
XLA Ops:
  0.0 0.0 copy-start.1
  0.0 0.1 pad_add_fusion.flags.refs_0_
  0.1 0.0 copy-start.2
  0.1 1.0 %shard_map.109 = (f32[32,128]{1,0:T(8,128)S(1)}, f32[32,128]{1,0:T(8,128)S(1)}, f32[32,128]{1,0:T(8,128)S(1)}) custom-call(s32[2]{0:T(128)S(1)} %pad_add_fusion.flags.refs_0_, s32[2]{0:T(128)} %times.1, f32[2]{0:T(128)} %sizes.1, f32[16,16,32]{2,1,0:T(8,128)} %bitcast.8), custom_call_target="tpu_custom_call" | custom-call | tf_op jit(solution)/shard_map/pallas_call | solution.py:467
  1.1 0.0 copy-start
  1.1 0.5 %collective-permute-start.1 = (f32[32,128]{1,0:T(8,128)S(1)}, f32[32,128]{1,0:T(8,128)S(1)}, u32[]{:S(2)}, u32[]{:S(2)}) collective-permute-start(f32[32,128]{1,0:T(8,128)S(1)} %get-tuple-element.28.refs_3_.refs_5_), channel_id=1, source_target_pairs={{0,1},{1,0},{2,3},{3,2},{4,5},{5,4},{6,7},{7,6},{8,9},{9,8},{10,11... | collective-permute-start | bytes 49160 | tf_op jit(solution)/shard_map/ppermute | solution.py:497
  1.6 0.7 %collective-permute-start = (f32[32,128]{1,0:T(8,128)S(1)}, f32[32,128]{1,0:T(8,128)S(1)}, u32[]{:S(2)}, u32[]{:S(2)}) collective-permute-start(f32[32,128]{1,0:T(8,128)S(1)} %get-tuple-element.27.refs_1_.refs_2_), channel_id=1, source_target_pairs={{1,2},{2,1},{3,4},{4,3},{5,6},{6,5},{7,8},{8,7},{9,10},{10,9},{11,... | collective-permute-start | bytes 49160 | tf_op jit(solution)/shard_map/ppermute | solution.py:500
  2.3 0.2 collective-permute-done.1.refs_4_.refs_6_
  2.5 0.0 copy-done.1
  2.5 0.0 copy-done.2
  2.5 0.0 copy-done.3
  2.5 0.0 copy-done
  2.5 5.8 %shard_map.110 = (f32[6,8,32,128]{3,2,1,0:T(8,128)S(1)}, f32[3,5,32,256]{3,2,1,0:T(8,128)S(1)}, f32[8,256]{1,0:T(8,128)S(1)}, bf16[896,256]{1,0:T(8,128)(2,1)S(1...) custom-call(s32[2]{0:T(128)S(1)} %pad_add_fusion.flags.refs_0_, ...), custom_call_target="tpu_custom_call" | custom-call | tf_op jit(solution)/shard_map/pallas_call | solution.py:436
  8.3 0.0 collective-permute-done.refs_1_
  8.3 5.9 %shard_map.111 = (f32[3,32,128]{2,1,0:T(8,128)S(1)}, bf16[3,32,128]{2,1,0:T(8,128)(2,1)S(1)}) custom-call(s32[2]{0:T(128)S(1)} %pad_add_fusion.flags.refs_0_, f32[32,128]{1,0:T(8,128)S(1)} %collective-permute-done.refs_1_, f32[32,128]{1,0:T(8,128)S(1)} %get-tuple-element.27.refs_1_.refs_2_, f32[32,128]{1,0:T(8,128)S(1)} %get-tuple-element.28.refs_3_.refs_5_, ...), custom_call_target="tpu_custom_call" | custom-call | tf_op jit(solution)/shard_map/pallas_call | solution.py:452
  14.2 3.8 %collective-permute-start.3 = (bf16[3,32,128]{2,1,0:T(8,128)(2,1)S(1)}, bf16[3,32,128]{2,1,0:T(8,128)(2,1)S(1)}, u32[]{:S(2)}, u32[]{:S(2)}) collective-permute-start(bf16[3,32,128]{2,1,0:T(8,128)(2,1)S(1)} %get-tuple-element.43), channel_id=1, source_target_pairs={{0,1},{1,0},{2,3},{3,2},{4,5},{5,4},{6,7},{7,6},{8,9},{9,8},{10,11... | collective-permute-start | bytes 73736 | tf_op jit(solution)/shard_map/ppermute | solution.py:497
  18.0 0.8 %collective-permute-start.2 = (bf16[3,32,128]{2,1,0:T(8,128)(2,1)S(1)}, bf16[3,32,128]{2,1,0:T(8,128)(2,1)S(1)}, u32[]{:S(2)}, u32[]{:S(2)}) collective-permute-start(bf16[3,32,128]{2,1,0:T(8,128)(2,1)S(1)} %get-tuple-element.43), channel_id=1, source_target_pairs={{1,2},{2,1},{3,4},{4,3},{5,6},{6,5},{7,8},{8,7},{9,10},{10,9},{11,... | collective-permute-start | bytes 73736 | tf_op jit(solution)/shard_map/ppermute | solution.py:500
  18.8 0.0 collective-permute-done.3.refs_4_
  18.8 5.1 %shard_map.112 = (f32[6,8,32,128]{3,2,1,0:T(8,128)S(1)}, f32[3,5,32,256]{3,2,1,0:T(8,128)S(1)}) custom-call(s32[2]{0:T(128)S(1)} %pad_add_fusion.flags.refs_0_, f32[32,128]{1,0:T(8,128)S(1)} %get-tuple-element.27.refs_1_.refs_2_, f32[32,128]{1,0:T(8,128)S(1)} %get-tuple-element.29.refs_2_, f32[3,32,128]{2,1,0:T(8,128)S(1)} %get-tuple-element.44.refs_3_.refs_4_, ...), custom_call_target="tpu_custom_call" | custom-call | tf_op jit(solution)/shard_map/pallas_call | solution.py:436
  23.9 0.0 collective-permute-done.2.refs_3_
  23.9 6.4 %shard_map.113 = (f32[2,32,128]{2,1,0:T(8,128)S(1)}, f32[2,32,128]{2,1,0:T(8,128)S(1)}) custom-call(s32[2]{0:T(128)S(1)} %pad_add_fusion.flags.refs_0_, f32[32,128]{1,0:T(8,128)S(1)} %collective-permute-done.refs_1_, f32[32,128]{1,0:T(8,128)S(1)} %get-tuple-element.27.refs_1_.refs_2_, bf16[3,32,128]{2,1,0:T(8,128)(2,1)S(1)} %collective-permute-done.2.refs_3_, ...), custom_call_target="tpu_custom_call" | custom-call | tf_op jit(solution)/shard_map/pallas_call | solution.py:452
  30.4 3.0 %collective-permute-start.4 = (f32[2,32,128]{2,1,0:T(8,128)S(1)}, f32[2,32,128]{2,1,0:T(8,128)S(1)}, u32[]{:S(2)}, u32[]{:S(2)}) collective-permute-start(f32[2,32,128]{2,1,0:T(8,128)S(1)} %get-tuple-element.48), channel_id=1, source_target_pairs={{0,1},{1,0},{2,3},{3,2},{4,5},{5,4},{6,7},{7,6},{8,9},{9,8},{10,11... | collective-permute-start | bytes 98312 | tf_op jit(solution)/shard_map/ppermute | solution.py:497
  33.3 0.9 %collective-permute-done.4.got = f32[2,32,128]{2,1,0:T(8,128)S(1)} collective-permute-done((f32[2,32,128]{2,1,0:T(8,128)S(1)}, f32[2,32,128]{2,1,0:T(8,128)S(1)}, u32[]{:S(2)}, u32[]{:S(2)}) %collective-permute-start.4) | collective-permute-done | bytes 32800 | tf_op jit(solution)/shard_map/ppermute | solution.py:497
  34.2 1.4 %shard_map.114 = f32[2,16,16,32]{3,2,1,0:T(8,128)} custom-call(s32[2]{0:T(128)S(1)} %pad_add_fusion.flags.refs_0_, f32[2,32,128]{2,1,0:T(8,128)S(1)} %get-tuple-element.47.keep, f32[2,32,128]{2,1,0:T(8,128)S(1)} %collective-permute-done.4.got), custom_call_target="tpu_custom_call" | custom-call | tf_op jit(solution)/shard_map/pallas_call | solution.py:477
  (1 shorter events, 0.0 us)
Async XLA Ops:
  0.0 2.5 %copy-start.1 = (f32[2,7,7,256]{3,0,2,1:T(2,128)S(1)}, f32[2,7,7,256]{3,0,2,1:T(2,128)}, u32[]{:S(2)}) copy-start(f32[2,7,7,256]{3,0,2,1:T(2,128)} %param.16) | copy-start | bytes 301060
  0.1 2.4 %copy-start.2 = (f32[16,256]{1,0:T(8,128)S(1)}, f32[16,256]{1,0:T(8,128)}, u32[]{:S(2)}) copy-start(f32[16,256]{1,0:T(8,128)} %refs_9_.1) | copy-start | bytes 49156
  0.1 2.4 %copy-start.3 = (f32[256,16]{0,1:T(8,128)S(1)}, f32[256,16]{0,1:T(8,128)}, u32[]{:S(2)}) copy-start(f32[256,16]{0,1:T(8,128)} %param.21) | copy-start | bytes 49156
  1.1 1.4 %copy-start = (f32[2,1024]{1,0:T(2,128)S(1)}, f32[2,1024]{1,0:T(2,128)}, u32[]{:S(2)}) copy-start(f32[2,1024]{1,0:T(2,128)} %refs_20_.1) | copy-start | bytes 24580
  1.1 1.4 %collective-permute-start.1 = (f32[32,128]{1,0:T(8,128)S(1)}, f32[32,128]{1,0:T(8,128)S(1)}, u32[]{:S(2)}, u32[]{:S(2)}) collective-permute-start(f32[32,128]{1,0:T(8,128)S(1)} %get-tuple-element.28.refs_3_.refs_5_), channel_id=1, source_target_pairs={{0,1},{1,0},{2,3},{3,2},{4,5},{5,4},{6,7},{7,6},{8,9},{9,8},{10,11... | collective-permute-start | bytes 49160 | tf_op jit(solution)/shard_map/ppermute | solution.py:497
  1.6 6.7 %collective-permute-start = (f32[32,128]{1,0:T(8,128)S(1)}, f32[32,128]{1,0:T(8,128)S(1)}, u32[]{:S(2)}, u32[]{:S(2)}) collective-permute-start(f32[32,128]{1,0:T(8,128)S(1)} %get-tuple-element.27.refs_1_.refs_2_), channel_id=1, source_target_pairs={{1,2},{2,1},{3,4},{4,3},{5,6},{6,5},{7,8},{8,7},{9,10},{10,9},{11,... | collective-permute-start | bytes 49160 | tf_op jit(solution)/shard_map/ppermute | solution.py:500
  14.2 4.7 %collective-permute-start.3 = (bf16[3,32,128]{2,1,0:T(8,128)(2,1)S(1)}, bf16[3,32,128]{2,1,0:T(8,128)(2,1)S(1)}, u32[]{:S(2)}, u32[]{:S(2)}) collective-permute-start(bf16[3,32,128]{2,1,0:T(8,128)(2,1)S(1)} %get-tuple-element.43), channel_id=1, source_target_pairs={{0,1},{1,0},{2,3},{3,2},{4,5},{5,4},{6,7},{7,6},{8,9},{9,8},{10,11... | collective-permute-start | bytes 73736 | tf_op jit(solution)/shard_map/ppermute | solution.py:497
  18.0 6.0 %collective-permute-start.2 = (bf16[3,32,128]{2,1,0:T(8,128)(2,1)S(1)}, bf16[3,32,128]{2,1,0:T(8,128)(2,1)S(1)}, u32[]{:S(2)}, u32[]{:S(2)}) collective-permute-start(bf16[3,32,128]{2,1,0:T(8,128)(2,1)S(1)} %get-tuple-element.43), channel_id=1, source_target_pairs={{1,2},{2,1},{3,4},{4,3},{5,6},{6,5},{7,8},{8,7},{9,10},{10,9},{11,... | collective-permute-start | bytes 73736 | tf_op jit(solution)/shard_map/ppermute | solution.py:500
  30.4 3.8 %collective-permute-start.4 = (f32[2,32,128]{2,1,0:T(8,128)S(1)}, f32[2,32,128]{2,1,0:T(8,128)S(1)}, u32[]{:S(2)}, u32[]{:S(2)}) collective-permute-start(f32[2,32,128]{2,1,0:T(8,128)S(1)} %get-tuple-element.48), channel_id=1, source_target_pairs={{0,1},{1,0},{2,3},{3,2},{4,5},{5,4},{6,7},{7,6},{8,9},{9,8},{10,11... | collective-permute-start | bytes 98312 | tf_op jit(solution)/shard_map/ppermute | solution.py:497

commit v9 on v8

--- a/solution.py
+++ b/solution.py
@@ -190,20 +190,35 @@
     return base.reshape(shape), stream.reshape(shape)
 
 
-def first_block(states, place, count, ones, first_time, temb, gain, up_w, up_b, down_w, weff, in_three, *scratch):
-    *scratch, normed = scratch
-    base, stream = block_zero(states, place, count, weff, in_three, *scratch)
-    residual = []
-    for t in range(TIMES):
+def first_block(
+    states, place, count, ones, first_time, temb, gain, up_w, up_b, down_w, weff, in_three, shift, patch, centre, spread, three,
+    normed, copies=(), batched=True,
+):
+    base, stream = block_zero(states, place, count, weff, in_three, shift, patch, centre, spread, three)
+    cells, residual = count * COLS, []
+
+    def prepare_time(t):
         n = min(t, len(states) - 1)
         shown = temb[first_time + t : first_time + t + 1, :]
         lift = [ones[i] * shown for i in range(len(ones))]
         for i in range(count):
-            low = (t * count + i) * COLS
+            low = t * cells + i * COLS
             normed[low : low + COLS, :] = normalise(base[n, i] + lift[min(i, len(ones) - 1)], gain[0:1, :])
         residual.append(stream[n] + shown)
-    out = pointwise(normed[...], 0, up_w, up_b, down_w).reshape(TIMES, count, COLS, WIDTH)
-    return [residual[t] + out[t] for t in range(TIMES)]
+
+    if batched:
+        for t in range(TIMES):
+            prepare_time(t)
+        for copy in copies:
+            copy.wait()
+        out = pointwise(normed[...], 0, up_w, up_b, down_w).reshape(TIMES, count, COLS, WIDTH)
+    for t in range(TIMES):
+        if batched:
+            yield residual[t] + out[t]
+        else:
+            prepare_time(t)
+            single = pointwise(normed[t * cells : (t + 1) * cells, :], 0, up_w, up_b, down_w)
+            yield residual[t] + single.reshape(count, COLS, WIDTH)
 
 
 def pointwise(normed, block, up_w, up_b, down_w):
@@ -246,7 +261,7 @@
         (flags, own, inner, mine, inner_terms, temb, weff, by_row, tap_rows, spread, three, in_three, _, gain, up_w, down_w, up_b,
          partial, kept, shift, patch, centre, normed, wide) = refs
         turn = flags[0]
-        states, state = [], [own[...], inner[...]]
+        copies, states, state = [], [], [own[...], inner[...]]
         for t in range(TIMES):
             state = [state[0] + mine[t], state[1] + inner_terms[t].astype(F32)]
             states.append(state)
@@ -255,11 +270,10 @@
          partial, kept, temb, weff, by_row, tap_rows, spread, three, in_three, out_three, gain, up_w, down_w,
          shift, patch, centre, normed, wide, time_w, sems) = refs
         turn = flags[0]
-        copies = [pltpu.make_async_copy(time_hbm, time_w, sems.at[4])]
+        copies = [pltpu.make_async_copy(time_hbm, time_w, sems.at[4]), pltpu.make_async_copy(gain_hbm, gain, sems.at[5])]
         for block in range(2):
             copies.append(pltpu.make_async_copy(up_hbm.at[block], up_w.at[block], sems.at[2 * block]))
             copies.append(pltpu.make_async_copy(down_hbm.at[block], down_w.at[block], sems.at[2 * block + 1]))
-        copies.append(pltpu.make_async_copy(gain_hbm, gain, sems.at[5]))
         for copy in copies:
             copy.start()
         make_weff(turn, in_w, taps, weff)
@@ -273,8 +287,6 @@
         temb[...] = embed(turn, clock, other_clock, time_w)
         states = [[own[...], inner[...]]]
         copies[1].wait()
-        copies[2].wait()
-        copies[5].wait()
     ones = by_row[0]
     for dy in range(1, TAPS):
         ones = ones + by_row[dy]
@@ -284,14 +296,14 @@
         i = j if k == 0 else 2 * OWN - 1 - j
         return i if i < count + REACH else None
 
-    after = first_block(
+    found = first_block(
         states, place, count, [ones], first_time, temb, gain, up_w, up_b, down_w, weff, in_three,
-        shift, patch, centre, spread, three, normed,
+        shift, patch, centre, spread, three, normed, copies[2:4],
     )
-    for t in range(TIMES):
-        kept[t] = after[t][0 : OWN - HALO]
+    for t, after in enumerate(found):
+        kept[t] = after[0 : OWN - HALO]
         for half in range(2):
-            wide[2 * t + half, :, PAD : PAD + COLS, :] = after[t][:, :, half * LANES : (half + 1) * LANES]
+            wide[2 * t + half, :, PAD : PAD + COLS, :] = after[:, :, half * LANES : (half + 1) * LANES]
 
     def tapped(half, t, carry):
         def source(i, dx):
@@ -304,11 +316,10 @@
         depthwise(tap_rows, half, source, pairs_of(NEAR), lambda h: jnp.zeros((COLS, LANES), F32), done, OWN)
         return carry
 
-    for half in range(2):
-        lax.fori_loop(0, TIMES, functools.partial(tapped, half), 0)
+    lax.fori_loop(0, TIMES, lambda t, carry: tapped(1, t, tapped(0, t, carry)), 0)
     if not last:
-        copies[3].wait()
         copies[4].wait()
+        copies[5].wait()
 
 
 def edge_kernel(last, *refs):
@@ -347,18 +358,17 @@
     for t in range(TIMES if last else 0):
         state = [state[0] + outer_terms[t].astype(F32), state[1] + mine[t]]
         states.append(state)
-    after = first_block(
+    found = first_block(
         states if last else [state], place, count, ones, first_time, temb, gain, up_w, up_b, down_w, weff, in_three,
         shift, patch, centre, spread, three, normed,
     )
-    for t in range(TIMES):
+    touched = len(pairs_of(EDGE))
+    terms = []
+    for t, after in enumerate(found):
         for half in range(2):
             lanes = slice(half * LANES, (half + 1) * LANES)
-            wide[2 * t + half][0:HALO, PAD : PAD + COLS, :] = after[t][0:HALO, :, lanes] * inside
-            wide[2 * t + half][HALO:, PAD : PAD + COLS, :] = after[t][HALO:, :, lanes]
-    touched = len(pairs_of(EDGE))
-    stream = []
-    for t in range(TIMES):
+            wide[2 * t + half][0:HALO, PAD : PAD + COLS, :] = after[0:HALO, :, lanes] * inside
+            wide[2 * t + half][HALO:, PAD : PAD + COLS, :] = after[HALO:, :, lanes]
 
         def source(half, i, dx):
             low = PAD - HALO + dx
@@ -372,22 +382,21 @@
                 tap_rows, half, functools.partial(source, half), pairs_of(EDGE), lambda h: partial[2 * t + half, h],
                 functools.partial(done, half),
             )
+        first = t * OWN * COLS
         for h in range(OWN):
-            low = (t * OWN + h) * COLS
+            low = first + h * COLS
             if h < touched:
                 conv = conv_buf[t][h]
             else:
                 conv = jnp.concatenate([partial[2 * t + half, h] for half in range(2)], axis=-1)
             second_normed[low : low + COLS, :] = normalise(conv, gain[1:2, :])
-        stream += [after[t][HALO:].reshape(HALO * COLS, WIDTH), kept[t].reshape((OWN - HALO) * COLS, WIDTH)]
-    out = pointwise(second_normed[...], 1, up_w, up_b, down_w)
-    hi, lo = split(jnp.concatenate(stream, axis=0) + out)
-    drifts = dot_nt(jnp.concatenate([hi, lo, hi], axis=-1), out_three[...]).reshape(TIMES, OWN, COLS, LANES)
-    terms = []
-    for t in range(TIMES):
-        dense = drifts[t, 0]
+        stream = [after[HALO:].reshape(HALO * COLS, WIDTH), kept[t].reshape((OWN - HALO) * COLS, WIDTH)]
+        out = pointwise(second_normed[first : first + OWN * COLS, :], 1, up_w, up_b, down_w)
+        hi, lo = split(jnp.concatenate(stream, axis=0) + out)
+        drift = dot_nt(jnp.concatenate([hi, lo, hi], axis=-1), out_three[...]).reshape(OWN, COLS, LANES)
+        dense = drift[0]
         for j in range(1, OWN):
-            dense = jnp.where(group == j, drifts[t, j], dense)
+            dense = jnp.where(group == j, drift[j], dense)
         terms.append(dense * sizes[first_time + t])
     if last:
         n0 = states[0][1]

time: 35.7 us -> 35.3 us (0.989)
  Pallas kernels: 25.6 us -> 25.1 us
where the time goes in v9:
time: 35.3 us; the launch traced here: 35.1 us
  Pallas kernels  25.1 us (71%)
  starting transfers between devices  8.77 us (25%)
  waiting for transfers between devices  1.06 us (3%)
    pallas_call x2, Pallas kernels, edge(): pl.pallas_call(functools.partial(edge_kernel, last), out_shape=outs, in_s...  12 us
    pallas_call x2, Pallas kernels, near(): pl.pallas_call(functools.partial(near_kernel, last), out_shape=outs, in_s...  10.8 us
    ppermute x3, starting transfers between devices, over_tm(): return lax.ppermute(x, 'tm', beside)  7.29 us
    ppermute x2, starting transfers between devices, over_space(): return lax.ppermute(x, ('space', 'tm'), across)  1.48 us
    pallas_call x1, Pallas kernels, finish(): pl.pallas_call(finish_kernel, out_shape=jax.ShapeDtypeStruct((2, 2 * OWN,...  1.38 us
    ppermute x3, waiting for transfers between devices, over_tm(): return lax.ppermute(x, 'tm', beside)  1.05 us
    pallas_call x1, Pallas kernels, prepare(): pl.pallas_call(prepare_kernel, out_shape=[dense, dense, jax.ShapeDtypeStr...  1 us
  transfers between devices with their start and end apart: 5, of which 2 were waited for; matrix products, arithmetic and copies ran while one was open for 0% of the time, Pallas kernels for 31%

profile of v9, /device:TPU:0, one launch (start us, length us, event | category | flops | bytes accessed | tf_op | source)
XLA Modules:
  0.0 35.1 jit_solution(6840999257910077694)
XLA Ops:
  0.0 0.0 copy-start.1
  0.0 0.1 pad_add_fusion.flags.refs_0_
  0.1 0.0 copy-start.2
  0.1 1.0 %shard_map.109 = (f32[32,128]{1,0:T(8,128)S(1)}, f32[32,128]{1,0:T(8,128)S(1)}, f32[32,128]{1,0:T(8,128)S(1)}) custom-call(s32[2]{0:T(128)S(1)} %pad_add_fusion.flags.refs_0_, s32[2]{0:T(128)} %times.1, f32[2]{0:T(128)} %sizes.1, f32[16,16,32]{2,1,0:T(8,128)} %bitcast.8), custom_call_target="tpu_custom_call" | custom-call | tf_op jit(solution)/shard_map/pallas_call | solution.py:476
  1.1 0.0 copy-start
  1.1 0.5 %collective-permute-start.1 = (f32[32,128]{1,0:T(8,128)S(1)}, f32[32,128]{1,0:T(8,128)S(1)}, u32[]{:S(2)}, u32[]{:S(2)}) collective-permute-start(f32[32,128]{1,0:T(8,128)S(1)} %get-tuple-element.28.refs_3_.refs_5_), channel_id=1, source_target_pairs={{0,1},{1,0},{2,3},{3,2},{4,5},{5,4},{6,7},{7,6},{8,9},{9,8},{10,11... | collective-permute-start | bytes 49160 | tf_op jit(solution)/shard_map/ppermute | solution.py:506
  1.6 0.7 %collective-permute-start = (f32[32,128]{1,0:T(8,128)S(1)}, f32[32,128]{1,0:T(8,128)S(1)}, u32[]{:S(2)}, u32[]{:S(2)}) collective-permute-start(f32[32,128]{1,0:T(8,128)S(1)} %get-tuple-element.27.refs_1_.refs_2_), channel_id=1, source_target_pairs={{1,2},{2,1},{3,4},{4,3},{5,6},{6,5},{7,8},{8,7},{9,10},{10,9},{11,... | collective-permute-start | bytes 49160 | tf_op jit(solution)/shard_map/ppermute | solution.py:509
  2.3 0.2 collective-permute-done.1.refs_4_.refs_6_
  2.5 0.0 copy-done.1
  2.5 0.0 copy-done.2
  2.5 0.0 copy-done.3
  2.5 0.0 copy-done
  2.5 5.8 %shard_map.110 = (f32[6,8,32,128]{3,2,1,0:T(8,128)S(1)}, f32[3,5,32,256]{3,2,1,0:T(8,128)S(1)}, f32[8,256]{1,0:T(8,128)S(1)}, bf16[896,256]{1,0:T(8,128)(2,1)S(1...) custom-call(s32[2]{0:T(128)S(1)} %pad_add_fusion.flags.refs_0_, ...), custom_call_target="tpu_custom_call" | custom-call | tf_op jit(solution)/shard_map/pallas_call | solution.py:445
  8.2 0.0 collective-permute-done.refs_1_
  8.2 5.7 %shard_map.111 = (f32[3,32,128]{2,1,0:T(8,128)S(1)}, bf16[3,32,128]{2,1,0:T(8,128)(2,1)S(1)}) custom-call(s32[2]{0:T(128)S(1)} %pad_add_fusion.flags.refs_0_, f32[32,128]{1,0:T(8,128)S(1)} %collective-permute-done.refs_1_, f32[32,128]{1,0:T(8,128)S(1)} %get-tuple-element.27.refs_1_.refs_2_, f32[32,128]{1,0:T(8,128)S(1)} %get-tuple-element.28.refs_3_.refs_5_, ...), custom_call_target="tpu_custom_call" | custom-call | tf_op jit(solution)/shard_map/pallas_call | solution.py:461
  13.9 3.8 %collective-permute-start.3 = (bf16[3,32,128]{2,1,0:T(8,128)(2,1)S(1)}, bf16[3,32,128]{2,1,0:T(8,128)(2,1)S(1)}, u32[]{:S(2)}, u32[]{:S(2)}) collective-permute-start(bf16[3,32,128]{2,1,0:T(8,128)(2,1)S(1)} %get-tuple-element.43), channel_id=1, source_target_pairs={{0,1},{1,0},{2,3},{3,2},{4,5},{5,4},{6,7},{7,6},{8,9},{9,8},{10,11... | collective-permute-start | bytes 73736 | tf_op jit(solution)/shard_map/ppermute | solution.py:506
  17.7 0.8 %collective-permute-start.2 = (bf16[3,32,128]{2,1,0:T(8,128)(2,1)S(1)}, bf16[3,32,128]{2,1,0:T(8,128)(2,1)S(1)}, u32[]{:S(2)}, u32[]{:S(2)}) collective-permute-start(bf16[3,32,128]{2,1,0:T(8,128)(2,1)S(1)} %get-tuple-element.43), channel_id=1, source_target_pairs={{1,2},{2,1},{3,4},{4,3},{5,6},{6,5},{7,8},{8,7},{9,10},{10,9},{11,... | collective-permute-start | bytes 73736 | tf_op jit(solution)/shard_map/ppermute | solution.py:509
  18.6 0.0 collective-permute-done.3.refs_4_
  18.6 5.1 %shard_map.112 = (f32[6,8,32,128]{3,2,1,0:T(8,128)S(1)}, f32[3,5,32,256]{3,2,1,0:T(8,128)S(1)}) custom-call(s32[2]{0:T(128)S(1)} %pad_add_fusion.flags.refs_0_, f32[32,128]{1,0:T(8,128)S(1)} %get-tuple-element.27.refs_1_.refs_2_, f32[32,128]{1,0:T(8,128)S(1)} %get-tuple-element.29.refs_2_, f32[3,32,128]{2,1,0:T(8,128)S(1)} %get-tuple-element.44.refs_3_.refs_4_, ...), custom_call_target="tpu_custom_call" | custom-call | tf_op jit(solution)/shard_map/pallas_call | solution.py:445
  23.6 0.0 collective-permute-done.2.refs_3_
  23.7 6.3 %shard_map.113 = (f32[2,32,128]{2,1,0:T(8,128)S(1)}, f32[2,32,128]{2,1,0:T(8,128)S(1)}) custom-call(s32[2]{0:T(128)S(1)} %pad_add_fusion.flags.refs_0_, f32[32,128]{1,0:T(8,128)S(1)} %collective-permute-done.refs_1_, f32[32,128]{1,0:T(8,128)S(1)} %get-tuple-element.27.refs_1_.refs_2_, bf16[3,32,128]{2,1,0:T(8,128)(2,1)S(1)} %collective-permute-done.2.refs_3_, ...), custom_call_target="tpu_custom_call" | custom-call | tf_op jit(solution)/shard_map/pallas_call | solution.py:461
  29.9 3.0 %collective-permute-start.4 = (f32[2,32,128]{2,1,0:T(8,128)S(1)}, f32[2,32,128]{2,1,0:T(8,128)S(1)}, u32[]{:S(2)}, u32[]{:S(2)}) collective-permute-start(f32[2,32,128]{2,1,0:T(8,128)S(1)} %get-tuple-element.48), channel_id=1, source_target_pairs={{0,1},{1,0},{2,3},{3,2},{4,5},{5,4},{6,7},{7,6},{8,9},{9,8},{10,11... | collective-permute-start | bytes 98312 | tf_op jit(solution)/shard_map/ppermute | solution.py:506
  32.9 0.9 %collective-permute-done.4.got = f32[2,32,128]{2,1,0:T(8,128)S(1)} collective-permute-done((f32[2,32,128]{2,1,0:T(8,128)S(1)}, f32[2,32,128]{2,1,0:T(8,128)S(1)}, u32[]{:S(2)}, u32[]{:S(2)}) %collective-permute-start.4) | collective-permute-done | bytes 32800 | tf_op jit(solution)/shard_map/ppermute | solution.py:506
  33.8 1.4 %shard_map.114 = f32[2,16,16,32]{3,2,1,0:T(8,128)} custom-call(s32[2]{0:T(128)S(1)} %pad_add_fusion.flags.refs_0_, f32[2,32,128]{2,1,0:T(8,128)S(1)} %get-tuple-element.47.keep, f32[2,32,128]{2,1,0:T(8,128)S(1)} %collective-permute-done.4.got), custom_call_target="tpu_custom_call" | custom-call | tf_op jit(solution)/shard_map/pallas_call | solution.py:486
  (1 shorter events, 0.0 us)
Async XLA Ops:
  0.0 2.5 %copy-start.1 = (f32[2,7,7,256]{3,0,2,1:T(2,128)S(1)}, f32[2,7,7,256]{3,0,2,1:T(2,128)}, u32[]{:S(2)}) copy-start(f32[2,7,7,256]{3,0,2,1:T(2,128)} %param.16) | copy-start | bytes 301060
  0.1 2.4 %copy-start.2 = (f32[16,256]{1,0:T(8,128)S(1)}, f32[16,256]{1,0:T(8,128)}, u32[]{:S(2)}) copy-start(f32[16,256]{1,0:T(8,128)} %refs_9_.1) | copy-start | bytes 49156
  0.1 2.4 %copy-start.3 = (f32[256,16]{0,1:T(8,128)S(1)}, f32[256,16]{0,1:T(8,128)}, u32[]{:S(2)}) copy-start(f32[256,16]{0,1:T(8,128)} %param.21) | copy-start | bytes 49156
  1.1 1.4 %copy-start = (f32[2,1024]{1,0:T(2,128)S(1)}, f32[2,1024]{1,0:T(2,128)}, u32[]{:S(2)}) copy-start(f32[2,1024]{1,0:T(2,128)} %refs_20_.1) | copy-start | bytes 24580
  1.1 1.4 %collective-permute-start.1 = (f32[32,128]{1,0:T(8,128)S(1)}, f32[32,128]{1,0:T(8,128)S(1)}, u32[]{:S(2)}, u32[]{:S(2)}) collective-permute-start(f32[32,128]{1,0:T(8,128)S(1)} %get-tuple-element.28.refs_3_.refs_5_), channel_id=1, source_target_pairs={{0,1},{1,0},{2,3},{3,2},{4,5},{5,4},{6,7},{7,6},{8,9},{9,8},{10,11... | collective-permute-start | bytes 49160 | tf_op jit(solution)/shard_map/ppermute | solution.py:506
  1.6 6.6 %collective-permute-start = (f32[32,128]{1,0:T(8,128)S(1)}, f32[32,128]{1,0:T(8,128)S(1)}, u32[]{:S(2)}, u32[]{:S(2)}) collective-permute-start(f32[32,128]{1,0:T(8,128)S(1)} %get-tuple-element.27.refs_1_.refs_2_), channel_id=1, source_target_pairs={{1,2},{2,1},{3,4},{4,3},{5,6},{6,5},{7,8},{8,7},{9,10},{10,9},{11,... | collective-permute-start | bytes 49160 | tf_op jit(solution)/shard_map/ppermute | solution.py:509
  13.9 4.6 %collective-permute-start.3 = (bf16[3,32,128]{2,1,0:T(8,128)(2,1)S(1)}, bf16[3,32,128]{2,1,0:T(8,128)(2,1)S(1)}, u32[]{:S(2)}, u32[]{:S(2)}) collective-permute-start(bf16[3,32,128]{2,1,0:T(8,128)(2,1)S(1)} %get-tuple-element.43), channel_id=1, source_target_pairs={{0,1},{1,0},{2,3},{3,2},{4,5},{5,4},{6,7},{7,6},{8,9},{9,8},{10,11... | collective-permute-start | bytes 73736 | tf_op jit(solution)/shard_map/ppermute | solution.py:506
  17.7 5.9 %collective-permute-start.2 = (bf16[3,32,128]{2,1,0:T(8,128)(2,1)S(1)}, bf16[3,32,128]{2,1,0:T(8,128)(2,1)S(1)}, u32[]{:S(2)}, u32[]{:S(2)}) collective-permute-start(bf16[3,32,128]{2,1,0:T(8,128)(2,1)S(1)} %get-tuple-element.43), channel_id=1, source_target_pairs={{1,2},{2,1},{3,4},{4,3},{5,6},{6,5},{7,8},{8,7},{9,10},{10,9},{11,... | collective-permute-start | bytes 73736 | tf_op jit(solution)/shard_map/ppermute | solution.py:509
  29.9 3.8 %collective-permute-start.4 = (f32[2,32,128]{2,1,0:T(8,128)S(1)}, f32[2,32,128]{2,1,0:T(8,128)S(1)}, u32[]{:S(2)}, u32[]{:S(2)}) collective-permute-start(f32[2,32,128]{2,1,0:T(8,128)S(1)} %get-tuple-element.48), channel_id=1, source_target_pairs={{0,1},{1,0},{2,3},{3,2},{4,5},{5,4},{6,7},{7,6},{8,9},{9,8},{10,11... | collective-permute-start | bytes 98312 | tf_op jit(solution)/shard_map/ppermute | solution.py:506

commit v10 on v9

--- a/solution.py
+++ b/solution.py
@@ -81,8 +81,9 @@
     clock[...] = filled
 
 
-def finish_kernel(flags, keep, got, out):
+def finish_kernel(flags, keep, got, out_hbm, out, sems):
     turned = flags[0] == 1
+    copies = [pltpu.make_async_copy(out.at[t], out_hbm.at[t], sems.at[t]) for t in range(2)]
     for t in range(2):
         top = jnp.where(turned, got[t], keep[t])
         bottom = jnp.where(turned, keep[t], got[t])
@@ -90,6 +91,9 @@
         flipped = bottom.T.reshape(OWN, CHAN, COLS)
         for h in range(OWN):
             out[t, 2 * OWN - 1 - h] = flipped[h]
+        copies[t].start()
+    for copy in copies:
+        copy.wait()
 
 
 def pinned(x):
@@ -487,7 +491,8 @@
         finish_kernel,
         out_shape=jax.ShapeDtypeStruct((2, 2 * OWN, CHAN, COLS), F32),
         in_specs=[SMEM, VMEM, VMEM],
-        out_specs=VMEM,
+        out_specs=HBM,
+        scratch_shapes=[pltpu.VMEM((2, 2 * OWN, CHAN, COLS), F32), pltpu.SemaphoreType.DMA((2,))],
         compiler_params=SMALL,
     )(flags, keep, got)
 

time: 35.3 us -> 35.5 us (level)
  no operation moved by 1% of the time
where the time goes in v10:
time: 35.5 us; the launch traced here: 35.3 us
  Pallas kernels  25.1 us (71%)
  starting transfers between devices  8.77 us (25%)
  waiting for transfers between devices  1.06 us (3%)
    pallas_call x2, Pallas kernels, edge(): pl.pallas_call(functools.partial(edge_kernel, last), out_shape=outs, in_s...  12 us
    pallas_call x2, Pallas kernels, near(): pl.pallas_call(functools.partial(near_kernel, last), out_shape=outs, in_s...  10.8 us
    ppermute x3, starting transfers between devices, over_tm(): return lax.ppermute(x, 'tm', beside)  7.29 us
    ppermute x2, starting transfers between devices, over_space(): return lax.ppermute(x, ('space', 'tm'), across)  1.48 us
    pallas_call x1, Pallas kernels, finish(): pl.pallas_call(finish_kernel, out_shape=jax.ShapeDtypeStruct((2, 2 * OWN,...  1.36 us
    ppermute x3, waiting for transfers between devices, over_tm(): return lax.ppermute(x, 'tm', beside)  1.05 us
    pallas_call x1, Pallas kernels, prepare(): pl.pallas_call(prepare_kernel, out_shape=[dense, dense, jax.ShapeDtypeStr...  1 us
  transfers between devices with their start and end apart: 5, of which 2 were waited for; matrix products, arithmetic and copies ran while one was open for 0% of the time, Pallas kernels for 31%

profile of v10, /device:TPU:0, one launch (start us, length us, event | category | flops | bytes accessed | tf_op | source)
XLA Modules:
  0.0 35.3 jit_solution(15492217831280669063)
XLA Ops:
  0.0 0.0 copy-start.1
  0.0 0.1 pad_add_fusion.flags.refs_0_
  0.1 0.0 copy-start.2
  0.1 1.0 %shard_map.109 = (f32[32,128]{1,0:T(8,128)S(1)}, f32[32,128]{1,0:T(8,128)S(1)}, f32[32,128]{1,0:T(8,128)S(1)}) custom-call(s32[2]{0:T(128)S(1)} %pad_add_fusion.flags.refs_0_, s32[2]{0:T(128)} %times.1, f32[2]{0:T(128)} %sizes.1, f32[16,16,32]{2,1,0:T(8,128)} %bitcast.8), custom_call_target="tpu_custom_call" | custom-call | tf_op jit(solution)/shard_map/pallas_call | solution.py:480
  1.1 0.0 copy-start
  1.1 0.5 %collective-permute-start.1 = (f32[32,128]{1,0:T(8,128)S(1)}, f32[32,128]{1,0:T(8,128)S(1)}, u32[]{:S(2)}, u32[]{:S(2)}) collective-permute-start(f32[32,128]{1,0:T(8,128)S(1)} %get-tuple-element.28.refs_3_.refs_5_), channel_id=1, source_target_pairs={{0,1},{1,0},{2,3},{3,2},{4,5},{5,4},{6,7},{7,6},{8,9},{9,8},{10,11... | collective-permute-start | bytes 49160 | tf_op jit(solution)/shard_map/ppermute | solution.py:511
  1.6 0.7 %collective-permute-start = (f32[32,128]{1,0:T(8,128)S(1)}, f32[32,128]{1,0:T(8,128)S(1)}, u32[]{:S(2)}, u32[]{:S(2)}) collective-permute-start(f32[32,128]{1,0:T(8,128)S(1)} %get-tuple-element.27.refs_1_.refs_2_), channel_id=1, source_target_pairs={{1,2},{2,1},{3,4},{4,3},{5,6},{6,5},{7,8},{8,7},{9,10},{10,9},{11,... | collective-permute-start | bytes 49160 | tf_op jit(solution)/shard_map/ppermute | solution.py:514
  2.3 0.2 collective-permute-done.1.refs_4_.refs_6_
  2.5 0.0 copy-done.1
  2.5 0.0 copy-done.2
  2.5 0.0 copy-done.3
  2.5 0.0 copy-done
  2.5 5.8 %shard_map.110 = (f32[6,8,32,128]{3,2,1,0:T(8,128)S(1)}, f32[3,5,32,256]{3,2,1,0:T(8,128)S(1)}, f32[8,256]{1,0:T(8,128)S(1)}, bf16[896,256]{1,0:T(8,128)(2,1)S(1...) custom-call(s32[2]{0:T(128)S(1)} %pad_add_fusion.flags.refs_0_, ...), custom_call_target="tpu_custom_call" | custom-call | tf_op jit(solution)/shard_map/pallas_call | solution.py:449
  8.2 0.0 collective-permute-done.refs_1_
  8.2 5.7 %shard_map.111 = (f32[3,32,128]{2,1,0:T(8,128)S(1)}, bf16[3,32,128]{2,1,0:T(8,128)(2,1)S(1)}) custom-call(s32[2]{0:T(128)S(1)} %pad_add_fusion.flags.refs_0_, f32[32,128]{1,0:T(8,128)S(1)} %collective-permute-done.refs_1_, f32[32,128]{1,0:T(8,128)S(1)} %get-tuple-element.27.refs_1_.refs_2_, f32[32,128]{1,0:T(8,128)S(1)} %get-tuple-element.28.refs_3_.refs_5_, ...), custom_call_target="tpu_custom_call" | custom-call | tf_op jit(solution)/shard_map/pallas_call | solution.py:465
  13.9 3.8 %collective-permute-start.3 = (bf16[3,32,128]{2,1,0:T(8,128)(2,1)S(1)}, bf16[3,32,128]{2,1,0:T(8,128)(2,1)S(1)}, u32[]{:S(2)}, u32[]{:S(2)}) collective-permute-start(bf16[3,32,128]{2,1,0:T(8,128)(2,1)S(1)} %get-tuple-element.43), channel_id=1, source_target_pairs={{0,1},{1,0},{2,3},{3,2},{4,5},{5,4},{6,7},{7,6},{8,9},{9,8},{10,11... | collective-permute-start | bytes 73736 | tf_op jit(solution)/shard_map/ppermute | solution.py:511
  17.7 0.8 %collective-permute-start.2 = (bf16[3,32,128]{2,1,0:T(8,128)(2,1)S(1)}, bf16[3,32,128]{2,1,0:T(8,128)(2,1)S(1)}, u32[]{:S(2)}, u32[]{:S(2)}) collective-permute-start(bf16[3,32,128]{2,1,0:T(8,128)(2,1)S(1)} %get-tuple-element.43), channel_id=1, source_target_pairs={{1,2},{2,1},{3,4},{4,3},{5,6},{6,5},{7,8},{8,7},{9,10},{10,9},{11,... | collective-permute-start | bytes 73736 | tf_op jit(solution)/shard_map/ppermute | solution.py:514
  18.6 0.0 collective-permute-done.3.refs_4_
  18.6 5.1 %shard_map.112 = (f32[6,8,32,128]{3,2,1,0:T(8,128)S(1)}, f32[3,5,32,256]{3,2,1,0:T(8,128)S(1)}) custom-call(s32[2]{0:T(128)S(1)} %pad_add_fusion.flags.refs_0_, f32[32,128]{1,0:T(8,128)S(1)} %get-tuple-element.27.refs_1_.refs_2_, f32[32,128]{1,0:T(8,128)S(1)} %get-tuple-element.29.refs_2_, f32[3,32,128]{2,1,0:T(8,128)S(1)} %get-tuple-element.44.refs_3_.refs_4_, ...), custom_call_target="tpu_custom_call" | custom-call | tf_op jit(solution)/shard_map/pallas_call | solution.py:449
  23.6 0.0 collective-permute-done.2.refs_3_
  23.7 6.3 %shard_map.113 = (f32[2,32,128]{2,1,0:T(8,128)S(1)}, f32[2,32,128]{2,1,0:T(8,128)S(1)}) custom-call(s32[2]{0:T(128)S(1)} %pad_add_fusion.flags.refs_0_, f32[32,128]{1,0:T(8,128)S(1)} %collective-permute-done.refs_1_, f32[32,128]{1,0:T(8,128)S(1)} %get-tuple-element.27.refs_1_.refs_2_, bf16[3,32,128]{2,1,0:T(8,128)(2,1)S(1)} %collective-permute-done.2.refs_3_, ...), custom_call_target="tpu_custom_call" | custom-call | tf_op jit(solution)/shard_map/pallas_call | solution.py:465
  29.9 3.0 %collective-permute-start.4 = (f32[2,32,128]{2,1,0:T(8,128)S(1)}, f32[2,32,128]{2,1,0:T(8,128)S(1)}, u32[]{:S(2)}, u32[]{:S(2)}) collective-permute-start(f32[2,32,128]{2,1,0:T(8,128)S(1)} %get-tuple-element.48), channel_id=1, source_target_pairs={{0,1},{1,0},{2,3},{3,2},{4,5},{5,4},{6,7},{7,6},{8,9},{9,8},{10,11... | collective-permute-start | bytes 98312 | tf_op jit(solution)/shard_map/ppermute | solution.py:511
  32.9 0.9 %collective-permute-done.4.got = f32[2,32,128]{2,1,0:T(8,128)S(1)} collective-permute-done((f32[2,32,128]{2,1,0:T(8,128)S(1)}, f32[2,32,128]{2,1,0:T(8,128)S(1)}, u32[]{:S(2)}, u32[]{:S(2)}) %collective-permute-start.4) | collective-permute-done | bytes 32800 | tf_op jit(solution)/shard_map/ppermute | solution.py:511
  33.8 1.4 %shard_map.114 = f32[2,16,16,32]{3,2,1,0:T(8,128)} custom-call(s32[2]{0:T(128)S(1)} %pad_add_fusion.flags.refs_0_, f32[2,32,128]{2,1,0:T(8,128)S(1)} %get-tuple-element.47.keep, f32[2,32,128]{2,1,0:T(8,128)S(1)} %collective-permute-done.4.got), custom_call_target="tpu_custom_call" | custom-call | tf_op jit(solution)/shard_map/pallas_call | solution.py:490
  (1 shorter events, 0.0 us)
Async XLA Ops:
  0.0 2.5 %copy-start.1 = (f32[2,7,7,256]{3,0,2,1:T(2,128)S(1)}, f32[2,7,7,256]{3,0,2,1:T(2,128)}, u32[]{:S(2)}) copy-start(f32[2,7,7,256]{3,0,2,1:T(2,128)} %param.16) | copy-start | bytes 301060
  0.1 2.4 %copy-start.2 = (f32[16,256]{1,0:T(8,128)S(1)}, f32[16,256]{1,0:T(8,128)}, u32[]{:S(2)}) copy-start(f32[16,256]{1,0:T(8,128)} %refs_9_.1) | copy-start | bytes 49156
  0.1 2.4 %copy-start.3 = (f32[256,16]{0,1:T(8,128)S(1)}, f32[256,16]{0,1:T(8,128)}, u32[]{:S(2)}) copy-start(f32[256,16]{0,1:T(8,128)} %param.21) | copy-start | bytes 49156
  1.1 1.4 %copy-start = (f32[2,1024]{1,0:T(2,128)S(1)}, f32[2,1024]{1,0:T(2,128)}, u32[]{:S(2)}) copy-start(f32[2,1024]{1,0:T(2,128)} %refs_20_.1) | copy-start | bytes 24580
  1.1 1.4 %collective-permute-start.1 = (f32[32,128]{1,0:T(8,128)S(1)}, f32[32,128]{1,0:T(8,128)S(1)}, u32[]{:S(2)}, u32[]{:S(2)}) collective-permute-start(f32[32,128]{1,0:T(8,128)S(1)} %get-tuple-element.28.refs_3_.refs_5_), channel_id=1, source_target_pairs={{0,1},{1,0},{2,3},{3,2},{4,5},{5,4},{6,7},{7,6},{8,9},{9,8},{10,11... | collective-permute-start | bytes 49160 | tf_op jit(solution)/shard_map/ppermute | solution.py:511
  1.6 6.6 %collective-permute-start = (f32[32,128]{1,0:T(8,128)S(1)}, f32[32,128]{1,0:T(8,128)S(1)}, u32[]{:S(2)}, u32[]{:S(2)}) collective-permute-start(f32[32,128]{1,0:T(8,128)S(1)} %get-tuple-element.27.refs_1_.refs_2_), channel_id=1, source_target_pairs={{1,2},{2,1},{3,4},{4,3},{5,6},{6,5},{7,8},{8,7},{9,10},{10,9},{11,... | collective-permute-start | bytes 49160 | tf_op jit(solution)/shard_map/ppermute | solution.py:514
  13.9 4.6 %collective-permute-start.3 = (bf16[3,32,128]{2,1,0:T(8,128)(2,1)S(1)}, bf16[3,32,128]{2,1,0:T(8,128)(2,1)S(1)}, u32[]{:S(2)}, u32[]{:S(2)}) collective-permute-start(bf16[3,32,128]{2,1,0:T(8,128)(2,1)S(1)} %get-tuple-element.43), channel_id=1, source_target_pairs={{0,1},{1,0},{2,3},{3,2},{4,5},{5,4},{6,7},{7,6},{8,9},{9,8},{10,11... | collective-permute-start | bytes 73736 | tf_op jit(solution)/shard_map/ppermute | solution.py:511
  17.7 5.9 %collective-permute-start.2 = (bf16[3,32,128]{2,1,0:T(8,128)(2,1)S(1)}, bf16[3,32,128]{2,1,0:T(8,128)(2,1)S(1)}, u32[]{:S(2)}, u32[]{:S(2)}) collective-permute-start(bf16[3,32,128]{2,1,0:T(8,128)(2,1)S(1)} %get-tuple-element.43), channel_id=1, source_target_pairs={{1,2},{2,1},{3,4},{4,3},{5,6},{6,5},{7,8},{8,7},{9,10},{10,9},{11,... | collective-permute-start | bytes 73736 | tf_op jit(solution)/shard_map/ppermute | solution.py:514
  29.9 3.8 %collective-permute-start.4 = (f32[2,32,128]{2,1,0:T(8,128)S(1)}, f32[2,32,128]{2,1,0:T(8,128)S(1)}, u32[]{:S(2)}, u32[]{:S(2)}) collective-permute-start(f32[2,32,128]{2,1,0:T(8,128)S(1)} %get-tuple-element.48), channel_id=1, source_target_pairs={{0,1},{1,0},{2,3},{3,2},{4,5},{5,4},{6,7},{7,6},{8,9},{9,8},{10,11... | collective-permute-start | bytes 98312 | tf_op jit(solution)/shard_map/ppermute | solution.py:511

commit v11 on v9

--- a/solution.py
+++ b/solution.py
@@ -380,7 +380,7 @@
         for half in range(2):
             depthwise(
                 tap_rows, half, functools.partial(source, half), pairs_of(EDGE), lambda h: partial[2 * t + half, h],
-                functools.partial(done, half),
+                functools.partial(done, half), OWN,
             )
         first = t * OWN * COLS
         for h in range(OWN):

time: 35.3 us -> 35.4 us (level)
  no operation moved by 1% of the time
where the time goes in v11:
time: 35.4 us; the launch traced here: 35.2 us
  Pallas kernels  25.2 us (71%)
  starting transfers between devices  8.78 us (25%)
  waiting for transfers between devices  1.06 us (3%)
    pallas_call x2, Pallas kernels, edge(): pl.pallas_call(functools.partial(edge_kernel, last), out_shape=outs, in_s...  12 us
    pallas_call x2, Pallas kernels, near(): pl.pallas_call(functools.partial(near_kernel, last), out_shape=outs, in_s...  10.8 us
    ppermute x3, starting transfers between devices, over_tm(): return lax.ppermute(x, 'tm', beside)  7.3 us
    ppermute x2, starting transfers between devices, over_space(): return lax.ppermute(x, ('space', 'tm'), across)  1.48 us
    pallas_call x1, Pallas kernels, finish(): pl.pallas_call(finish_kernel, out_shape=jax.ShapeDtypeStruct((2, 2 * OWN,...  1.38 us
    ppermute x3, waiting for transfers between devices, over_tm(): return lax.ppermute(x, 'tm', beside)  1.05 us
    pallas_call x1, Pallas kernels, prepare(): pl.pallas_call(prepare_kernel, out_shape=[dense, dense, jax.ShapeDtypeStr...  1 us
  transfers between devices with their start and end apart: 5, of which 2 were waited for; matrix products, arithmetic and copies ran while one was open for 0% of the time, Pallas kernels for 31%

profile of v11, /device:TPU:0, one launch (start us, length us, event | category | flops | bytes accessed | tf_op | source)
XLA Modules:
  0.0 35.2 jit_solution(7789281175620987927)
XLA Ops:
  0.0 0.0 copy-start.1
  0.0 0.1 pad_add_fusion.flags.refs_0_
  0.1 0.0 copy-start.2
  0.1 1.0 %shard_map.109 = (f32[32,128]{1,0:T(8,128)S(1)}, f32[32,128]{1,0:T(8,128)S(1)}, f32[32,128]{1,0:T(8,128)S(1)}) custom-call(s32[2]{0:T(128)S(1)} %pad_add_fusion.flags.refs_0_, s32[2]{0:T(128)} %times.1, f32[2]{0:T(128)} %sizes.1, f32[16,16,32]{2,1,0:T(8,128)} %bitcast.8), custom_call_target="tpu_custom_call" | custom-call | tf_op jit(solution)/shard_map/pallas_call | solution.py:476
  1.1 0.0 copy-start
  1.1 0.5 %collective-permute-start.1 = (f32[32,128]{1,0:T(8,128)S(1)}, f32[32,128]{1,0:T(8,128)S(1)}, u32[]{:S(2)}, u32[]{:S(2)}) collective-permute-start(f32[32,128]{1,0:T(8,128)S(1)} %get-tuple-element.28.refs_3_.refs_5_), channel_id=1, source_target_pairs={{0,1},{1,0},{2,3},{3,2},{4,5},{5,4},{6,7},{7,6},{8,9},{9,8},{10,11... | collective-permute-start | bytes 49160 | tf_op jit(solution)/shard_map/ppermute | solution.py:506
  1.6 0.7 %collective-permute-start = (f32[32,128]{1,0:T(8,128)S(1)}, f32[32,128]{1,0:T(8,128)S(1)}, u32[]{:S(2)}, u32[]{:S(2)}) collective-permute-start(f32[32,128]{1,0:T(8,128)S(1)} %get-tuple-element.27.refs_1_.refs_2_), channel_id=1, source_target_pairs={{1,2},{2,1},{3,4},{4,3},{5,6},{6,5},{7,8},{8,7},{9,10},{10,9},{11,... | collective-permute-start | bytes 49160 | tf_op jit(solution)/shard_map/ppermute | solution.py:509
  2.3 0.2 collective-permute-done.1.refs_4_.refs_6_
  2.5 0.0 copy-done.1
  2.5 0.0 copy-done.2
  2.5 0.0 copy-done.3
  2.5 0.0 copy-done
  2.5 5.8 %shard_map.110 = (f32[6,8,32,128]{3,2,1,0:T(8,128)S(1)}, f32[3,5,32,256]{3,2,1,0:T(8,128)S(1)}, f32[8,256]{1,0:T(8,128)S(1)}, bf16[896,256]{1,0:T(8,128)(2,1)S(1...) custom-call(s32[2]{0:T(128)S(1)} %pad_add_fusion.flags.refs_0_, ...), custom_call_target="tpu_custom_call" | custom-call | tf_op jit(solution)/shard_map/pallas_call | solution.py:445
  8.2 0.0 collective-permute-done.refs_1_
  8.2 5.7 %shard_map.111 = (f32[3,32,128]{2,1,0:T(8,128)S(1)}, bf16[3,32,128]{2,1,0:T(8,128)(2,1)S(1)}) custom-call(s32[2]{0:T(128)S(1)} %pad_add_fusion.flags.refs_0_, f32[32,128]{1,0:T(8,128)S(1)} %collective-permute-done.refs_1_, f32[32,128]{1,0:T(8,128)S(1)} %get-tuple-element.27.refs_1_.refs_2_, f32[32,128]{1,0:T(8,128)S(1)} %get-tuple-element.28.refs_3_.refs_5_, ...), custom_call_target="tpu_custom_call" | custom-call | tf_op jit(solution)/shard_map/pallas_call | solution.py:461
  14.0 3.8 %collective-permute-start.3 = (bf16[3,32,128]{2,1,0:T(8,128)(2,1)S(1)}, bf16[3,32,128]{2,1,0:T(8,128)(2,1)S(1)}, u32[]{:S(2)}, u32[]{:S(2)}) collective-permute-start(bf16[3,32,128]{2,1,0:T(8,128)(2,1)S(1)} %get-tuple-element.43), channel_id=1, source_target_pairs={{0,1},{1,0},{2,3},{3,2},{4,5},{5,4},{6,7},{7,6},{8,9},{9,8},{10,11... | collective-permute-start | bytes 73736 | tf_op jit(solution)/shard_map/ppermute | solution.py:506
  17.7 0.8 %collective-permute-start.2 = (bf16[3,32,128]{2,1,0:T(8,128)(2,1)S(1)}, bf16[3,32,128]{2,1,0:T(8,128)(2,1)S(1)}, u32[]{:S(2)}, u32[]{:S(2)}) collective-permute-start(bf16[3,32,128]{2,1,0:T(8,128)(2,1)S(1)} %get-tuple-element.43), channel_id=1, source_target_pairs={{1,2},{2,1},{3,4},{4,3},{5,6},{6,5},{7,8},{8,7},{9,10},{10,9},{11,... | collective-permute-start | bytes 73736 | tf_op jit(solution)/shard_map/ppermute | solution.py:509
  18.6 0.0 collective-permute-done.3.refs_4_
  18.6 5.1 %shard_map.112 = (f32[6,8,32,128]{3,2,1,0:T(8,128)S(1)}, f32[3,5,32,256]{3,2,1,0:T(8,128)S(1)}) custom-call(s32[2]{0:T(128)S(1)} %pad_add_fusion.flags.refs_0_, f32[32,128]{1,0:T(8,128)S(1)} %get-tuple-element.27.refs_1_.refs_2_, f32[32,128]{1,0:T(8,128)S(1)} %get-tuple-element.29.refs_2_, f32[3,32,128]{2,1,0:T(8,128)S(1)} %get-tuple-element.44.refs_3_.refs_4_, ...), custom_call_target="tpu_custom_call" | custom-call | tf_op jit(solution)/shard_map/pallas_call | solution.py:445
  23.7 0.0 collective-permute-done.2.refs_3_
  23.7 6.3 %shard_map.113 = (f32[2,32,128]{2,1,0:T(8,128)S(1)}, f32[2,32,128]{2,1,0:T(8,128)S(1)}) custom-call(s32[2]{0:T(128)S(1)} %pad_add_fusion.flags.refs_0_, f32[32,128]{1,0:T(8,128)S(1)} %collective-permute-done.refs_1_, f32[32,128]{1,0:T(8,128)S(1)} %get-tuple-element.27.refs_1_.refs_2_, bf16[3,32,128]{2,1,0:T(8,128)(2,1)S(1)} %collective-permute-done.2.refs_3_, ...), custom_call_target="tpu_custom_call" | custom-call | tf_op jit(solution)/shard_map/pallas_call | solution.py:461
  30.0 3.0 %collective-permute-start.4 = (f32[2,32,128]{2,1,0:T(8,128)S(1)}, f32[2,32,128]{2,1,0:T(8,128)S(1)}, u32[]{:S(2)}, u32[]{:S(2)}) collective-permute-start(f32[2,32,128]{2,1,0:T(8,128)S(1)} %get-tuple-element.48), channel_id=1, source_target_pairs={{0,1},{1,0},{2,3},{3,2},{4,5},{5,4},{6,7},{7,6},{8,9},{9,8},{10,11... | collective-permute-start | bytes 98312 | tf_op jit(solution)/shard_map/ppermute | solution.py:506
  33.0 0.9 %collective-permute-done.4.got = f32[2,32,128]{2,1,0:T(8,128)S(1)} collective-permute-done((f32[2,32,128]{2,1,0:T(8,128)S(1)}, f32[2,32,128]{2,1,0:T(8,128)S(1)}, u32[]{:S(2)}, u32[]{:S(2)}) %collective-permute-start.4) | collective-permute-done | bytes 32800 | tf_op jit(solution)/shard_map/ppermute | solution.py:506
  33.8 1.4 %shard_map.114 = f32[2,16,16,32]{3,2,1,0:T(8,128)} custom-call(s32[2]{0:T(128)S(1)} %pad_add_fusion.flags.refs_0_, f32[2,32,128]{2,1,0:T(8,128)S(1)} %get-tuple-element.47.keep, f32[2,32,128]{2,1,0:T(8,128)S(1)} %collective-permute-done.4.got), custom_call_target="tpu_custom_call" | custom-call | tf_op jit(solution)/shard_map/pallas_call | solution.py:486
  (1 shorter events, 0.0 us)
Async XLA Ops:
  0.0 2.5 %copy-start.1 = (f32[2,7,7,256]{3,0,2,1:T(2,128)S(1)}, f32[2,7,7,256]{3,0,2,1:T(2,128)}, u32[]{:S(2)}) copy-start(f32[2,7,7,256]{3,0,2,1:T(2,128)} %param.16) | copy-start | bytes 301060
  0.1 2.4 %copy-start.2 = (f32[16,256]{1,0:T(8,128)S(1)}, f32[16,256]{1,0:T(8,128)}, u32[]{:S(2)}) copy-start(f32[16,256]{1,0:T(8,128)} %refs_9_.1) | copy-start | bytes 49156
  0.1 2.4 %copy-start.3 = (f32[256,16]{0,1:T(8,128)S(1)}, f32[256,16]{0,1:T(8,128)}, u32[]{:S(2)}) copy-start(f32[256,16]{0,1:T(8,128)} %param.21) | copy-start | bytes 49156
  1.1 1.4 %copy-start = (f32[2,1024]{1,0:T(2,128)S(1)}, f32[2,1024]{1,0:T(2,128)}, u32[]{:S(2)}) copy-start(f32[2,1024]{1,0:T(2,128)} %refs_20_.1) | copy-start | bytes 24580
  1.1 1.4 %collective-permute-start.1 = (f32[32,128]{1,0:T(8,128)S(1)}, f32[32,128]{1,0:T(8,128)S(1)}, u32[]{:S(2)}, u32[]{:S(2)}) collective-permute-start(f32[32,128]{1,0:T(8,128)S(1)} %get-tuple-element.28.refs_3_.refs_5_), channel_id=1, source_target_pairs={{0,1},{1,0},{2,3},{3,2},{4,5},{5,4},{6,7},{7,6},{8,9},{9,8},{10,11... | collective-permute-start | bytes 49160 | tf_op jit(solution)/shard_map/ppermute | solution.py:506
  1.6 6.6 %collective-permute-start = (f32[32,128]{1,0:T(8,128)S(1)}, f32[32,128]{1,0:T(8,128)S(1)}, u32[]{:S(2)}, u32[]{:S(2)}) collective-permute-start(f32[32,128]{1,0:T(8,128)S(1)} %get-tuple-element.27.refs_1_.refs_2_), channel_id=1, source_target_pairs={{1,2},{2,1},{3,4},{4,3},{5,6},{6,5},{7,8},{8,7},{9,10},{10,9},{11,... | collective-permute-start | bytes 49160 | tf_op jit(solution)/shard_map/ppermute | solution.py:509
  14.0 4.6 %collective-permute-start.3 = (bf16[3,32,128]{2,1,0:T(8,128)(2,1)S(1)}, bf16[3,32,128]{2,1,0:T(8,128)(2,1)S(1)}, u32[]{:S(2)}, u32[]{:S(2)}) collective-permute-start(bf16[3,32,128]{2,1,0:T(8,128)(2,1)S(1)} %get-tuple-element.43), channel_id=1, source_target_pairs={{0,1},{1,0},{2,3},{3,2},{4,5},{5,4},{6,7},{7,6},{8,9},{9,8},{10,11... | collective-permute-start | bytes 73736 | tf_op jit(solution)/shard_map/ppermute | solution.py:506
  17.7 5.9 %collective-permute-start.2 = (bf16[3,32,128]{2,1,0:T(8,128)(2,1)S(1)}, bf16[3,32,128]{2,1,0:T(8,128)(2,1)S(1)}, u32[]{:S(2)}, u32[]{:S(2)}) collective-permute-start(bf16[3,32,128]{2,1,0:T(8,128)(2,1)S(1)} %get-tuple-element.43), channel_id=1, source_target_pairs={{1,2},{2,1},{3,4},{4,3},{5,6},{6,5},{7,8},{8,7},{9,10},{10,9},{11,... | collective-permute-start | bytes 73736 | tf_op jit(solution)/shard_map/ppermute | solution.py:509
  30.0 3.8 %collective-permute-start.4 = (f32[2,32,128]{2,1,0:T(8,128)S(1)}, f32[2,32,128]{2,1,0:T(8,128)S(1)}, u32[]{:S(2)}, u32[]{:S(2)}) collective-permute-start(f32[2,32,128]{2,1,0:T(8,128)S(1)} %get-tuple-element.48), channel_id=1, source_target_pairs={{0,1},{1,0},{2,3},{3,2},{4,5},{5,4},{6,7},{7,6},{8,9},{9,8},{10,11... | collective-permute-start | bytes 98312 | tf_op jit(solution)/shard_map/ppermute | solution.py:506
